TPU v7x, 128 devices: a whole 4x4x4 slice. The times are simulated.
128 devices in a mesh: rows: 128 (over z, x, y, core).
Axes of the slice: x: 4, y: 4, z: 4, core: 2. Of those that a mesh axis runs over, the one named last changes fastest.
Arguments:
- diag_noise: bfloat16 [1792, 128, 128], P('rows'), may hold values from -1 to 1
- couplings: bfloat16 [1792, 3, 128, 128], P('rows'), may hold values from -1 to 1
- shifts: bfloat16 [1792, 128], P('rows'), may hold values from 1.5 to 3
- near_devices: int32 [1792, 3], P('rows'), may hold values from 0 to 126, all different within a row; in each aligned block of 14 rows (0 to 13, 14 to 27, ...) at most 2 rows name the same one
- near_slots: int32 [1792, 3], P('rows'), may hold values from 0 to 13
- vectors: float32 [32, 229376], P(None, 'rows'), may hold values from -6 to 6
Outputs:
- transformed: float32 [32, 229376], P(None, 'rows')
Inputs may be any that keep to these rules, and one draw needn't show every extreme that they name: `near_devices`: each row names three different distances. Among the 14 block rows of one device, no distance is named by more than 2 rows, and in some such group one distance is named by exactly 2 rows.
All inputs are finite; a program needn't handle non-finite values.
Results may differ from a plain program's by a relative error of at most 0.0014.
Values may be sent and summed in bfloat16 or wider, within the bound.
No kernel may reach another device: no remote copies, remote signals or barrier semaphores. Data moves between devices by JAX's collectives and lax.ppermute only.
A program may use at most 128 MiB of HBM per device.

v0:
```python
import math

import jax
import jax.numpy as jnp
from jax import lax
from jax.sharding import PartitionSpec as P

highest = lax.Precision.HIGHEST


def invert(matrix):
    lower_factor = jnp.linalg.cholesky(matrix)
    identity = jnp.broadcast_to(jnp.eye(matrix.shape[-1], dtype=matrix.dtype), matrix.shape)
    inverse_lower = jax.scipy.linalg.solve_triangular(lower_factor, identity, lower=True)
    return jnp.einsum("...ba,...bc->...ac", inverse_lower, inverse_lower, precision=highest)


def build_diag(noise_block, shift_block, factor):
    noise_block = noise_block.astype(jnp.float32) * factor
    symmetric = (noise_block + jnp.swapaxes(noise_block, -1, -2)) * 0.5
    eye_block = jnp.eye(noise_block.shape[-1], dtype=jnp.float32)
    return symmetric + shift_block.astype(jnp.float32)[..., :, None] * eye_block


def row_factors(diag_own, coupling, inverse_near):
    product = jnp.einsum("rmab,rmbc->rmac", coupling, inverse_near, precision=highest)
    schur_block = diag_own - jnp.einsum("rmab,rmcb->rac", product, coupling, precision=highest)
    lower_factor = jnp.linalg.cholesky(invert(schur_block))
    factor_diag = jnp.swapaxes(lower_factor, -1, -2)
    factor_off = -jnp.einsum("rba,rmbc->rmac", lower_factor, product, precision=highest)
    return (factor_diag, factor_off)


def body(diag_noise, couplings, shifts, near_devices, near_slots, vectors):
    dev_count = lax.axis_size("rows")
    my_index = lax.axis_index("rows")
    row_count = diag_noise.shape[0]
    block_size = diag_noise.shape[1]
    vec_count = vectors.shape[0]
    capacity = 3 * row_count // (dev_count - 1) + 2
    slot_total = dev_count * capacity
    request_count = 3 * row_count
    factor = 0.5 / math.sqrt(block_size)
    coupling_factor = 0.4 / math.sqrt(block_size)
    target = ((my_index - 1 - near_devices) % dev_count).reshape(-1)
    device_onehot = (target[:, None] == jnp.arange(dev_count, dtype=jnp.int32)[None, :]).astype(
        jnp.int32
    )
    running = jnp.cumsum(device_onehot, axis=0) - 1
    rank_within = jnp.sum(running * device_onehot, axis=1)
    position = target * capacity + rank_within
    source_index = (
        jnp.full((slot_total,), request_count, jnp.int32)
        .at[position]
        .set(jnp.arange(request_count, dtype=jnp.int32))
    )
    filled = source_index < request_count
    safe_source = jnp.minimum(source_index, request_count - 1)
    asked_slots = jnp.where(filled, near_slots.reshape(-1)[safe_source], -1)
    incoming = lax.all_to_all(
        asked_slots.reshape(dev_count, capacity), "rows", split_axis=0, concat_axis=0, tiled=True
    ).reshape(-1)
    served = jnp.maximum(incoming, 0)
    landing = (incoming[:, None] == jnp.arange(row_count, dtype=jnp.int32)[None, :]).astype(
        jnp.float32
    )
    diag_own = build_diag(diag_noise, shifts, factor)
    inverse_own = invert(diag_own)
    answer = inverse_own[served].reshape(dev_count, capacity, block_size, block_size)
    returned = lax.all_to_all(answer, "rows", split_axis=0, concat_axis=0, tiled=True)
    inverse_near = returned.reshape(slot_total, block_size, block_size)[position]
    inverse_near = inverse_near.reshape(row_count, 3, block_size, block_size)
    coupling = couplings.astype(jnp.float32) * coupling_factor
    factor_diag, factor_off = row_factors(diag_own, coupling, inverse_near)
    vector_rows = vectors.reshape(vec_count, row_count, block_size).transpose(1, 0, 2)
    left_product = jnp.einsum("rva,rab->rvb", vector_rows, factor_diag, precision=highest)
    outgoing = jnp.einsum("rva,rmab->rmvb", vector_rows, factor_off, precision=highest).reshape(
        request_count, vec_count, block_size
    )
    outgoing_slots = jnp.where(filled[:, None, None], outgoing[safe_source], 0.0).reshape(
        dev_count, capacity, vec_count, block_size
    )
    arrived = (
        lax.all_to_all(
            outgoing_slots.astype(jnp.bfloat16), "rows", split_axis=0, concat_axis=0, tiled=True
        )
        .astype(outgoing_slots.dtype)
        .reshape(slot_total, vec_count, block_size)
    )
    left_product = left_product + jnp.einsum("pr,pvb->rvb", landing, arrived, precision=highest)
    left_answer = left_product[served].reshape(dev_count, capacity, vec_count, block_size)
    pushed = jnp.einsum("rva,rmab->rmvb", left_product, coupling, precision=highest).reshape(
        request_count, vec_count, block_size
    )
    pushed_slots = jnp.where(filled[:, None, None], pushed[safe_source], 0.0).reshape(
        dev_count, capacity, vec_count, block_size
    )
    left_returned, pushed_arrived = (
        lax.all_to_all(left_answer, "rows", split_axis=0, concat_axis=0, tiled=True),
        lax.all_to_all(pushed_slots, "rows", split_axis=0, concat_axis=0, tiled=True),
    )
    left_near = left_returned.reshape(slot_total, vec_count, block_size)[position].reshape(
        row_count, 3, vec_count, block_size
    )
    middle_product = jnp.einsum("rva,rab->rvb", left_product, diag_own, precision=highest)
    middle_product = middle_product + jnp.einsum(
        "rmvb,rmab->rva", left_near, coupling, precision=highest
    )
    middle_product = middle_product + jnp.einsum(
        "pr,pvb->rvb",
        landing,
        pushed_arrived.reshape(slot_total, vec_count, block_size),
        precision=highest,
    )
    middle_answer = middle_product[served].reshape(dev_count, capacity, vec_count, block_size)
    middle_returned = lax.all_to_all(
        middle_answer.astype(jnp.bfloat16), "rows", split_axis=0, concat_axis=0, tiled=True
    ).astype(middle_answer.dtype)
    middle_near = middle_returned.reshape(slot_total, vec_count, block_size)[position].reshape(
        row_count, 3, vec_count, block_size
    )
    result = jnp.einsum("rvb,rab->rva", middle_product, factor_diag, precision=highest)
    result = result + jnp.einsum("rmvb,rmab->rva", middle_near, factor_off, precision=highest)
    return result.transpose(1, 0, 2).reshape(vec_count, row_count * block_size)


def solution(mesh):
    return jax.shard_map(
        body,
        mesh=mesh,
        in_specs=(
            P("rows", None, None),
            P("rows", None, None, None),
            P("rows", None),
            P("rows", None),
            P("rows", None),
            P(None, "rows"),
        ),
        out_specs=P(None, "rows"),
        check_vma=False,
    )
```

profile of v0, /device:TPU:1, one launch (start us, length us, event | category | flops | bytes accessed | tf_op | source)
XLA Modules:
  0.0 1342.2 jit_solution(212793399763485334)
XLA Ops:
  0.0 0.8 copy.108
  0.9 0.7 fusion.76
  1.7 0.7 fusion.77
  2.4 0.7 fusion.78
  3.1 0.7 broadcast_multiply_fusion
  4.5 0.7 scatter_custom_fusion
  5.2 26.3 %fusion.61 = (s32[256]{0:T(256)S(1)}, pred[256]{0:T(512)(128)(4,1)S(1)}) fusion(s32[]{:T(128)} %bitcast.6, s32[]{:T(128)} %bitcast.7, s32[]{:T(128)} %bitcast.8, s32[]{:T(128)} %bitcast.9, s32[]{:T(128)} %bitcast.10, s32[]{:T(128)} %bitcast.11, s32[]{:T(128)} %bitcast.12, s32[]{:T(128)} %bitcast.13, s32[]{:T(128)} %bitcast.14, s32[]{:T(128)} %bitcast.15, ...), kind=kLoop, calls=%fused_computation.143 | loop fusion | flops 22528 | bytes 2472 | tf_op jit(solution)/shard_map/jit(_where)/select_n | solution.py:59
  31.5 0.8 all_to_all.21
  32.2 11.5 all-to-all-start
  43.8 1.1 convert_multiply_fusion.11
  45.9 164.1 %custom-call.9 = f32[14,128,128]{2,1,0:T(8,128)S(1)} custom-call(f32[14,128,128]{2,1,0:T(8,128)S(1)} %fusion.31), custom_call_target="Cholesky" | custom-call | tf_op jit(solution)/shard_map/jit(cholesky)/cholesky | solution.py:12
  210.4 137.7 %custom-call.10 = f32[14,1,128,128]{2,3,1,0:T(8,128)S(1)} custom-call(f32[14,1,128,128]{3,2,1,0:T(8,128)S(1)} %select_bitcast_fusion.1), custom_call_target="InvertDiagBlocksLowerTriangular" | custom-call | tf_op jit(solution)/shard_map/jit(_solve_triangular)/vmap()/triangular_solve | solution.py:14
  348.1 1.6 fusion.29
  349.7 1.6 fusion.79
  351.4 0.5 broadcast.319
  351.9 1.0 fusion.75
  353.1 7.3 gather_fusion
  360.4 10.7 all-to-all-start.1
  371.3 212.5 %all-to-all-done.1 = f32[128,2,128,128]{3,2,1,0:T(8,128)} async-done(((f32[128,2,128,128]{3,2,1,0:T(8,128)}), f32[128,2,128,128]{3,2,1,0:T(8,128)}, u32[]{:S(2)}, u32[]{:S(2)}) %all-to-all-start.1) | async-done | bytes 16777248 | tf_op jit(solution)/shard_map/all_to_all | solution.py:70
  583.9 8.0 gather_fusion.1
  591.9 5.3 fusion.7
  597.3 4.7 fusion.15
  602.0 2.4 copy.111
  604.4 2.5 fusion.28
  606.9 165.6 %custom-call.11 = f32[14,128,128]{2,1,0:T(8,128)} custom-call(f32[14,128,128]{2,1,0:T(8,128)} %fusion.28), custom_call_target="Cholesky" | custom-call | tf_op jit(solution)/shard_map/jit(cholesky)/cholesky | solution.py:12
  772.5 1.3 select_reduce_fusion.1
  773.9 2.3 select_bitcast_fusion
  776.2 139.4 %custom-call.12 = f32[14,1,128,128]{2,3,1,0:T(8,128)} custom-call(f32[14,1,128,128]{3,2,1,0:T(8,128)} %select_bitcast_fusion), custom_call_target="InvertDiagBlocksLowerTriangular" | custom-call | tf_op jit(solution)/shard_map/jit(_solve_triangular)/vmap()/triangular_solve | solution.py:14
  915.6 2.8 fusion.26
  918.4 2.6 fusion.80
  921.0 2.4 copy.115
  923.4 2.5 fusion.25
  925.9 165.7 %custom-call.13 = f32[14,128,128]{2,1,0:T(8,128)} custom-call(f32[14,128,128]{2,1,0:T(8,128)} %fusion.25), custom_call_target="Cholesky" | custom-call | tf_op jit(solution)/shard_map/jit(cholesky)/cholesky | solution.py:28
  1091.7 1.3 select_reduce_fusion
  1093.1 6.1 fusion.23
  1099.1 1.5 copy-done
  1100.7 3.1 fusion.2
  1103.8 1.0 gather_fusion.2
  1104.8 0.6 select_convert_fusion
  1105.4 3.7 copy.120
  1109.1 15.3 %all-to-all-start.2 = ((bf16[128,2,32,128]{3,1,2,0:T(2,128)(2,1)}), bf16[128,2,32,128]{3,1,2,0:T(2,128)(2,1)}, u32[]{:S(2)}, u32[]{:S(2)}) async-start(bf16[128,2,32,128]{3,1,2,0:T(2,128)(2,1)} %copy.120), calls=%async_computation.2 | async-start | bytes 4194304 | tf_op jit(solution)/shard_map/all_to_all | solution.py:84
  1124.6 29.9 %all-to-all-done.2 = bf16[128,2,32,128]{3,1,2,0:T(2,128)(2,1)} async-done(((bf16[128,2,32,128]{3,1,2,0:T(2,128)(2,1)}), bf16[128,2,32,128]{3,1,2,0:T(2,128)(2,1)}, u32[]{:S(2)}, u32[]{:S(2)}) %all-to-all-start.2) | async-done | bytes 2097184 | tf_op jit(solution)/shard_map/all_to_all | solution.py:84
  1154.5 3.8 copy.121
  1158.6 1.7 fusion.19
  1160.3 2.0 fusion.4
  1162.3 3.0 gather_fusion.5
  1165.3 2.5 broadcast_select_fusion
  1167.8 6.0 copy.124
  1173.8 5.4 all-to-all-start.4
  1179.2 3.0 gather_fusion.3
  1182.3 49.9 %all-to-all-done.4 = f32[128,2,32,128]{3,1,2,0:T(2,128)} async-done(((f32[128,2,32,128]{3,1,2,0:T(2,128)}), f32[128,2,32,128]{3,1,2,0:T(2,128)}, u32[]{:S(2)}, u32[]{:S(2)}) %all-to-all-start.4) | async-done | bytes 4194336 | tf_op jit(solution)/shard_map/all_to_all | solution.py:100
  1232.2 5.6 all-to-all-start.3
  1237.8 4.5 copy.125
  1242.3 1.5 fusion.54
  1243.8 47.0 %all-to-all-done.3 = f32[128,2,32,128]{3,2,1,0:T(8,128)} async-done(((f32[128,2,32,128]{3,2,1,0:T(8,128)}), f32[128,2,32,128]{3,2,1,0:T(8,128)}, u32[]{:S(2)}, u32[]{:S(2)}) %all-to-all-start.3) | async-done | bytes 4194336 | tf_op jit(solution)/shard_map/all_to_all | solution.py:99
  1290.8 2.8 gather_fusion.4
  1293.6 3.0 fusion.20
  1296.6 1.5 fusion.22
  1298.1 2.4 gather_fusion.6
  1300.5 36.1 %all_to_all.34 = bf16[128,2,32,128]{3,2,1,0:T(8,128)(2,1)} all-to-all(bf16[128,2,32,128]{3,2,1,0:T(8,128)(2,1)} %bitcast.162), channel_id=1, replica_groups=mesh['rows'=128] {'rows'}, dimensions={0} | all-to-all | bytes 4194304 | tf_op jit(solution)/shard_map/all_to_all | solution.py:116
  1336.6 2.2 gather_fusion.7
  1338.8 1.2 fusion.16
  1340.1 1.0 fusion.21
  1341.1 0.7 copy.156
  (56 shorter events, 3.2 us)
Async XLA Ops:
  0.0 45.3 %copy-start.9 = (bf16[14,128,128]{2,1,0:T(8,128)(2,1)S(1)}, bf16[14,128,128]{2,1,0:T(8,128)(2,1)}, u32[]{:S(2)}) copy-start(bf16[14,128,128]{2,1,0:T(8,128)(2,1)} %param.9) | copy-start | bytes 1376260
  0.0 45.2 %copy-start.11 = (bf16[14,128]{1,0:T(8,128)(2,1)S(1)}, bf16[14,128]{1,0:T(8,128)(2,1)}, u32[]{:S(2)}) copy-start(bf16[14,128]{1,0:T(8,128)(2,1)} %param.11) | copy-start | bytes 10756
  32.2 319.1 %all-to-all-start = ((s32[128,1,2]{2,1,0:T(1,128)}), s32[128,1,2]{2,1,0:T(1,128)S(1)}, u32[]{:S(2)}, u32[]{:S(2)}) async-start(s32[128,1,2]{2,1,0:T(1,128)} %bitcast.48), calls=%async_computation | async-start | bytes 131072 | tf_op jit(solution)/shard_map/all_to_all | solution.py:60
  45.5 164.6 %copy-start.2 = (f32[14,128,128]{1,2,0:T(8,128)}, f32[14,128,128]{1,2,0:T(8,128)S(1)}, u32[]{:S(2)}) copy-start(f32[14,128,128]{1,2,0:T(8,128)S(1)} %fusion.33) | copy-start | bytes 2752516
  360.4 10.7 copy-start.10
  360.4 223.5 %all-to-all-start.1 = ((f32[128,2,128,128]{3,2,1,0:T(8,128)}), f32[128,2,128,128]{3,2,1,0:T(8,128)}, u32[]{:S(2)}, u32[]{:S(2)}) async-start(f32[128,2,128,128]{3,2,1,0:T(8,128)} %bitcast.154), calls=%async_computation.1 | async-start | bytes 33554432 | tf_op jit(solution)/shard_map/all_to_all | solution.py:70
  591.9 5.4 copy-start.3
  591.9 5.4 copy-start.5
  1099.1 1.5 copy-start
  1109.1 45.3 %all-to-all-start.2 = ((bf16[128,2,32,128]{3,1,2,0:T(2,128)(2,1)}), bf16[128,2,32,128]{3,1,2,0:T(2,128)(2,1)}, u32[]{:S(2)}, u32[]{:S(2)}) async-start(bf16[128,2,32,128]{3,1,2,0:T(2,128)(2,1)} %copy.120), calls=%async_computation.2 | async-start | bytes 4194304 | tf_op jit(solution)/shard_map/all_to_all | solution.py:84
  1124.6 34.0 %copy-start.7 = (f32[14,128,128]{2,1,0:T(8,128)S(1)}, f32[14,128,128]{2,1,0:T(8,128)}, u32[]{:S(2)}) copy-start(f32[14,128,128]{2,1,0:T(8,128)} %custom-call.13) | copy-start | bytes 2752516
  1158.2 2.1 copy-start.6
  1173.8 58.4 %all-to-all-start.4 = ((f32[128,2,32,128]{3,1,2,0:T(2,128)}), f32[128,2,32,128]{3,1,2,0:T(2,128)}, u32[]{:S(2)}, u32[]{:S(2)}) async-start(f32[128,2,32,128]{3,1,2,0:T(2,128)} %copy.124), calls=%async_computation.4 | async-start | bytes 8388608 | tf_op jit(solution)/shard_map/all_to_all | solution.py:100
  1232.2 58.6 %all-to-all-start.3 = ((f32[128,2,32,128]{3,2,1,0:T(8,128)}), f32[128,2,32,128]{3,2,1,0:T(8,128)}, u32[]{:S(2)}, u32[]{:S(2)}) async-start(f32[128,2,32,128]{3,2,1,0:T(8,128)} %bitcast.157), calls=%async_computation.3 | async-start | bytes 8388608 | tf_op jit(solution)/shard_map/all_to_all | solution.py:99
  1243.8 52.8 %copy-start.4 = (f32[14,128,128]{1,2,0:T(8,128)S(1)}, f32[14,128,128]{1,2,0:T(8,128)}, u32[]{:S(2)}) copy-start(f32[14,128,128]{1,2,0:T(8,128)} %copy-done.2) | copy-start | bytes 2752516
  1300.5 38.3 %copy-start.1 = (f32[14,3,128,128]{3,2,1,0:T(8,128)S(1)}, f32[14,3,128,128]{3,2,1,0:T(8,128)}, u32[]{:S(2)}) copy-start(f32[14,3,128,128]{3,2,1,0:T(8,128)} %copy-done) | copy-start | bytes 8257540
  1338.8 1.3 copy-start.8
where the time goes:
time: 1350 us; the launch traced here: 1340 us
  other arithmetic  816 us (60%)
  waiting for transfers between devices  339 us (25%)
  local copies, waits for them, and re-layouts  61.4 us (5%)
  starting transfers between devices  48.5 us (4%)
  matrix products  40.1 us (3%)
  blocking collectives  36.1 us (3%)
    another operation x6, other arithmetic, invert(): lower_factor = jnp.linalg.cholesky(matrix)  331 us
    another operation x4, other arithmetic, invert(): jax.scipy.linalg.solve_triangular(lower_factor, identity, lower=True)  280 us
    all_to_all x1, waiting for transfers between devices, body(): lax.all_to_all(answer, 'rows', split_axis=0, concat_axis=0, tiled=True)  213 us
    another operation x4, other arithmetic, row_factors(): lower_factor = jnp.linalg.cholesky(invert(schur_block))  167 us
    all_to_all x1, waiting for transfers between devices, body(): lax.all_to_all(pushed_slots, 'rows', split_axis=0, concat_axis=0, tiled=T...  49.9 us
    all_to_all x1, waiting for transfers between devices, body(): lax.all_to_all(left_answer, 'rows', split_axis=0, concat_axis=0, tiled=True)  47 us
    all_to_all x1, blocking collectives, body(): lax.all_to_all(middle_answer.astype(jnp.bfloat16), 'rows', split_axis=0,...  36.1 us
    all_to_all x1, waiting for transfers between devices, body(): lax.all_to_all(outgoing_slots.astype(jnp.bfloat16), 'rows', split_axis=0,...  29.9 us
  transfers between devices with their start and end apart: 5, of which 4 were waited for; matrix products, arithmetic and copies ran while one was open for 24% of the time, Pallas kernels for 0%

commit v1 on v0

v1 whole, which is shorter than its diff:
```python
import math

import jax
import jax.numpy as jnp
from jax import lax
from jax.experimental import pallas as pl
from jax.experimental.pallas import tpu as pltpu
from jax.sharding import PartitionSpec as P

F32 = jnp.float32
BF16 = jnp.bfloat16
BLK = 128
SLOTS = 2
TRI = 64
PAY = 80
VMEM_LIMIT = 56 * 1024 * 1024
SM = pltpu.SMEM
VM = pltpu.VMEM
highest = lax.Precision.HIGHEST


def spec(space):
    return pl.BlockSpec(memory_space=space)


def call(kernel, out_shape, ins, outs, scratch=(), flops=0, moved=0, name=None):
    return pl.pallas_call(
        kernel,
        out_shape=out_shape,
        in_specs=[spec(s) for s in ins],
        out_specs=jax.tree.map(spec, outs),
        scratch_shapes=list(scratch),
        compiler_params=pltpu.CompilerParams(vmem_limit_bytes=VMEM_LIMIT),
        cost_estimate=pl.CostEstimate(flops=flops, bytes_accessed=moved, transcendentals=0),
        name=name,
    )


def iotas(rows, lanes=BLK):
    return (
        lax.broadcasted_iota(jnp.int32, (rows, lanes), 0),
        lax.broadcasted_iota(jnp.int32, (rows, lanes), 1),
    )


def split(x):
    hi = x.astype(BF16)
    lo = (x - hi.astype(F32)).astype(BF16)
    return hi, lo


def dot(a, b, ca=1, cb=0):
    return lax.dot_general(a, b, (((ca,), (cb,)), ((), ())), preferred_element_type=F32)


def dot_exact(a, b, ca=1, cb=0):
    return lax.dot_general(
        a, b, (((ca,), (cb,)), ((), ())), preferred_element_type=F32, precision=highest
    )


def rows_times_bf16(x, b, cb=0):
    hi, lo = split(x)
    both = dot(jnp.concatenate([hi, lo], axis=0), b, 1, cb)
    n = x.shape[0]
    return both[:n] + both[n:]


def factor(z, vs, count):
    sub, lane = iotas(8)

    def panel(step, carry):
        kb = BLK // 8 - 1 - step
        row0 = pl.multiple_of(kb * 8, 8)
        part = [z[b, pl.ds(row0, 8), :] for b in range(count)]
        for j in range(7, -1, -1):
            c = row0 + j
            index = jnp.full((8, BLK), c, jnp.int32)
            at_c = lane == c
            for b in range(count):
                p = part[b]
                col = jnp.take_along_axis(p, index, axis=1, mode="promise_in_bounds")
                row = jnp.broadcast_to(p[j : j + 1, :], (8, BLK))
                d = jnp.broadcast_to(col[j : j + 1, :], (8, BLK))
                rs = lax.rsqrt(d)
                v = jnp.where(at_c, rs, row * rs)
                scaled = jnp.where(at_c, 1.0 + rs * rs, v * rs)
                vs[b, j] = scaled
                part[b] = jnp.where(sub < j, p - col * scaled, jnp.where(sub == j, v, p))
        for b in range(count):
            z[b, pl.ds(row0, 8), :] = part[b]

        def above(r, inner):
            r0 = pl.multiple_of(r * 8, 8)
            rows = [z[b, pl.ds(r0, 8), :] for b in range(count)]
            for j in range(7, -1, -1):
                index = jnp.full((8, BLK), row0 + j, jnp.int32)
                for b in range(count):
                    col = jnp.take_along_axis(rows[b], index, axis=1, mode="promise_in_bounds")
                    rows[b] = rows[b] - col * vs[b, j]
            for b in range(count):
                z[b, pl.ds(r0, 8), :] = rows[b]
            return inner

        lax.fori_loop(0, kb, above, 0)
        return carry

    lax.fori_loop(0, BLK // 8, panel, 0)


def factor_scratch(count):
    return [VM((count, BLK, BLK), F32), VM((count, 8, 8, BLK), F32)]


def build_diag(noise, shift, b, factor_value):
    sub, lane = iotas(BLK)
    n = noise[b]
    eye = (sub == lane).astype(BF16)
    turned = dot(eye, n, 1, 1)
    sym = (n.astype(F32) + turned) * (0.5 * factor_value)
    shift_row = shift[pl.ds(b, 1), :].astype(F32)
    return sym + jnp.where(sub == lane, shift_row, 0.0)


def route_kernel(me_ref, dev_ref, slot_ref, ask_ref, pos_ref, count_ref):
    n_dev = count_ref.shape[0]
    me = me_ref[0]

    def clear(t, carry):
        count_ref[t] = 0
        for r in range(SLOTS):
            ask_ref[t, r] = -1
        return carry

    lax.fori_loop(0, n_dev, clear, 0)

    def one(i, carry):
        for m in range(3):
            t = me - 1 - dev_ref[i, m]
            t = jnp.where(t < 0, t + n_dev, t)
            rank = count_ref[t]
            count_ref[t] = rank + 1
            ask_ref[t, rank] = slot_ref[i, m]
            pos_ref[i * 3 + m] = t * SLOTS + rank
        return carry

    lax.fori_loop(0, dev_ref.shape[0], one, 0)


def invert_kernel(factor_value, noise, shift, x_out, pay_out, z, vs):
    count = noise.shape[0]
    for b in range(count):
        z[b] = build_diag(noise, shift, b, factor_value)
    factor(z, vs, count)
    sub, lane = iotas(BLK)
    top_sub, top_lane = iotas(TRI)
    low_eye = (top_lane == top_sub + TRI).astype(BF16)
    diag_sub, _ = iotas(16)
    for b in range(count):
        x = jnp.where(lane >= sub, z[b], 0.0)
        x_out[b] = x
        bottom = jnp.concatenate(
            [x[TRI:].astype(BF16), jnp.zeros((TRI, BLK), BF16)], axis=0
        )
        turned = dot(low_eye, bottom, 1, 1)
        tri = jnp.where(top_lane > top_sub, x[:TRI], jnp.where(top_lane < top_sub, turned, 0.0))
        pay_out[b, :TRI, :] = tri.astype(BF16)
        diag = jnp.sum(jnp.where(sub == lane, x, 0.0), axis=0, keepdims=True)
        hi, lo = split(diag)
        tail = jnp.where(
            diag_sub == 0, hi.astype(F32), jnp.where(diag_sub == 1, lo.astype(F32), 0.0)
        )
        pay_out[b, TRI:, :] = tail.astype(BF16)


def serve_kernel(incoming, pay, out, list_pos, list_slot, list_count):
    n_dev = incoming.shape[0]
    g = pl.program_id(0)
    per = out.shape[0]

    @pl.when(g == 0)
    def _():
        list_count[0] = 0

    def one(t, carry):
        pos = g * per + t
        slot = incoming[pos // SLOTS, pos % SLOTS]

        @pl.when(slot >= 0)
        def _():
            out[t] = pay[slot]
            n = list_count[0]
            list_pos[n] = pos
            list_slot[n] = slot
            list_count[0] = n + 1

        return carry

    lax.fori_loop(0, per, one, 0)


def gram_kernel(x, e_out):
    for b in range(x.shape[0]):
        e_out[b] = dot_exact(x[b], x[b], 0, 0)


def row_kernel(
    factor_value, coupling_factor, pos, noise, shift, couplings, vectors, arrived,
    w_out, y_out, send, z, vs, near, sems,
):
    count = noise.shape[0]
    n_vec = vectors.shape[0]
    copies = []
    for q in range(3 * count):
        copy = pltpu.make_async_copy(arrived.at[pos[q]], near.at[q], sems.at[q])
        copy.start()
        copies.append(copy)
    for b in range(count):
        z[b] = build_diag(noise, shift, b, factor_value)
    for copy in copies:
        copy.wait()
    top_sub, top_lane = iotas(TRI)

    def schur(b, carry):
        total = jnp.zeros((BLK, BLK), F32)
        for m in range(3):
            q = b * 3 + m
            tri = near[q, :TRI, :].astype(F32)
            upper = jnp.where(top_lane > top_sub, tri, 0.0).astype(BF16)
            lower = jnp.where(top_lane < top_sub, tri, 0.0).astype(BF16)
            lower = pltpu.roll(lower.astype(F32), TRI, 1).astype(BF16)
            tail = near[q, TRI:, :].astype(F32)
            diag = tail[0:1] + tail[1:2]
            c = couplings[b, m]
            zero = jnp.zeros((TRI, BLK), BF16)
            y = dot(c, jnp.concatenate([upper, zero], axis=0), 1, 1)
            y = y + dot(c, jnp.concatenate([zero, lower], axis=0), 1, 0)
            y = y + c.astype(F32) * diag
            yh = y.astype(BF16)
            total = total + dot(yh, yh, 1, 1)
        z[b] = z[b] - total * (coupling_factor * coupling_factor)
        return carry

    lax.fori_loop(0, count, schur, 0)
    factor(z, vs, count)
    sub, lane = iotas(BLK)
    for b in range(count):
        w = jnp.where(lane >= sub, z[b], 0.0)
        w_out[b] = w
        y = dot_exact(vectors[:, b * BLK : (b + 1) * BLK], w)
        y_out[b] = y
        for m in range(3):
            p = rows_times_bf16(y, couplings[b, m]) * coupling_factor
            send[pos[b * 3 + m]] = p.astype(BF16)


def own_kernel(factor_value, noise, shift, y, out):
    for b in range(noise.shape[0]):
        d = build_diag(noise, shift, b, factor_value)
        out[b] = dot_exact(y[b], d)


def left_kernel(
    coupling_factor, pos, list_pos, list_slot, list_count, arrived, y, e, couplings, send, left, total
):
    count = y.shape[0]
    n_vec = y.shape[1]
    total[...] = jnp.zeros_like(total)

    def add(t, carry):
        slot = list_slot[t]
        total[slot] += arrived[list_pos[t]].astype(F32)
        return carry

    lax.fori_loop(0, list_count[0], add, 0)
    for b in range(count):
        u = dot_exact(total[b], e[b])
        left[b] = (y[b] - u).astype(BF16)
        for m in range(3):
            p = rows_times_bf16(u, couplings[b, m]) * coupling_factor
            at = pos[b * 3 + m]
            send[at // SLOTS, SLOTS + at % SLOTS] = p.astype(BF16)

    def give(t, carry):
        at = list_pos[t]
        send[at // SLOTS, at % SLOTS] = left[list_slot[t]]
        return carry

    lax.fori_loop(0, list_count[0], give, 0)


def middle_kernel(
    coupling_factor, pos, list_pos, list_slot, list_count, arrived, own, e, couplings,
    middle, send, total, answer,
):
    count = own.shape[0]
    total[...] = jnp.zeros_like(total)

    def add(t, carry):
        slot = list_slot[t]
        at = list_pos[t]
        total[slot] += arrived[at // SLOTS, SLOTS + at % SLOTS].astype(F32)
        return carry

    lax.fori_loop(0, list_count[0], add, 0)
    for b in range(count):
        near = jnp.zeros(total.shape[1:], F32)
        for m in range(3):
            at = pos[b * 3 + m]
            near = near + dot(arrived[at // SLOTS, at % SLOTS], couplings[b, m], 1, 1)
        mid = own[b] - total[b] + near * coupling_factor
        middle[b] = mid
        answer[b] = dot_exact(mid, e[b]).astype(BF16)

    def give(t, carry):
        send[list_pos[t]] = answer[list_slot[t]]
        return carry

    lax.fori_loop(0, list_count[0], give, 0)


def result_kernel(coupling_factor, pos, arrived, middle, w, couplings, out):
    for b in range(middle.shape[0]):
        near = jnp.zeros(middle.shape[1:], F32)
        for m in range(3):
            near = near + dot(arrived[pos[b * 3 + m]], couplings[b, m], 1, 1)
        mid = middle[b] - near * coupling_factor
        out[:, b * BLK : (b + 1) * BLK] = dot_exact(mid, w[b], 1, 1)


def exchange(x):
    return lax.all_to_all(x, "rows", split_axis=0, concat_axis=0, tiled=True)


def body(diag_noise, couplings, shifts, near_devices, near_slots, vectors):
    n_dev = lax.axis_size("rows")
    me = lax.axis_index("rows").astype(jnp.int32).reshape(1)
    count = diag_noise.shape[0]
    n_vec = vectors.shape[0]
    total_slots = n_dev * SLOTS
    factor_value = 0.5 / math.sqrt(BLK)
    coupling_factor = 0.4 / math.sqrt(BLK)

    def shape(dims, dtype=F32):
        return jax.ShapeDtypeStruct(dims, dtype)

    blocks = shape((count, BLK, BLK))
    rows = shape((count, n_vec, BLK))

    def with_factors(kernel, *values):
        def wrapped(*refs):
            kernel(*values, *refs)

        return wrapped

    ask, pos = call(
        route_kernel,
        (shape((n_dev, SLOTS), jnp.int32), shape((3 * count,), jnp.int32)),
        [SM, SM, SM],
        (SM, SM),
        [SM((n_dev,), jnp.int32)],
        name="route",
    )(me, near_devices, near_slots)
    incoming = exchange(ask)
    x, pay = call(
        with_factors(invert_kernel, factor_value),
        (blocks, shape((count, PAY, BLK), BF16)),
        [VM, VM],
        (VM, VM),
        factor_scratch(count),
        flops=2 * 10**9,
        moved=10**8,
        name="invert",
    )(diag_noise, shifts)
    per = 16
    answer, list_pos, list_slot, list_count = pl.pallas_call(
        serve_kernel,
        grid=(total_slots // per,),
        out_shape=(
            shape((total_slots, PAY, BLK), BF16),
            shape((total_slots,), jnp.int32),
            shape((total_slots,), jnp.int32),
            shape((1,), jnp.int32),
        ),
        in_specs=[spec(SM), spec(VM)],
        out_specs=(
            pl.BlockSpec((per, PAY, BLK), lambda g: (g, 0, 0)),
            spec(SM),
            spec(SM),
            spec(SM),
        ),
        compiler_params=pltpu.CompilerParams(
            vmem_limit_bytes=VMEM_LIMIT, dimension_semantics=("arbitrary",)
        ),
        name="serve",
    )(incoming, pay)
    arrived = exchange(answer.reshape(n_dev, SLOTS * PAY, BLK)).reshape(total_slots, PAY, BLK)
    e = call(
        gram_kernel, blocks, [VM], VM, flops=10**9, moved=10**7, name="gram"
    )(x)
    w, y, push = call(
        with_factors(row_kernel, factor_value, coupling_factor),
        (blocks, rows, shape((total_slots, n_vec, BLK), BF16)),
        [SM, VM, VM, VM, VM, pl.ANY],
        (VM, VM, VM),
        factor_scratch(count)
        + [VM((3 * count, PAY, BLK), BF16), pltpu.SemaphoreType.DMA((3 * count,))],
        name="row",
    )(pos, diag_noise, shifts, couplings, vectors, arrived)
    pushed = exchange(push.reshape(n_dev, SLOTS * n_vec, BLK)).reshape(total_slots, n_vec, BLK)
    own = call(
        with_factors(own_kernel, factor_value),
        rows, [VM, VM, VM], VM, flops=10**9, moved=10**7, name="own",
    )(diag_noise, shifts, y)
    lists = (list_pos, list_slot, list_count)
    both = call(
        with_factors(left_kernel, coupling_factor),
        shape((n_dev, 2 * SLOTS, n_vec, BLK), BF16),
        [SM] * 4 + [VM] * 4,
        VM,
        [VM((count, n_vec, BLK), BF16), VM((count, n_vec, BLK), F32)],
        name="left",
    )(pos, *lists, pushed, y, e, couplings)
    both = exchange(both.reshape(n_dev, 2 * SLOTS * n_vec, BLK)).reshape(
        n_dev, 2 * SLOTS, n_vec, BLK
    )
    middle, back = call(
        with_factors(middle_kernel, coupling_factor),
        (rows, shape((total_slots, n_vec, BLK), BF16)),
        [SM] * 4 + [VM] * 4,
        (VM, VM),
        [VM((count, n_vec, BLK), F32), VM((count, n_vec, BLK), BF16)],
        name="middle",
    )(pos, *lists, both, own, e, couplings)
    back = exchange(back.reshape(n_dev, SLOTS * n_vec, BLK)).reshape(total_slots, n_vec, BLK)
    return call(
        with_factors(result_kernel, coupling_factor),
        shape((n_vec, count * BLK)),
        [SM] + [VM] * 4,
        VM,
        name="result",
    )(pos, back, middle, w, couplings)


def solution(mesh):
    return jax.shard_map(
        body,
        mesh=mesh,
        in_specs=(
            P("rows", None, None),
            P("rows", None, None, None),
            P("rows", None),
            P("rows", None),
            P("rows", None),
            P(None, "rows"),
        ),
        out_specs=P(None, "rows"),
        check_vma=False,
    )
```

time: 1350 us -> 438 us (0.32)
  other arithmetic: 816 us -> 0 us
  waiting for transfers between devices: 339 us -> 76.5 us
  Pallas kernels: 0 us -> 225 us
  blocking collectives: 36.1 us -> 110 us
  local copies, waits for them, and re-layouts: 61.4 us -> 4.68 us
  matrix products: 40.1 us -> 0 us
  starting transfers between devices: 48.5 us -> 21.7 us
    another operation x15 -> x0, other arithmetic: 778 us -> none  [the longest x6 331 us: invert(): lower_factor = jnp.linalg.cholesky(matrix)]
    all_to_all x5 -> x3, waiting for transfers between devices: 339 us -> 76.5 us  [exchange(): return lax.all_to_all(x, 'rows', split_axis=0, concat_axis=0, tiled=True)]
    pallas_call x0 -> x9, Pallas kernels: none -> 225 us  [the longest x1 96.6 us: body(): call(with_factors(row_kernel, factor_value, coupling_factor), (blocks, ro...]
    all_to_all x1 -> x2, blocking collectives: 36.1 us -> 110 us  [exchange(): return lax.all_to_all(x, 'rows', split_axis=0, concat_axis=0, tiled=True)]
    dot_general x14 -> x0, matrix products: 35.7 us -> none  [the longest x1 6.05 us: row_factors(): jnp.einsum('rba,rmbc->rmac', lower_factor, product, precision=highest)]
    gather x11 -> x0, local copies, waits for them, and re-layouts: 31.9 us -> none  [the longest x1 8.05 us: body(): returned.reshape(slot_total, block_size, block_size)[position]]
    select_n x4 -> x0, other arithmetic: 28.7 us -> none  [the longest x2 26.3 us: body(): asked_slots = jnp.where(filled, near_slots.reshape(-1)[safe_source], -1)]
    all_to_all x5 -> x3, starting transfers between devices: 48.5 us -> 21.7 us  [exchange(): return lax.all_to_all(x, 'rows', split_axis=0, concat_axis=0, tiled=True)]
  transfers between devices with their start and end apart: 5 -> 3, of which waited for: 4 -> 2; matrix products, arithmetic and copies ran while one was open for 24% -> 0% of each run, Pallas kernels for 0% -> 21%
where the time goes in v1:
time: 438 us; the launch traced here: 437 us
  Pallas kernels  225 us (51%)
  blocking collectives  110 us (25%)
  waiting for transfers between devices  76.5 us (17%)
  starting transfers between devices  21.7 us (5%)
  local copies, waits for them, and re-layouts  4.68 us (1%)
    all_to_all x2, blocking collectives, exchange(): return lax.all_to_all(x, 'rows', split_axis=0, concat_axis=0, tiled=True)  110 us
    pallas_call x1, Pallas kernels, body(): call(with_factors(row_kernel, factor_value, coupling_factor), (blocks, ro...  96.6 us
    pallas_call x1, Pallas kernels, body(): call(with_factors(invert_kernel, factor_value), (blocks, shape((count, PA...  83.2 us
    all_to_all x3, waiting for transfers between devices, exchange(): return lax.all_to_all(x, 'rows', split_axis=0, concat_axis=0, tiled=True)  76.5 us
    all_to_all x3, starting transfers between devices, exchange(): return lax.all_to_all(x, 'rows', split_axis=0, concat_axis=0, tiled=True)  21.7 us
    pallas_call x1, Pallas kernels, body(): pl.pallas_call(serve_kernel, grid=(total_slots // per,), out_shape=(shape...  11 us
    pallas_call x1, Pallas kernels, body(): call(with_factors(left_kernel, coupling_factor), shape((n_dev, 2 * SLOTS,...  9.49 us
  transfers between devices with their start and end apart: 3, of which 2 were waited for; matrix products, arithmetic and copies ran while one was open for 0% of the time, Pallas kernels for 21%

profile of v1, /device:TPU:1, one launch (start us, length us, event | category | flops | bytes accessed | tf_op | source)
XLA Modules:
  0.0 437.5 jit_solution(4996330063622129101)
XLA Ops:
  0.0 1.4 copy.9.dev_ref
  1.4 1.4 copy.10.slot_ref
  2.7 3.9 route.1
  6.6 11.5 %all-to-all-start = ((s32[128,1,2]{2,1,0:T(1,128)}), s32[128,1,2]{2,1,0:T(1,128)S(1)}, u32[]{:S(2)}, u32[]{:S(2)}) async-start(s32[128,1,2]{2,1,0:T(1,128)} %bitcast.21), calls=%async_computation | async-start | bytes 131072 | tf_op jit(solution)/shard_map/all_to_all | solution.py:332
  18.1 83.2 %invert.1 = (f32[14,128,128]{2,1,0:T(8,128)}, bf16[14,80,128]{2,1,0:T(8,128)(2,1)}) custom-call(bf16[14,128,128]{2,1,0:T(8,128)(2,1)} %refs_0_.3, bf16[14,128]{1,0:T(8,128)(2,1)} %refs_1_.5), custom_call_target="tpu_custom_call" | custom-call | flops 2000000000 | bytes 100000000 | tf_op jit(solution)/shard_map/invert/pallas_call | solution.py:365
  101.3 0.0 all-to-all-done
  101.3 0.0 copy-start.1
  101.3 0.6 copy-done.1
  101.9 11.0 %serve.1 = (bf16[256,80,128]{2,1,0:T(8,128)(2,1)}, s32[256]{0:T(256)}, s32[256]{0:T(256)}, s32[1]{0:T(128)}) custom-call(s32[128,2]{1,0:T(8,128)} %bitcast.20, bf16[14,80,128]{2,1,0:T(8,128)(2,1)} %get-tuple-element.20.pay), custom_call_target="tpu_custom_call" | custom-call | tf_op jit(solution)/shard_map/serve/pallas_call | solution.py:376
  113.0 73.7 %all_to_all.31 = bf16[128,160,128]{2,1,0:T(8,128)(2,1)} all-to-all(bf16[128,160,128]{2,1,0:T(8,128)(2,1)} %bitcast.17), channel_id=1, replica_groups=mesh['rows'=128] {'rows'}, dimensions={0} | all-to-all | bytes 10485760 | tf_op jit(solution)/shard_map/all_to_all | solution.py:332
  186.7 96.6 %row.1 = (f32[14,128,128]{2,1,0:T(8,128)}, f32[14,32,128]{2,1,0:T(8,128)}, bf16[256,32,128]{2,1,0:T(8,128)(2,1)}) custom-call(s32[42]{0:T(128)} %get-tuple-element.18.refs_0_, bf16[14,128,128]{2,1,0:T(8,128)(2,1)} %refs_0_.3, bf16[14,128]{1,0:T(8,128)(2,1)} %refs_1_.5, bf16[14,3,128,128]{3,2,1,0:T(8,128)(2,1)} %refs_4_.3, f32[32,1792]{1,0:T(8,128)} %refs_4_.2, ...), custom_call_target="tpu_custom_call" | custom-call | tf_op jit(solution)/shard_map/row/pallas_call | solution.py:401
  283.4 4.8 %all-to-all-start.2 = ((bf16[128,64,128]{2,1,0:T(8,128)(2,1)}), bf16[128,64,128]{2,1,0:T(8,128)(2,1)S(1)}, u32[]{:S(2)}, u32[]{:S(2)}) async-start(bf16[128,64,128]{2,1,0:T(8,128)(2,1)} %bitcast.18), calls=%async_computation.2 | async-start | bytes 4194304 | tf_op jit(solution)/shard_map/all_to_all | solution.py:332
  288.1 3.2 gram.1.refs_6_
  291.3 27.4 %all-to-all-done.2 = bf16[128,64,128]{2,1,0:T(8,128)(2,1)S(1)} async-done(((bf16[128,64,128]{2,1,0:T(8,128)(2,1)}), bf16[128,64,128]{2,1,0:T(8,128)(2,1)S(1)}, u32[]{:S(2)}, u32[]{:S(2)}) %all-to-all-start.2) | async-done | bytes 2097184 | tf_op jit(solution)/shard_map/all_to_all | solution.py:332
  318.7 0.0 copy-start
  318.7 1.3 copy-done
  320.1 9.5 %left.1 = bf16[128,4,32,128]{3,2,1,0:T(8,128)(2,1)} custom-call(s32[42]{0:T(128)} %get-tuple-element.18.refs_0_, s32[256]{0:T(256)} %get-tuple-element.21.refs_1_, s32[256]{0:T(256)} %get-tuple-element.22.refs_2_, s32[1]{0:T(128)} %get-tuple-element.23.refs_3_, bf16[256,32,128]{2,1,0:T(8,128)(2,1)} %bitcast.15, ...), custom_call_target="tpu_custom_call" | custom-call | tf_op jit(solution)/shard_map/left/pallas_call | solution.py:416
  329.6 5.4 %all-to-all-start.3 = ((bf16[128,128,128]{2,1,0:T(8,128)(2,1)}), bf16[128,128,128]{2,1,0:T(8,128)(2,1)}, u32[]{:S(2)}, u32[]{:S(2)}) async-start(bf16[128,128,128]{2,1,0:T(8,128)(2,1)} %bitcast.14), calls=%async_computation.3 | async-start | bytes 8388608 | tf_op jit(solution)/shard_map/all_to_all | solution.py:332
  335.0 3.9 own.1.refs_5_
  338.8 49.1 %all-to-all-done.3 = bf16[128,128,128]{2,1,0:T(8,128)(2,1)} async-done(((bf16[128,128,128]{2,1,0:T(8,128)(2,1)}), bf16[128,128,128]{2,1,0:T(8,128)(2,1)}, u32[]{:S(2)}, u32[]{:S(2)}) %all-to-all-start.3) | async-done | bytes 4194336 | tf_op jit(solution)/shard_map/all_to_all | solution.py:332
  387.9 7.8 %middle.1 = (f32[14,32,128]{2,1,0:T(8,128)}, bf16[256,32,128]{2,1,0:T(8,128)(2,1)}) custom-call(s32[42]{0:T(128)} %get-tuple-element.18.refs_0_, s32[256]{0:T(256)} %get-tuple-element.21.refs_1_, s32[256]{0:T(256)} %get-tuple-element.22.refs_2_, s32[1]{0:T(128)} %get-tuple-element.23.refs_3_, bf16[128,4,32,128]{3,2,1,0:T(8,128)(2,1)} %bitcast.9.refs_4_, ...), custom_call_target="tpu_custom_call" | custom-call | tf_op jit(solution)/shard_map/middle/pallas_call | solution.py:427
  395.7 35.8 %all_to_all.32 = bf16[128,64,128]{2,1,0:T(8,128)(2,1)} all-to-all(bf16[128,64,128]{2,1,0:T(8,128)(2,1)} %bitcast.19), channel_id=1, replica_groups=mesh['rows'=128] {'rows'}, dimensions={0} | all-to-all | bytes 4194304 | tf_op jit(solution)/shard_map/all_to_all | solution.py:332
  431.5 6.0 %result.1 = f32[32,1792]{1,0:T(8,128)} custom-call(s32[42]{0:T(128)} %get-tuple-element.18.refs_0_, bf16[256,32,128]{2,1,0:T(8,128)(2,1)} %bitcast.16, f32[14,32,128]{2,1,0:T(8,128)} %get-tuple-element.29.refs_2_, f32[14,128,128]{2,1,0:T(8,128)} %get-tuple-element.30.refs_3_, bf16[14,3,128,128]{3,2,1,0:T(8,128)(2,1)} %refs_4_.3), custom_call_target="tpu_custom_call" | custom-call | tf_op jit(solution)/shard_map/result/pallas_call | solution.py:436
Async XLA Ops:
  6.6 94.7 %all-to-all-start = ((s32[128,1,2]{2,1,0:T(1,128)}), s32[128,1,2]{2,1,0:T(1,128)S(1)}, u32[]{:S(2)}, u32[]{:S(2)}) async-start(s32[128,1,2]{2,1,0:T(1,128)} %bitcast.21), calls=%async_computation | async-start | bytes 131072 | tf_op jit(solution)/shard_map/all_to_all | solution.py:332
  101.3 0.6 copy-start.1
  283.4 35.4 %all-to-all-start.2 = ((bf16[128,64,128]{2,1,0:T(8,128)(2,1)}), bf16[128,64,128]{2,1,0:T(8,128)(2,1)S(1)}, u32[]{:S(2)}, u32[]{:S(2)}) async-start(bf16[128,64,128]{2,1,0:T(8,128)(2,1)} %bitcast.18), calls=%async_computation.2 | async-start | bytes 4194304 | tf_op jit(solution)/shard_map/all_to_all | solution.py:332
  318.7 1.3 copy-start
  329.6 58.4 %all-to-all-start.3 = ((bf16[128,128,128]{2,1,0:T(8,128)(2,1)}), bf16[128,128,128]{2,1,0:T(8,128)(2,1)}, u32[]{:S(2)}, u32[]{:S(2)}) async-start(bf16[128,128,128]{2,1,0:T(8,128)(2,1)} %bitcast.14), calls=%async_computation.3 | async-start | bytes 8388608 | tf_op jit(solution)/shard_map/all_to_all | solution.py:332

commit v2 on v1

v2 whole, which is shorter than its diff:
```python
import math

import jax
import jax.numpy as jnp
from jax import lax
from jax.experimental import pallas as pl
from jax.experimental.pallas import tpu as pltpu
from jax.sharding import PartitionSpec as P

F32 = jnp.float32
BF16 = jnp.bfloat16
BLK = 128
SLOTS = 2
TRI = 64
TAIL = 16
CHUNK = 2 * TRI + TAIL
SEG = 32
GROUP = BLK // SEG
CODE = 16
VMEM_LIMIT = 56 * 1024 * 1024
SM = pltpu.SMEM
VM = pltpu.VMEM
highest = lax.Precision.HIGHEST


def spec(space):
    return pl.BlockSpec(memory_space=space)


def call(kernel, out_shape, ins, outs, scratch=(), flops=0, moved=0, name=None):
    return pl.pallas_call(
        kernel,
        out_shape=out_shape,
        in_specs=[spec(s) for s in ins],
        out_specs=jax.tree.map(spec, outs),
        scratch_shapes=list(scratch),
        compiler_params=pltpu.CompilerParams(vmem_limit_bytes=VMEM_LIMIT),
        cost_estimate=pl.CostEstimate(flops=flops, bytes_accessed=moved, transcendentals=0),
        name=name,
    )


def iotas(rows, lanes=BLK):
    return (
        lax.broadcasted_iota(jnp.int32, (rows, lanes), 0),
        lax.broadcasted_iota(jnp.int32, (rows, lanes), 1),
    )


def split(x):
    hi = x.astype(BF16)
    lo = (x - hi.astype(F32)).astype(BF16)
    return hi, lo


def dot(a, b, ca=1, cb=0):
    return lax.dot_general(a, b, (((ca,), (cb,)), ((), ())), preferred_element_type=F32)


def dot_exact(a, b, ca=1, cb=0):
    return lax.dot_general(
        a, b, (((ca,), (cb,)), ((), ())), preferred_element_type=F32, precision=highest
    )


def rows_times_bf16(x, b, cb=0):
    hi, lo = split(x)
    both = dot(jnp.concatenate([hi, lo], axis=0), b, 1, cb)
    n = x.shape[0]
    return both[:n] + both[n:]


def stacked(b):
    hi, lo = split(b)
    return jnp.concatenate(
        [
            jnp.concatenate([hi, lo], axis=1),
            jnp.concatenate([hi, jnp.zeros_like(hi)], axis=1),
        ],
        axis=0,
    )


def dot_wide(a, b):
    hi, lo = split(a)
    out = dot(jnp.concatenate([hi, lo], axis=1), stacked(b))
    return out[:, :BLK] + out[:, BLK:]


def dot_rows(a, b, turned=False):
    n = a.shape[0]
    both = jnp.concatenate(split(a), axis=0)
    out = dot(both, jnp.concatenate(split(b), axis=0 if turned else 1), 1, 1 if turned else 0)
    return out[:n, :BLK] + (out[n:, :BLK] + out[:n, BLK:] + out[n:, BLK:])


def eliminate(packs):
    sub, lane = iotas(8)
    start = lane - lane % SEG
    parts = [[p[8 * t : 8 * t + 8] for t in range(SEG // 8)] for p in packs]
    for k in range(SEG - 1, -1, -1):
        i, j = divmod(k, 8)
        index = start + k
        at_k = lane == index
        for part in parts:
            row = jnp.broadcast_to(part[i][j : j + 1], (8, BLK))
            d = jnp.take_along_axis(row, index, axis=1, mode="promise_in_bounds")
            rs = lax.rsqrt(d)
            v = jnp.where(at_k, rs, row * rs)
            scaled = jnp.where(at_k, 1.0 + rs * rs, v * rs)
            for t in range(i + 1):
                if t == i and j == 0:
                    part[t] = jnp.where(sub == 0, v, part[t])
                    continue
                col = jnp.take_along_axis(part[t], index, axis=1, mode="promise_in_bounds")
                new = part[t] - col * scaled
                if t == i:
                    new = jnp.where(sub < j, new, jnp.where(sub == j, v, part[t]))
                part[t] = new
    return [jnp.concatenate(part, axis=0) for part in parts]


def factor(z, count):
    sub, lane = iotas(SEG)
    seg = lane // SEG
    groups = -(-count // GROUP)
    for kb in range(GROUP - 1, -1, -1):
        r0 = kb * SEG
        panels = [
            [z[min(q * GROUP + g, count - 1), r0 : r0 + SEG, :] for g in range(GROUP)]
            for q in range(groups)
        ]
        packs = []
        for q in range(groups):
            pack = jnp.zeros((SEG, BLK), F32)
            for g in range(GROUP):
                shift = (SEG * g - r0) % BLK
                x = panels[q][g]
                x = pltpu.roll(x, shift, 1) if shift else x
                pack = jnp.where(seg == g, x, pack)
            packs.append(pack)
        packs = eliminate(packs)
        eye = (lane - r0 == sub).astype(F32)
        for q in range(groups):
            w = jnp.where(lane % SEG >= sub, packs[q], 0.0)
            wide = jnp.concatenate([jnp.where(seg == g, w, 0.0) for g in range(GROUP)], axis=0)
            tall = jnp.concatenate(
                [jnp.where(seg == kb, eye, panels[q][g]) for g in range(GROUP)], axis=0
            )
            v = dot_wide(wide, tall)
            if kb:
                v2 = dot_wide(wide.T, v)
            for g in range(GROUP):
                b = q * GROUP + g
                if b >= count:
                    continue
                z[b, r0 : r0 + SEG, :] = v[SEG * g : SEG * g + SEG]
                if kb:
                    pads = [jnp.zeros((r0, BLK), F32), v2[SEG * g : SEG * g + SEG]]
                    if r0 + SEG < BLK:
                        pads.append(jnp.zeros((BLK - r0 - SEG, BLK), F32))
                    top = z[b, 0:r0, :]
                    update = dot_wide(top, jnp.concatenate(pads, axis=0))
                    _, top_lane = iotas(r0)
                    z[b, 0:r0, :] = jnp.where(top_lane // SEG == kb, 0.0, top) - update


def build_diag(noise, shift, b, factor_value):
    sub, lane = iotas(BLK)
    n = noise[b]
    eye = (sub == lane).astype(BF16)
    turned = dot(eye, n, 1, 1)
    sym = (n.astype(F32) + turned) * (0.5 * factor_value)
    shift_row = shift[pl.ds(b, 1), :].astype(F32)
    return sym + jnp.where(sub == lane, shift_row, 0.0)


def route_kernel(me_ref, dev_ref, slot_ref, ask_ref, pos_ref, count_ref):
    n_dev = count_ref.shape[0]
    me = me_ref[0]

    def clear(t, carry):
        count_ref[t] = 0
        ask_ref[t, 0] = 0
        return carry

    lax.fori_loop(0, n_dev, clear, 0, unroll=16)
    for i in range(dev_ref.shape[1]):
        for m in range(3):
            t = me - 1 - dev_ref[m, i]
            t = jnp.where(t < 0, t + n_dev, t)
            rank = count_ref[t]
            count_ref[t] = rank + 1
            code = slot_ref[m, i] + 1
            ask_ref[t, 0] = ask_ref[t, 0] + jnp.where(rank == 0, code, code * CODE)
            pos_ref[i * 3 + m] = t * SLOTS + rank


def list_kernel(incoming, list_pos, list_slot, list_count):
    def one(t, n):
        code = incoming[t, 0]
        for r in range(SLOTS):
            slot = (code % CODE if r == 0 else code // CODE) - 1
            list_pos[n] = t * SLOTS + r
            list_slot[n] = slot
            n = n + (slot >= 0).astype(jnp.int32)
        return n

    list_count[0] = lax.fori_loop(0, incoming.shape[0], one, 0, unroll=8)


def invert_kernel(factor_value, noise, shift, x_out, tri_out, tail_out, z):
    count = noise.shape[0]
    for b in range(count):
        z[b] = build_diag(noise, shift, b, factor_value)
    factor(z, count)
    sub, lane = iotas(BLK)
    top_sub, top_lane = iotas(TRI)
    low_eye = (top_lane == top_sub + TRI).astype(BF16)
    tail_sub, _ = iotas(TAIL)
    for b in range(count):
        x = jnp.where(lane >= sub, z[b], 0.0)
        x_out[b] = x
        bottom = jnp.concatenate([x[TRI:].astype(BF16), jnp.zeros((TRI, BLK), BF16)], axis=0)
        turned = dot(low_eye, bottom, 1, 1)
        tri = jnp.where(top_lane > top_sub, x[:TRI], jnp.where(top_lane < top_sub, turned, 0.0))
        tri_out[b] = tri.astype(BF16)
        diag = jnp.sum(jnp.where(sub == lane, x, 0.0), axis=0, keepdims=True)
        hi, lo = split(diag)
        hi, lo = hi.astype(F32), lo.astype(F32)
        for r in range(SLOTS):
            tail = jnp.where(
                tail_sub == 2 * r, hi, jnp.where(tail_sub == 2 * r + 1, lo, 0.0)
            )
            tail_out[r, b] = tail.astype(BF16)


def serve_kernel(incoming, tri, tail, out):
    per = out.shape[0]
    first = pl.program_id(0) * per
    for t in range(per):
        code = incoming[first + t, 0]
        slots = [jnp.maximum(code % CODE - 1, 0), jnp.maximum(code // CODE - 1, 0)]
        for r in range(SLOTS):
            out[t, r * TRI : (r + 1) * TRI] = tri[slots[r]]
        out[t, SLOTS * TRI :] = tail[0, slots[0]] + tail[1, slots[1]]


def gram_kernel(x, e_out):
    for b in range(x.shape[0]):
        e_out[b] = dot_exact(x[b], x[b], 0, 0)


def row_kernel(
    factor_value, coupling_factor, pos, noise, shift, couplings, vectors, arrived,
    w_out, y_out, send, z, near, tails, sems,
):
    count = noise.shape[0]
    n_vec = vectors.shape[0]
    copies = []
    for q in range(3 * count):
        at = pos[q]
        row = pl.multiple_of((at % SLOTS) * TRI, TRI)
        for k, (source, target) in enumerate(
            (
                (arrived.at[at // SLOTS, pl.ds(row, TRI)], near.at[q]),
                (arrived.at[at // SLOTS, pl.ds(SLOTS * TRI, TAIL)], tails.at[q]),
            )
        ):
            copy = pltpu.make_async_copy(source, target, sems.at[q, k])
            copy.start()
            copies.append(copy)
    for b in range(count):
        z[b] = build_diag(noise, shift, b, factor_value)
    for copy in copies:
        copy.wait()
    top_sub, top_lane = iotas(TRI)

    tail_sub, _ = iotas(TAIL)
    zero = jnp.zeros((TRI, BLK), BF16)

    def schur(b, carry):
        wide = []
        for m in range(3):
            q = b * 3 + m
            tri = near[q].astype(F32)
            upper = jnp.where(top_lane > top_sub, tri, 0.0).astype(BF16)
            lower = pltpu.roll(jnp.where(top_lane < top_sub, tri, 0.0), TRI, 1).astype(BF16)
            rank = pos[q] % SLOTS
            diag = jnp.sum(
                jnp.where(tail_sub // 2 == rank, tails[q].astype(F32), 0.0),
                axis=0,
                keepdims=True,
            )
            c = couplings[b, m]
            y = dot(c, jnp.concatenate([upper, zero], axis=0), 1, 1)
            y = y + dot(c, jnp.concatenate([zero, lower], axis=0), 1, 0)
            wide.append((y + c.astype(F32) * diag).astype(BF16))
        wide = jnp.concatenate(wide, axis=1)
        z[b] = z[b] - dot(wide, wide, 1, 1) * (coupling_factor * coupling_factor)
        return carry

    lax.fori_loop(0, count, schur, 0, unroll=2)
    factor(z, count)
    sub, lane = iotas(BLK)
    for b in range(count):
        w = jnp.where(lane >= sub, z[b], 0.0)
        w_out[b] = w
        y = dot_rows(vectors[:, b * BLK : (b + 1) * BLK], w)
        y_out[b] = y
        for m in range(3):
            p = rows_times_bf16(y, couplings[b, m]) * coupling_factor
            send[pos[b * 3 + m]] = p.astype(BF16)


def own_kernel(factor_value, noise, shift, y, out):
    for b in range(noise.shape[0]):
        d = build_diag(noise, shift, b, factor_value)
        out[b] = dot_rows(y[b], d)


def left_kernel(
    coupling_factor, pos, list_pos, list_slot, list_count, arrived, y, e, couplings, send, left, total
):
    count = y.shape[0]
    n_vec = y.shape[1]
    total[...] = jnp.zeros_like(total)

    def add(t, carry):
        slot = list_slot[t]
        total[slot] += arrived[list_pos[t]].astype(F32)
        return carry

    lax.fori_loop(0, list_count[0], add, 0)
    for b in range(count):
        u = dot_rows(total[b], e[b])
        left[b] = (y[b] - u).astype(BF16)
        for m in range(3):
            p = rows_times_bf16(u, couplings[b, m]) * coupling_factor
            at = pos[b * 3 + m]
            send[at // SLOTS, SLOTS + at % SLOTS] = p.astype(BF16)

    def give(t, carry):
        at = list_pos[t]
        send[at // SLOTS, at % SLOTS] = left[list_slot[t]]
        return carry

    lax.fori_loop(0, list_count[0], give, 0)


def middle_kernel(
    coupling_factor, pos, list_pos, list_slot, list_count, arrived, own, e, couplings,
    middle, send, total, answer,
):
    count = own.shape[0]
    total[...] = jnp.zeros_like(total)

    def add(t, carry):
        slot = list_slot[t]
        at = list_pos[t]
        total[slot] += arrived[at // SLOTS, SLOTS + at % SLOTS].astype(F32)
        return carry

    lax.fori_loop(0, list_count[0], add, 0)
    for b in range(count):
        near = jnp.zeros(total.shape[1:], F32)
        for m in range(3):
            at = pos[b * 3 + m]
            near = near + dot(arrived[at // SLOTS, at % SLOTS], couplings[b, m], 1, 1)
        mid = own[b] - total[b] + near * coupling_factor
        middle[b] = mid
        answer[b] = dot_rows(mid, e[b]).astype(BF16)

    def give(t, carry):
        send[list_pos[t]] = answer[list_slot[t]]
        return carry

    lax.fori_loop(0, list_count[0], give, 0)


def result_kernel(coupling_factor, pos, arrived, middle, w, couplings, out):
    for b in range(middle.shape[0]):
        near = jnp.zeros(middle.shape[1:], F32)
        for m in range(3):
            near = near + dot(arrived[pos[b * 3 + m]], couplings[b, m], 1, 1)
        mid = middle[b] - near * coupling_factor
        out[:, b * BLK : (b + 1) * BLK] = dot_rows(mid, w[b], True)


def exchange(x):
    return lax.all_to_all(x, "rows", split_axis=0, concat_axis=0, tiled=True)


def body(diag_noise, couplings, shifts, near_devices, near_slots, vectors):
    n_dev = lax.axis_size("rows")
    me = lax.axis_index("rows").astype(jnp.int32).reshape(1)
    count = diag_noise.shape[0]
    n_vec = vectors.shape[0]
    total_slots = n_dev * SLOTS
    factor_value = 0.5 / math.sqrt(BLK)
    coupling_factor = 0.4 / math.sqrt(BLK)

    def shape(dims, dtype=F32):
        return jax.ShapeDtypeStruct(dims, dtype)

    blocks = shape((count, BLK, BLK))
    rows = shape((count, n_vec, BLK))

    def with_factors(kernel, *values):
        def wrapped(*refs):
            kernel(*values, *refs)

        return wrapped

    ask, pos = call(
        route_kernel,
        (shape((n_dev, 1), jnp.int32), shape((3 * count,), jnp.int32)),
        [SM, SM, SM],
        (SM, SM),
        [SM((n_dev,), jnp.int32)],
        name="route",
    )(me, near_devices.T, near_slots.T)
    incoming = exchange(ask)
    x, tri, tail = call(
        with_factors(invert_kernel, factor_value),
        (
            blocks,
            shape((count, TRI, BLK), BF16),
            shape((SLOTS, count, TAIL, BLK), BF16),
        ),
        [VM, VM],
        (VM, VM, VM),
        [VM((count, BLK, BLK), F32)],
        flops=2 * 10**9,
        moved=10**8,
        name="invert",
    )(diag_noise, shifts)
    per = 16
    answer = pl.pallas_call(
        serve_kernel,
        grid=(n_dev // per,),
        out_shape=shape((n_dev, CHUNK, BLK), BF16),
        in_specs=[spec(SM), spec(VM), spec(VM)],
        out_specs=pl.BlockSpec((per, CHUNK, BLK), lambda g: (g, 0, 0)),
        compiler_params=pltpu.CompilerParams(dimension_semantics=("arbitrary",)),
        name="serve",
    )(incoming, tri, tail)
    arrived = exchange(answer)
    lists = call(
        list_kernel,
        (
            shape((total_slots + SLOTS,), jnp.int32),
            shape((total_slots + SLOTS,), jnp.int32),
            shape((1,), jnp.int32),
        ),
        [SM],
        (SM, SM, SM),
        flops=10**9,
        moved=10**7,
        name="list",
    )(incoming)
    e = call(
        gram_kernel, blocks, [VM], VM, flops=10**9, moved=10**7, name="gram"
    )(x)
    w, y, push = call(
        with_factors(row_kernel, factor_value, coupling_factor),
        (blocks, rows, shape((total_slots, n_vec, BLK), BF16)),
        [SM, VM, VM, VM, VM, pl.ANY],
        (VM, VM, VM),
        [
            VM((count, BLK, BLK), F32),
            VM((3 * count, TRI, BLK), BF16),
            VM((3 * count, TAIL, BLK), BF16),
            pltpu.SemaphoreType.DMA((3 * count, 2)),
        ],
        name="row",
    )(pos, diag_noise, shifts, couplings, vectors, arrived)
    pushed = exchange(push.reshape(n_dev, SLOTS * n_vec, BLK)).reshape(total_slots, n_vec, BLK)
    own = call(
        with_factors(own_kernel, factor_value),
        rows, [VM, VM, VM], VM, flops=10**9, moved=10**7, name="own",
    )(diag_noise, shifts, y)
    both = call(
        with_factors(left_kernel, coupling_factor),
        shape((n_dev, 2 * SLOTS, n_vec, BLK), BF16),
        [SM] * 4 + [VM] * 4,
        VM,
        [VM((count, n_vec, BLK), BF16), VM((count, n_vec, BLK), F32)],
        name="left",
    )(pos, *lists, pushed, y, e, couplings)
    both = exchange(both.reshape(n_dev, 2 * SLOTS * n_vec, BLK)).reshape(
        n_dev, 2 * SLOTS, n_vec, BLK
    )
    middle, back = call(
        with_factors(middle_kernel, coupling_factor),
        (rows, shape((total_slots, n_vec, BLK), BF16)),
        [SM] * 4 + [VM] * 4,
        (VM, VM),
        [VM((count, n_vec, BLK), F32), VM((count, n_vec, BLK), BF16)],
        name="middle",
    )(pos, *lists, both, own, e, couplings)
    back = exchange(back.reshape(n_dev, SLOTS * n_vec, BLK)).reshape(total_slots, n_vec, BLK)
    return call(
        with_factors(result_kernel, coupling_factor),
        shape((n_vec, count * BLK)),
        [SM] + [VM] * 4,
        VM,
        name="result",
    )(pos, back, middle, w, couplings)


def solution(mesh):
    return jax.shard_map(
        body,
        mesh=mesh,
        in_specs=(
            P("rows", None, None),
            P("rows", None, None, None),
            P("rows", None),
            P("rows", None),
            P("rows", None),
            P(None, "rows"),
        ),
        out_specs=P(None, "rows"),
        check_vma=False,
    )
```

time: 438 us -> 294 us (0.67)
  Pallas kernels: 225 us -> 92.1 us
  blocking collectives: 110 us -> 104 us
    pallas_call x1, Pallas kernels: 96.6 us -> 29.5 us  [body(): call(with_factors(row_kernel, factor_value, coupling_factor), (blocks, ro...]
    pallas_call x3 -> x4, Pallas kernels: 98.1 us -> 31.3 us  [the longest x1 18.8 us: body(): call(with_factors(invert_kernel, factor_value), (blocks, shape((count, TR...]
    all_to_all x2, blocking collectives: 110 us -> 104 us  [exchange(): return lax.all_to_all(x, 'rows', split_axis=0, concat_axis=0, tiled=True)]
  transfers between devices with their start and end apart: 3 -> 3, of which waited for: 2 -> 2; matrix products, arithmetic and copies ran while one was open for 0% -> 0% of each run, Pallas kernels for 21% -> 10%
where the time goes in v2:
time: 294 us; the launch traced here: 293 us
  blocking collectives  104 us (35%)
  Pallas kernels  92.1 us (31%)
  waiting for transfers between devices  72.2 us (25%)
  starting transfers between devices  22.3 us (8%)
    all_to_all x2, blocking collectives, exchange(): return lax.all_to_all(x, 'rows', split_axis=0, concat_axis=0, tiled=True)  104 us
    all_to_all x3, waiting for transfers between devices, exchange(): return lax.all_to_all(x, 'rows', split_axis=0, concat_axis=0, tiled=True)  72.2 us
    pallas_call x1, Pallas kernels, body(): call(with_factors(row_kernel, factor_value, coupling_factor), (blocks, ro...  29.5 us
    all_to_all x3, starting transfers between devices, exchange(): return lax.all_to_all(x, 'rows', split_axis=0, concat_axis=0, tiled=True)  22.3 us
    pallas_call x1, Pallas kernels, body(): call(with_factors(invert_kernel, factor_value), (blocks, shape((count, TR...  18.8 us
    pallas_call x1, Pallas kernels, body(): call(with_factors(middle_kernel, coupling_factor), (rows, shape((total_sl...  9.11 us
    pallas_call x1, Pallas kernels, body(): call(with_factors(left_kernel, coupling_factor), shape((n_dev, 2 * SLOTS,...  8.38 us
    pallas_call x1, Pallas kernels, body(): call(with_factors(result_kernel, coupling_factor), shape((n_vec, count *...  6.3 us
  transfers between devices with their start and end apart: 3, of which 2 were waited for; matrix products, arithmetic and copies ran while one was open for 0% of the time, Pallas kernels for 10%

profile of v2, /device:TPU:1, one launch (start us, length us, event | category | flops | bytes accessed | tf_op | source)
XLA Modules:
  0.0 293.0 jit_solution(16933148054494326328)
XLA Ops:
  0.0 2.7 route.1
  2.8 11.5 %all-to-all-start = ((s32[128,1,1]{2,1,0:T(1,128)}), s32[128,1,1]{2,1,0:T(1,128)S(1)}, u32[]{:S(2)}, u32[]{:S(2)}) async-start(s32[128,1,1]{2,1,0:T(1,128)} %bitcast.18), calls=%async_computation | async-start | bytes 131072 | tf_op jit(solution)/shard_map/all_to_all | solution.py:391
  14.3 18.8 %invert.1 = (f32[14,128,128]{2,1,0:T(8,128)}, bf16[14,64,128]{2,1,0:T(8,128)(2,1)}, bf16[2,14,16,128]{3,2,1,0:T(8,128)(2,1)}) custom-call(bf16[14,128,128]{2,1,0:T(8,128)(2,1)} %refs_0_.3, bf16[14,128]{1,0:T(8,128)(2,1)} %refs_1_.5), custom_call_target="tpu_custom_call" | custom-call | flops 2000000000 | bytes 100000000 | tf_op jit(solution)/shard_map/invert/pallas_call | solution.py:424
  33.1 0.0 all-to-all-done
  33.1 0.0 copy-start.1
  33.1 0.6 copy-done.1
  33.7 6.0 %serve.1 = bf16[128,144,128]{2,1,0:T(8,128)(2,1)} custom-call(s32[128,1]{1,0:T(8,128)} %bitcast.16, bf16[14,64,128]{2,1,0:T(8,128)(2,1)} %get-tuple-element.23.tri, bf16[2,14,16,128]{3,2,1,0:T(8,128)(2,1)} %get-tuple-element.24.tail), custom_call_target="tpu_custom_call" | custom-call | tf_op jit(solution)/shard_map/serve/pallas_call | solution.py:439
  39.7 68.3 %all_to_all.31.refs_5_ = bf16[128,144,128]{2,1,0:T(8,128)(2,1)} all-to-all(bf16[128,144,128]{2,1,0:T(8,128)(2,1)} %serve.1), channel_id=1, replica_groups=mesh['rows'=128] {'rows'}, dimensions={0} | all-to-all | bytes 9437184 | tf_op jit(solution)/shard_map/all_to_all | solution.py:391
  108.0 29.5 %row.1 = (f32[14,128,128]{2,1,0:T(8,128)}, f32[14,32,128]{2,1,0:T(8,128)}, bf16[256,32,128]{2,1,0:T(8,128)(2,1)}) custom-call(s32[42]{0:T(128)} %get-tuple-element.18.refs_0_, bf16[14,128,128]{2,1,0:T(8,128)(2,1)} %refs_0_.3, bf16[14,128]{1,0:T(8,128)(2,1)} %refs_1_.5, bf16[14,3,128,128]{3,2,1,0:T(8,128)(2,1)} %refs_4_.3, f32[32,1792]{1,0:T(8,128)} %refs_4_.2, ...), custom_call_target="tpu_custom_call" | custom-call | tf_op jit(solution)/shard_map/row/pallas_call | solution.py:465
  137.5 5.1 %all-to-all-start.2 = ((bf16[128,64,128]{2,1,0:T(8,128)(2,1)}), bf16[128,64,128]{2,1,0:T(8,128)(2,1)S(1)}, u32[]{:S(2)}, u32[]{:S(2)}) async-start(bf16[128,64,128]{2,1,0:T(8,128)(2,1)} %bitcast.14), calls=%async_computation.2 | async-start | bytes 4194304 | tf_op jit(solution)/shard_map/all_to_all | solution.py:391
  142.6 3.1 %gram.1.refs_6_ = f32[14,128,128]{2,1,0:T(8,128)} custom-call(f32[14,128,128]{2,1,0:T(8,128)} %get-tuple-element.27.x), custom_call_target="tpu_custom_call" | custom-call | flops 1000000000 | bytes 10000000 | tf_op jit(solution)/shard_map/gram/pallas_call | solution.py:462
  145.7 3.8 %list.1 = (s32[258]{0:T(512)}, s32[258]{0:T(512)}, s32[1]{0:T(128)}) custom-call(s32[128,1]{1,0:T(8,128)} %bitcast.17), custom_call_target="tpu_custom_call" | custom-call | flops 1000000000 | bytes 10000000 | tf_op jit(solution)/shard_map/list/pallas_call | solution.py:449
  149.4 23.7 %all-to-all-done.2 = bf16[128,64,128]{2,1,0:T(8,128)(2,1)S(1)} async-done(((bf16[128,64,128]{2,1,0:T(8,128)(2,1)}), bf16[128,64,128]{2,1,0:T(8,128)(2,1)S(1)}, u32[]{:S(2)}, u32[]{:S(2)}) %all-to-all-start.2) | async-done | bytes 2097184 | tf_op jit(solution)/shard_map/all_to_all | solution.py:391
  173.1 0.0 copy-start
  173.1 1.3 copy-done
  174.4 8.4 %left.1 = bf16[128,4,32,128]{3,2,1,0:T(8,128)(2,1)} custom-call(s32[42]{0:T(128)} %get-tuple-element.18.refs_0_, s32[258]{0:T(512)} %get-tuple-element.20.refs_1_, s32[258]{0:T(512)} %get-tuple-element.21.refs_2_, s32[1]{0:T(128)} %get-tuple-element.22.refs_3_, bf16[256,32,128]{2,1,0:T(8,128)(2,1)} %bitcast.13, ...), custom_call_target="tpu_custom_call" | custom-call | tf_op jit(solution)/shard_map/left/pallas_call | solution.py:483
  182.8 5.7 %all-to-all-start.3 = ((bf16[128,128,128]{2,1,0:T(8,128)(2,1)}), bf16[128,128,128]{2,1,0:T(8,128)(2,1)}, u32[]{:S(2)}, u32[]{:S(2)}) async-start(bf16[128,128,128]{2,1,0:T(8,128)(2,1)} %bitcast.11), calls=%async_computation.3 | async-start | bytes 8388608 | tf_op jit(solution)/shard_map/all_to_all | solution.py:391
  188.5 4.4 %own.1.refs_5_ = f32[14,32,128]{2,1,0:T(8,128)} custom-call(bf16[14,128,128]{2,1,0:T(8,128)(2,1)} %refs_0_.3, bf16[14,128]{1,0:T(8,128)(2,1)} %refs_1_.5, f32[14,32,128]{2,1,0:T(8,128)} %get-tuple-element.26.refs_5_.refs_2_), custom_call_target="tpu_custom_call" | custom-call | flops 1000000000 | bytes 10000000 | tf_op jit(solution)/shard_map/own/pallas_call | solution.py:479
  192.9 48.5 %all-to-all-done.3 = bf16[128,128,128]{2,1,0:T(8,128)(2,1)} async-done(((bf16[128,128,128]{2,1,0:T(8,128)(2,1)}), bf16[128,128,128]{2,1,0:T(8,128)(2,1)}, u32[]{:S(2)}, u32[]{:S(2)}) %all-to-all-start.3) | async-done | bytes 4194336 | tf_op jit(solution)/shard_map/all_to_all | solution.py:391
  241.5 9.1 %middle.1 = (f32[14,32,128]{2,1,0:T(8,128)}, bf16[256,32,128]{2,1,0:T(8,128)(2,1)}) custom-call(s32[42]{0:T(128)} %get-tuple-element.18.refs_0_, s32[258]{0:T(512)} %get-tuple-element.20.refs_1_, s32[258]{0:T(512)} %get-tuple-element.21.refs_2_, s32[1]{0:T(128)} %get-tuple-element.22.refs_3_, bf16[128,4,32,128]{3,2,1,0:T(8,128)(2,1)} %bitcast.8.refs_4_, ...), custom_call_target="tpu_custom_call" | custom-call | tf_op jit(solution)/shard_map/middle/pallas_call | solution.py:494
  250.6 36.1 %all_to_all.32 = bf16[128,64,128]{2,1,0:T(8,128)(2,1)} all-to-all(bf16[128,64,128]{2,1,0:T(8,128)(2,1)} %bitcast.15), channel_id=1, replica_groups=mesh['rows'=128] {'rows'}, dimensions={0} | all-to-all | bytes 4194304 | tf_op jit(solution)/shard_map/all_to_all | solution.py:391
  286.7 6.3 %result.1 = f32[32,1792]{1,0:T(8,128)} custom-call(s32[42]{0:T(128)} %get-tuple-element.18.refs_0_, bf16[256,32,128]{2,1,0:T(8,128)(2,1)} %bitcast.12, f32[14,32,128]{2,1,0:T(8,128)} %get-tuple-element.29.refs_2_, f32[14,128,128]{2,1,0:T(8,128)} %get-tuple-element.30.refs_3_, bf16[14,3,128,128]{3,2,1,0:T(8,128)(2,1)} %refs_4_.3), custom_call_target="tpu_custom_call" | custom-call | tf_op jit(solution)/shard_map/result/pallas_call | solution.py:503
Async XLA Ops:
  2.8 30.3 %all-to-all-start = ((s32[128,1,1]{2,1,0:T(1,128)}), s32[128,1,1]{2,1,0:T(1,128)S(1)}, u32[]{:S(2)}, u32[]{:S(2)}) async-start(s32[128,1,1]{2,1,0:T(1,128)} %bitcast.18), calls=%async_computation | async-start | bytes 131072 | tf_op jit(solution)/shard_map/all_to_all | solution.py:391
  33.1 0.6 copy-start.1
  137.5 35.6 %all-to-all-start.2 = ((bf16[128,64,128]{2,1,0:T(8,128)(2,1)}), bf16[128,64,128]{2,1,0:T(8,128)(2,1)S(1)}, u32[]{:S(2)}, u32[]{:S(2)}) async-start(bf16[128,64,128]{2,1,0:T(8,128)(2,1)} %bitcast.14), calls=%async_computation.2 | async-start | bytes 4194304 | tf_op jit(solution)/shard_map/all_to_all | solution.py:391
  173.1 1.3 copy-start
  182.8 58.6 %all-to-all-start.3 = ((bf16[128,128,128]{2,1,0:T(8,128)(2,1)}), bf16[128,128,128]{2,1,0:T(8,128)(2,1)}, u32[]{:S(2)}, u32[]{:S(2)}) async-start(bf16[128,128,128]{2,1,0:T(8,128)(2,1)} %bitcast.11), calls=%async_computation.3 | async-start | bytes 8388608 | tf_op jit(solution)/shard_map/all_to_all | solution.py:391

commit v3 on v2

--- a/solution.py
+++ b/solution.py
@@ -17,7 +17,7 @@
 SEG = 32
 GROUP = BLK // SEG
 CODE = 16
-VMEM_LIMIT = 56 * 1024 * 1024
+VMEM_LIMIT = 16 * 1024 * 1024
 SM = pltpu.SMEM
 VM = pltpu.VMEM
 highest = lax.Precision.HIGHEST
@@ -236,14 +236,15 @@
 
 
 def serve_kernel(incoming, tri, tail, out):
-    per = out.shape[0]
-    first = pl.program_id(0) * per
-    for t in range(per):
-        code = incoming[first + t, 0]
+    def one(t, carry):
+        code = incoming[t, 0]
         slots = [jnp.maximum(code % CODE - 1, 0), jnp.maximum(code // CODE - 1, 0)]
         for r in range(SLOTS):
             out[t, r * TRI : (r + 1) * TRI] = tri[slots[r]]
         out[t, SLOTS * TRI :] = tail[0, slots[0]] + tail[1, slots[1]]
+        return carry
+
+    lax.fori_loop(0, out.shape[0], one, 0, unroll=8)
 
 
 def gram_kernel(x, e_out):
@@ -253,27 +254,12 @@
 
 def row_kernel(
     factor_value, coupling_factor, pos, noise, shift, couplings, vectors, arrived,
-    w_out, y_out, send, z, near, tails, sems,
+    w_out, y_out, send, z,
 ):
     count = noise.shape[0]
     n_vec = vectors.shape[0]
-    copies = []
-    for q in range(3 * count):
-        at = pos[q]
-        row = pl.multiple_of((at % SLOTS) * TRI, TRI)
-        for k, (source, target) in enumerate(
-            (
-                (arrived.at[at // SLOTS, pl.ds(row, TRI)], near.at[q]),
-                (arrived.at[at // SLOTS, pl.ds(SLOTS * TRI, TAIL)], tails.at[q]),
-            )
-        ):
-            copy = pltpu.make_async_copy(source, target, sems.at[q, k])
-            copy.start()
-            copies.append(copy)
     for b in range(count):
         z[b] = build_diag(noise, shift, b, factor_value)
-    for copy in copies:
-        copy.wait()
     top_sub, top_lane = iotas(TRI)
 
     tail_sub, _ = iotas(TAIL)
@@ -283,12 +269,14 @@
         wide = []
         for m in range(3):
             q = b * 3 + m
-            tri = near[q].astype(F32)
+            at = pos[q]
+            dev, rank = at // SLOTS, at % SLOTS
+            first = pl.multiple_of(rank * TRI, TRI)
+            tri = arrived[dev, pl.ds(first, TRI), :].astype(F32)
             upper = jnp.where(top_lane > top_sub, tri, 0.0).astype(BF16)
             lower = pltpu.roll(jnp.where(top_lane < top_sub, tri, 0.0), TRI, 1).astype(BF16)
-            rank = pos[q] % SLOTS
             diag = jnp.sum(
-                jnp.where(tail_sub // 2 == rank, tails[q].astype(F32), 0.0),
+                jnp.where(tail_sub // 2 == rank, arrived[dev, SLOTS * TRI :, :].astype(F32), 0.0),
                 axis=0,
                 keepdims=True,
             )
@@ -435,14 +423,11 @@
         moved=10**8,
         name="invert",
     )(diag_noise, shifts)
-    per = 16
-    answer = pl.pallas_call(
+    answer = call(
         serve_kernel,
-        grid=(n_dev // per,),
-        out_shape=shape((n_dev, CHUNK, BLK), BF16),
-        in_specs=[spec(SM), spec(VM), spec(VM)],
-        out_specs=pl.BlockSpec((per, CHUNK, BLK), lambda g: (g, 0, 0)),
-        compiler_params=pltpu.CompilerParams(dimension_semantics=("arbitrary",)),
+        shape((n_dev, CHUNK, BLK), BF16),
+        [SM, VM, VM],
+        VM,
         name="serve",
     )(incoming, tri, tail)
     arrived = exchange(answer)
@@ -465,14 +450,9 @@
     w, y, push = call(
         with_factors(row_kernel, factor_value, coupling_factor),
         (blocks, rows, shape((total_slots, n_vec, BLK), BF16)),
-        [SM, VM, VM, VM, VM, pl.ANY],
+        [SM, VM, VM, VM, VM, VM],
         (VM, VM, VM),
-        [
-            VM((count, BLK, BLK), F32),
-            VM((3 * count, TRI, BLK), BF16),
-            VM((3 * count, TAIL, BLK), BF16),
-            pltpu.SemaphoreType.DMA((3 * count, 2)),
-        ],
+        [VM((count, BLK, BLK), F32)],
         name="row",
     )(pos, diag_noise, shifts, couplings, vectors, arrived)
     pushed = exchange(push.reshape(n_dev, SLOTS * n_vec, BLK)).reshape(total_slots, n_vec, BLK)

time: 294 us -> 284 us (0.966)
  Pallas kernels: 92.1 us -> 71.1 us
  local copies, waits for them, and re-layouts: 1.94 us -> 13.3 us
    unnamed x4 -> x42, local copies, waits for them, and re-layouts: 1.94 us -> 13.3 us
    pallas_call x1, Pallas kernels: 29.5 us -> 25.3 us  [body(): call(with_factors(row_kernel, factor_value, coupling_factor), (blocks, ro...]
    pallas_call x1, Pallas kernels: 8.38 us -> 4.54 us  [body(): call(with_factors(left_kernel, coupling_factor), shape((n_dev, 2 * SLOTS,...]
    pallas_call x1, Pallas kernels: 6.02 us -> 2.9 us  [body(): call(serve_kernel, shape((n_dev, CHUNK, BLK), BF16), [SM, VM, VM], VM, na...]
  transfers between devices with their start and end apart: 3 -> 3, of which waited for: 2 -> 2; matrix products, arithmetic and copies ran while one was open for 0% -> 0% of each run, Pallas kernels for 10% -> 9%
where the time goes in v3:
time: 284 us; the launch traced here: 283 us
  blocking collectives  102 us (36%)
  waiting for transfers between devices  74 us (26%)
  Pallas kernels  71.1 us (25%)
  starting transfers between devices  22.3 us (8%)
  local copies, waits for them, and re-layouts  13.3 us (5%)
    all_to_all x2, blocking collectives, exchange(): return lax.all_to_all(x, 'rows', split_axis=0, concat_axis=0, tiled=True)  102 us
    all_to_all x3, waiting for transfers between devices, exchange(): return lax.all_to_all(x, 'rows', split_axis=0, concat_axis=0, tiled=True)  74 us
    pallas_call x1, Pallas kernels, body(): call(with_factors(row_kernel, factor_value, coupling_factor), (blocks, ro...  25.3 us
    all_to_all x3, starting transfers between devices, exchange(): return lax.all_to_all(x, 'rows', split_axis=0, concat_axis=0, tiled=True)  22.3 us
    pallas_call x1, Pallas kernels, body(): call(with_factors(invert_kernel, factor_value), (blocks, shape((count, TR...  16.9 us
    unnamed x42, local copies, waits for them, and re-layouts  13.3 us
    pallas_call x1, Pallas kernels, body(): call(with_factors(middle_kernel, coupling_factor), (rows, shape((total_sl...  7.08 us
  transfers between devices with their start and end apart: 3, of which 2 were waited for; matrix products, arithmetic and copies ran while one was open for 0% of the time, Pallas kernels for 9%

profile of v3, /device:TPU:1, one launch (start us, length us, event | category | flops | bytes accessed | tf_op | source)
XLA Modules:
  0.0 283.2 jit_solution(16468637384720221842)
XLA Ops:
  0.0 0.0 copy-start.17
  0.0 0.7 copy-done.17
  0.7 0.0 copy-start.18
  0.7 0.7 copy-done.18
  1.4 2.7 route.1
  4.1 11.5 %all-to-all-start = ((s32[128,1,1]{2,1,0:T(1,128)}), s32[128,1,1]{2,1,0:T(1,128)S(1)}, u32[]{:S(2)}, u32[]{:S(2)}) async-start(s32[128,1,1]{2,1,0:T(1,128)} %bitcast.3), calls=%async_computation | async-start | bytes 131072 | tf_op jit(solution)/shard_map/all_to_all | solution.py:379
  15.6 0.0 copy-start.8
  15.6 1.0 copy-done.8
  16.6 0.0 copy-start.15
  16.6 0.7 copy-done.15
  17.3 16.9 %invert.1 = (f32[14,128,128]{2,1,0:T(8,128)S(1)}, bf16[14,64,128]{2,1,0:T(8,128)(2,1)S(1)}, bf16[2,14,16,128]{3,2,1,0:T(8,128)(2,1)S(1)}) custom-call(bf16[14,128,128]{2,1,0:T(8,128)(2,1)S(1)} %copy-done.8, bf16[14,128]{1,0:T(8,128)(2,1)S(1)} %copy-done.15), custom_call_target="tpu_custom_call" | custom-call | flops 2000000000 | bytes 100000000 | tf_op jit(solution)/shard_map/invert/pallas_call | solution.py:412
  34.1 0.0 copy-start.19
  34.2 0.9 copy-done.19
  35.1 0.0 all-to-all-done
  35.1 2.9 %serve.1 = bf16[128,144,128]{2,1,0:T(8,128)(2,1)S(1)} custom-call(s32[128,1]{1,0:T(8,128)S(1)} %bitcast.16, bf16[14,64,128]{2,1,0:T(8,128)(2,1)S(1)} %get-tuple-element.23.tri, bf16[2,14,16,128]{3,2,1,0:T(8,128)(2,1)S(1)} %get-tuple-element.24.tail), custom_call_target="tpu_custom_call" | custom-call | tf_op jit(solution)/shard_map/serve/pallas_call | solution.py:426
  38.0 0.0 copy-start
  38.0 0.0 copy-start.9
  38.0 0.0 copy-start.11
  38.0 68.0 %all_to_all.31.refs_5_ = bf16[128,144,128]{2,1,0:T(8,128)(2,1)S(1)} all-to-all(bf16[128,144,128]{2,1,0:T(8,128)(2,1)S(1)} %serve.1), channel_id=1, replica_groups=mesh['rows'=128] {'rows'}, dimensions={0} | all-to-all | bytes 9437184 | tf_op jit(solution)/shard_map/all_to_all | solution.py:379
  106.0 0.0 copy-done
  106.1 0.0 copy-done.9
  106.1 0.0 copy-done.11
  106.1 25.3 %row.1 = (f32[14,128,128]{2,1,0:T(8,128)S(1)}, f32[14,32,128]{2,1,0:T(8,128)S(1)}, bf16[256,32,128]{2,1,0:T(8,128)(2,1)S(1)}) custom-call(s32[42]{0:T(128)S(1)} %get-tuple-element.18.refs_0_, bf16[14,128,128]{2,1,0:T(8,128)(2,1)S(1)} %copy-done.9, bf16[14,128]{1,0:T(8,128)(2,1)S(1)} %copy-done.15, bf16[14,3,128,128]{3,2,1,0:T(8,128)(2,1)S(1)} %copy-done, ...), custom_call_target="tpu_custom_call" | custom-call | tf_op jit(solution)/shard_map/row/pallas_call | solution.py:450
  131.4 0.0 copy-start.5
  131.4 1.3 copy-done.5
  132.8 0.0 copy-start.6
  132.8 1.0 copy-done.6
  133.8 0.0 copy-start.12
  133.8 0.7 copy-done.12
  134.4 5.1 %all-to-all-start.2 = ((bf16[128,64,128]{2,1,0:T(8,128)(2,1)}), bf16[128,64,128]{2,1,0:T(8,128)(2,1)S(1)}, u32[]{:S(2)}, u32[]{:S(2)}) async-start(bf16[128,64,128]{2,1,0:T(8,128)(2,1)} %bitcast.14), calls=%async_computation.2 | async-start | bytes 4194304 | tf_op jit(solution)/shard_map/all_to_all | solution.py:379
  139.5 0.0 copy-start.20
  139.5 1.2 copy-done.20
  140.7 1.0 gram.1.refs_6_
  141.7 0.0 copy-start.2
  141.7 0.9 copy-done.2
  142.6 3.7 %list.1 = (s32[258]{0:T(512)S(1)}, s32[258]{0:T(512)S(1)}, s32[1]{0:T(128)}) custom-call(s32[128,1]{1,0:T(8,128)S(1)} %bitcast.17), custom_call_target="tpu_custom_call" | custom-call | flops 1000000000 | bytes 10000000 | tf_op jit(solution)/shard_map/list/pallas_call | solution.py:434
  146.3 23.7 %all-to-all-done.2 = bf16[128,64,128]{2,1,0:T(8,128)(2,1)S(1)} async-done(((bf16[128,64,128]{2,1,0:T(8,128)(2,1)}), bf16[128,64,128]{2,1,0:T(8,128)(2,1)S(1)}, u32[]{:S(2)}, u32[]{:S(2)}) %all-to-all-start.2) | async-done | bytes 2097184 | tf_op jit(solution)/shard_map/all_to_all | solution.py:379
  170.0 0.0 copy-start.3
  170.0 1.2 copy-done.3
  171.2 0.0 copy-start.13
  171.2 0.9 copy-done.13
  172.2 4.5 %left.1 = bf16[128,4,32,128]{3,2,1,0:T(8,128)(2,1)S(1)} custom-call(s32[42]{0:T(128)S(1)} %get-tuple-element.18.refs_0_, s32[258]{0:T(512)S(1)} %get-tuple-element.20.refs_1_, s32[258]{0:T(512)S(1)} %get-tuple-element.21.refs_2_, s32[1]{0:T(128)} %get-tuple-element.22.refs_3_, bf16[256,32,128]{2,1,0:T(8,128)(2,1)S(1)} %bitcast.13, ...), custom_call_target="tpu_custom_call" | custom-call | tf_op jit(solution)/shard_map/left/pallas_call | solution.py:463
  176.7 0.0 copy-start.1
  176.7 2.0 copy-done.1
  178.7 0.0 copy-start.10
  178.7 0.0 copy-start.14
  178.7 0.0 copy-start.16
  178.7 5.7 %all-to-all-start.3 = ((bf16[128,128,128]{2,1,0:T(8,128)(2,1)}), bf16[128,128,128]{2,1,0:T(8,128)(2,1)}, u32[]{:S(2)}, u32[]{:S(2)}) async-start(bf16[128,128,128]{2,1,0:T(8,128)(2,1)} %bitcast.11), calls=%async_computation.3 | async-start | bytes 8388608 | tf_op jit(solution)/shard_map/all_to_all | solution.py:379
  184.4 0.0 copy-done.10
  184.4 0.0 copy-done.14
  184.4 0.0 copy-done.16
  184.5 0.0 copy-start.4
  184.5 2.6 own.1.refs_5_
  187.1 50.3 %all-to-all-done.3 = bf16[128,128,128]{2,1,0:T(8,128)(2,1)} async-done(((bf16[128,128,128]{2,1,0:T(8,128)(2,1)}), bf16[128,128,128]{2,1,0:T(8,128)(2,1)}, u32[]{:S(2)}, u32[]{:S(2)}) %all-to-all-start.3) | async-done | bytes 4194336 | tf_op jit(solution)/shard_map/all_to_all | solution.py:379
  237.4 0.0 copy-done.4
  237.4 7.1 %middle.1 = (f32[14,32,128]{2,1,0:T(8,128)S(1)}, bf16[256,32,128]{2,1,0:T(8,128)(2,1)S(1)}) custom-call(s32[42]{0:T(128)S(1)} %get-tuple-element.18.refs_0_, s32[258]{0:T(512)S(1)} %get-tuple-element.20.refs_1_, s32[258]{0:T(512)S(1)} %get-tuple-element.21.refs_2_, s32[1]{0:T(128)} %get-tuple-element.22.refs_3_, bf16[128,4,32,128]{3,2,1,0:T(8,128)(2,1)} %bitcast.8.refs_4_, ...), custom_call_target="tpu_custom_call" | custom-call | tf_op jit(solution)/shard_map/middle/pallas_call | solution.py:474
  244.5 0.0 copy-start.7
  244.5 34.3 %all_to_all.32 = bf16[128,64,128]{2,1,0:T(8,128)(2,1)S(1)} all-to-all(bf16[128,64,128]{2,1,0:T(8,128)(2,1)S(1)} %bitcast.15), channel_id=1, replica_groups=mesh['rows'=128] {'rows'}, dimensions={0} | all-to-all | bytes 4194304 | tf_op jit(solution)/shard_map/all_to_all | solution.py:379
  278.8 0.0 copy-done.7
  278.8 4.5 %result.1 = f32[32,1792]{1,0:T(8,128)} custom-call(s32[42]{0:T(128)S(1)} %get-tuple-element.18.refs_0_, bf16[256,32,128]{2,1,0:T(8,128)(2,1)S(1)} %bitcast.12, f32[14,32,128]{2,1,0:T(8,128)S(1)} %get-tuple-element.29.refs_2_, f32[14,128,128]{2,1,0:T(8,128)S(1)} %copy-done.7, bf16[14,3,128,128]{3,2,1,0:T(8,128)(2,1)S(1)} %copy-done), custom_call_target="tpu_custom_call" | custom-call | tf_op jit(solution)/shard_map/result/pallas_call | solution.py:483
Async XLA Ops:
  0.0 0.7 copy-start.17
  0.7 0.7 copy-start.18
  4.1 31.0 %all-to-all-start = ((s32[128,1,1]{2,1,0:T(1,128)}), s32[128,1,1]{2,1,0:T(1,128)S(1)}, u32[]{:S(2)}, u32[]{:S(2)}) async-start(s32[128,1,1]{2,1,0:T(1,128)} %bitcast.3), calls=%async_computation | async-start | bytes 131072 | tf_op jit(solution)/shard_map/all_to_all | solution.py:379
  15.6 1.0 copy-start.8
  16.6 0.7 copy-start.15
  34.1 0.9 copy-start.19
  38.0 68.1 %copy-start = (bf16[14,3,128,128]{3,2,1,0:T(8,128)(2,1)S(1)}, bf16[14,3,128,128]{3,2,1,0:T(8,128)(2,1)}, u32[]{:S(2)}) copy-start(bf16[14,3,128,128]{3,2,1,0:T(8,128)(2,1)} %refs_4_.3) | copy-start | bytes 4128772
  38.0 68.0 %copy-start.9 = (bf16[14,128,128]{2,1,0:T(8,128)(2,1)S(1)}, bf16[14,128,128]{2,1,0:T(8,128)(2,1)}, u32[]{:S(2)}) copy-start(bf16[14,128,128]{2,1,0:T(8,128)(2,1)} %refs_0_.3) | copy-start | bytes 1376260
  38.0 68.0 %copy-start.11 = (f32[32,1792]{1,0:T(8,128)S(1)}, f32[32,1792]{1,0:T(8,128)}, u32[]{:S(2)}) copy-start(f32[32,1792]{1,0:T(8,128)} %refs_4_.2) | copy-start | bytes 688132
  131.4 1.4 copy-start.5
  132.8 1.0 copy-start.6
  133.8 0.7 copy-start.12
  134.4 35.6 %all-to-all-start.2 = ((bf16[128,64,128]{2,1,0:T(8,128)(2,1)}), bf16[128,64,128]{2,1,0:T(8,128)(2,1)S(1)}, u32[]{:S(2)}, u32[]{:S(2)}) async-start(bf16[128,64,128]{2,1,0:T(8,128)(2,1)} %bitcast.14), calls=%async_computation.2 | async-start | bytes 4194304 | tf_op jit(solution)/shard_map/all_to_all | solution.py:379
  139.5 1.2 copy-start.20
  141.7 0.9 copy-start.2
  170.0 1.2 copy-start.3
  171.2 0.9 copy-start.13
  176.7 2.0 copy-start.1
  178.7 5.7 %copy-start.10 = (bf16[14,128,128]{2,1,0:T(8,128)(2,1)S(1)}, bf16[14,128,128]{2,1,0:T(8,128)(2,1)}, u32[]{:S(2)}) copy-start(bf16[14,128,128]{2,1,0:T(8,128)(2,1)} %refs_0_.3) | copy-start | bytes 1376260
  178.7 5.7 %copy-start.14 = (f32[14,32,128]{2,1,0:T(8,128)S(1)}, f32[14,32,128]{2,1,0:T(8,128)}, u32[]{:S(2)}) copy-start(f32[14,32,128]{2,1,0:T(8,128)} %copy-done.12) | copy-start | bytes 688132
  178.7 5.7 %copy-start.16 = (bf16[14,128]{1,0:T(8,128)(2,1)S(1)}, bf16[14,128]{1,0:T(8,128)(2,1)}, u32[]{:S(2)}) copy-start(bf16[14,128]{1,0:T(8,128)(2,1)} %refs_1_.5) | copy-start | bytes 10756
  178.7 58.6 %all-to-all-start.3 = ((bf16[128,128,128]{2,1,0:T(8,128)(2,1)}), bf16[128,128,128]{2,1,0:T(8,128)(2,1)}, u32[]{:S(2)}, u32[]{:S(2)}) async-start(bf16[128,128,128]{2,1,0:T(8,128)(2,1)} %bitcast.11), calls=%async_computation.3 | async-start | bytes 8388608 | tf_op jit(solution)/shard_map/all_to_all | solution.py:379
  184.5 52.9 %copy-start.4 = (f32[14,128,128]{2,1,0:T(8,128)S(1)}, f32[14,128,128]{2,1,0:T(8,128)}, u32[]{:S(2)}) copy-start(f32[14,128,128]{2,1,0:T(8,128)} %copy-done.2) | copy-start | bytes 2752516
  244.5 34.3 %copy-start.7 = (f32[14,128,128]{2,1,0:T(8,128)S(1)}, f32[14,128,128]{2,1,0:T(8,128)}, u32[]{:S(2)}) copy-start(f32[14,128,128]{2,1,0:T(8,128)} %copy-done.6) | copy-start | bytes 2752516

commit v4 on v3

--- a/solution.py
+++ b/solution.py
@@ -14,7 +14,8 @@
 TRI = 64
 TAIL = 16
 CHUNK = 2 * TRI + TAIL
-SEG = 32
+SEG = 16
+STEP = 8
 GROUP = BLK // SEG
 CODE = 16
 VMEM_LIMIT = 16 * 1024 * 1024
@@ -87,36 +88,63 @@
     return out[:, :BLK] + out[:, BLK:]
 
 
-def dot_rows(a, b, turned=False):
+def pair(b, axis):
+    return jnp.concatenate(split(b), axis=axis)
+
+
+def dot_pair(a, b, cb=0):
     n = a.shape[0]
-    both = jnp.concatenate(split(a), axis=0)
-    out = dot(both, jnp.concatenate(split(b), axis=0 if turned else 1), 1, 1 if turned else 0)
+    out = dot(pair(a, 0), b, 1, cb)
     return out[:n, :BLK] + (out[n:, :BLK] + out[:n, BLK:] + out[n:, BLK:])
+
+
+def side_by_side(c, b):
+    return jnp.concatenate([c[b, m] for m in range(3)], axis=1)
 
 
 def eliminate(packs):
     sub, lane = iotas(8)
     start = lane - lane % SEG
     parts = [[p[8 * t : 8 * t + 8] for t in range(SEG // 8)] for p in packs]
-    for k in range(SEG - 1, -1, -1):
-        i, j = divmod(k, 8)
-        index = start + k
-        at_k = lane == index
+    for k in range(SEG - 1, -1, -STEP):
+        i = k // 8
+        spots = [k % 8 - b for b in range(STEP)]
+        index = [start + (k - b) for b in range(STEP)]
+        at = [lane == x for x in index]
         for part in parts:
-            row = jnp.broadcast_to(part[i][j : j + 1], (8, BLK))
-            d = jnp.take_along_axis(row, index, axis=1, mode="promise_in_bounds")
-            rs = lax.rsqrt(d)
-            v = jnp.where(at_k, rs, row * rs)
-            scaled = jnp.where(at_k, 1.0 + rs * rs, v * rs)
-            for t in range(i + 1):
-                if t == i and j == 0:
-                    part[t] = jnp.where(sub == 0, v, part[t])
-                    continue
-                col = jnp.take_along_axis(part[t], index, axis=1, mode="promise_in_bounds")
-                new = part[t] - col * scaled
-                if t == i:
-                    new = jnp.where(sub < j, new, jnp.where(sub == j, v, part[t]))
+            cols = [
+                [jnp.take_along_axis(part[t], x, axis=1, mode="promise_in_bounds") for x in index]
+                for t in range(i + 1)
+            ]
+            pivot = [
+                [jnp.broadcast_to(c[spots[b] : spots[b] + 1], (8, BLK)) for c in cols[i]]
+                for b in range(STEP)
+            ]
+            ratio = [[None] * STEP for _ in range(STEP)]
+            final, scaled = [], []
+            for b in range(STEP):
+                row = jnp.broadcast_to(part[i][spots[b] : spots[b] + 1], (8, BLK))
+                for a in range(b):
+                    row = row - pivot[a][b] * scaled[a]
+                    for c in range(b, STEP):
+                        pivot[b][c] = pivot[b][c] - ratio[a][b] * pivot[a][c]
+                root = lax.rsqrt(pivot[b][b])
+                inverse = root * root
+                for c in range(b + 1, STEP):
+                    ratio[b][c] = inverse * pivot[b][c]
+                final.append(jnp.where(at[b], root, row * root))
+                scaled.append(jnp.where(at[b], 1.0 + inverse, row * inverse))
+            for t in range(i):
+                new = part[t]
+                for b in range(STEP):
+                    col = cols[t][b]
+                    for a in range(b):
+                        col = col - cols[t][a] * ratio[a][b]
+                    cols[t][b] = col
+                    new = new - col * scaled[b]
                 part[t] = new
+            for b in range(STEP):
+                part[i] = jnp.where(sub == spots[b], final[b], part[i])
     return [jnp.concatenate(part, axis=0) for part in parts]
 
 
@@ -249,12 +277,12 @@
 
 def gram_kernel(x, e_out):
     for b in range(x.shape[0]):
-        e_out[b] = dot_exact(x[b], x[b], 0, 0)
+        e_out[b] = pair(dot_exact(x[b], x[b], 0, 0), 1)
 
 
 def row_kernel(
     factor_value, coupling_factor, pos, noise, shift, couplings, vectors, arrived,
-    w_out, y_out, send, z,
+    w_out, y_out, send, z, stage, sems,
 ):
     count = noise.shape[0]
     n_vec = vectors.shape[0]
@@ -291,24 +319,33 @@
     lax.fori_loop(0, count, schur, 0, unroll=2)
     factor(z, count)
     sub, lane = iotas(BLK)
+    copies = []
     for b in range(count):
         w = jnp.where(lane >= sub, z[b], 0.0)
-        w_out[b] = w
-        y = dot_rows(vectors[:, b * BLK : (b + 1) * BLK], w)
+        hi, lo = split(w)
+        w_out[b] = jnp.concatenate([hi, lo], axis=0)
+        y = dot_pair(vectors[:, b * BLK : (b + 1) * BLK], jnp.concatenate([hi, lo], axis=1))
         y_out[b] = y
+        p = (rows_times_bf16(y, side_by_side(couplings, b)) * coupling_factor).astype(BF16)
         for m in range(3):
-            p = rows_times_bf16(y, couplings[b, m]) * coupling_factor
-            send[pos[b * 3 + m]] = p.astype(BF16)
+            q = b * 3 + m
+            stage[q] = p[:, m * BLK : (m + 1) * BLK]
+            copy = pltpu.make_async_copy(stage.at[q], send.at[pos[q]], sems.at[q])
+            copy.start()
+            copies.append(copy)
+    for copy in copies:
+        copy.wait()
 
 
 def own_kernel(factor_value, noise, shift, y, out):
     for b in range(noise.shape[0]):
         d = build_diag(noise, shift, b, factor_value)
-        out[b] = dot_rows(y[b], d)
+        out[b] = dot_pair(y[b], pair(d, 1))
 
 
 def left_kernel(
-    coupling_factor, pos, list_pos, list_slot, list_count, arrived, y, e, couplings, send, left, total
+    coupling_factor, pos, list_pos, list_slot, list_count, arrived, y, e, couplings, send,
+    left, total, stage, sems, give_sems,
 ):
     count = y.shape[0]
     n_vec = y.shape[1]
@@ -320,20 +357,39 @@
         return carry
 
     lax.fori_loop(0, list_count[0], add, 0)
+    copies = []
     for b in range(count):
-        u = dot_rows(total[b], e[b])
+        u = dot_pair(total[b], e[b])
         left[b] = (y[b] - u).astype(BF16)
+        p = (rows_times_bf16(u, side_by_side(couplings, b)) * coupling_factor).astype(BF16)
         for m in range(3):
-            p = rows_times_bf16(u, couplings[b, m]) * coupling_factor
-            at = pos[b * 3 + m]
-            send[at // SLOTS, SLOTS + at % SLOTS] = p.astype(BF16)
+            q = b * 3 + m
+            at = pos[q]
+            stage[q] = p[:, m * BLK : (m + 1) * BLK]
+            copy = pltpu.make_async_copy(
+                stage.at[q], send.at[at // SLOTS, SLOTS + at % SLOTS], sems.at[q]
+            )
+            copy.start()
+            copies.append(copy)
+
+    def gift(t):
+        at = list_pos[t]
+        return pltpu.make_async_copy(
+            left.at[list_slot[t]], send.at[at // SLOTS, at % SLOTS], give_sems.at[t]
+        )
 
     def give(t, carry):
-        at = list_pos[t]
-        send[at // SLOTS, at % SLOTS] = left[list_slot[t]]
+        gift(t).start()
+        return carry
+
+    def finish(t, carry):
+        gift(t).wait()
         return carry
 
     lax.fori_loop(0, list_count[0], give, 0)
+    for copy in copies:
+        copy.wait()
+    lax.fori_loop(0, list_count[0], finish, 0)
 
 
 def middle_kernel(
@@ -351,13 +407,12 @@
 
     lax.fori_loop(0, list_count[0], add, 0)
     for b in range(count):
-        near = jnp.zeros(total.shape[1:], F32)
-        for m in range(3):
-            at = pos[b * 3 + m]
-            near = near + dot(arrived[at // SLOTS, at % SLOTS], couplings[b, m], 1, 1)
+        places = [pos[b * 3 + m] for m in range(3)]
+        near = jnp.concatenate([arrived[at // SLOTS, at % SLOTS] for at in places], axis=1)
+        near = dot(near, side_by_side(couplings, b), 1, 1)
         mid = own[b] - total[b] + near * coupling_factor
         middle[b] = mid
-        answer[b] = dot_rows(mid, e[b]).astype(BF16)
+        answer[b] = dot_pair(mid, e[b]).astype(BF16)
 
     def give(t, carry):
         send[list_pos[t]] = answer[list_slot[t]]
@@ -368,11 +423,10 @@
 
 def result_kernel(coupling_factor, pos, arrived, middle, w, couplings, out):
     for b in range(middle.shape[0]):
-        near = jnp.zeros(middle.shape[1:], F32)
-        for m in range(3):
-            near = near + dot(arrived[pos[b * 3 + m]], couplings[b, m], 1, 1)
+        near = jnp.concatenate([arrived[pos[b * 3 + m]] for m in range(3)], axis=1)
+        near = dot(near, side_by_side(couplings, b), 1, 1)
         mid = middle[b] - near * coupling_factor
-        out[:, b * BLK : (b + 1) * BLK] = dot_rows(mid, w[b], True)
+        out[:, b * BLK : (b + 1) * BLK] = dot_pair(mid, w[b], 1)
 
 
 def exchange(x):
@@ -445,14 +499,18 @@
         name="list",
     )(incoming)
     e = call(
-        gram_kernel, blocks, [VM], VM, flops=10**9, moved=10**7, name="gram"
+        gram_kernel, shape((count, BLK, 2 * BLK), BF16), [VM], VM, flops=10**9, moved=10**7, name="gram"
     )(x)
     w, y, push = call(
         with_factors(row_kernel, factor_value, coupling_factor),
-        (blocks, rows, shape((total_slots, n_vec, BLK), BF16)),
+        (shape((count, 2 * BLK, BLK), BF16), rows, pltpu.HBM((total_slots, n_vec, BLK), BF16)),
         [SM, VM, VM, VM, VM, VM],
-        (VM, VM, VM),
-        [VM((count, BLK, BLK), F32)],
+        (VM, VM, pltpu.HBM),
+        [
+            VM((count, BLK, BLK), F32),
+            VM((3 * count, n_vec, BLK), BF16),
+            pltpu.SemaphoreType.DMA((3 * count,)),
+        ],
         name="row",
     )(pos, diag_noise, shifts, couplings, vectors, arrived)
     pushed = exchange(push.reshape(n_dev, SLOTS * n_vec, BLK)).reshape(total_slots, n_vec, BLK)
@@ -462,10 +520,16 @@
     )(diag_noise, shifts, y)
     both = call(
         with_factors(left_kernel, coupling_factor),
-        shape((n_dev, 2 * SLOTS, n_vec, BLK), BF16),
+        pltpu.HBM((n_dev, 2 * SLOTS, n_vec, BLK), BF16),
         [SM] * 4 + [VM] * 4,
-        VM,
-        [VM((count, n_vec, BLK), BF16), VM((count, n_vec, BLK), F32)],
+        pltpu.HBM,
+        [
+            VM((count, n_vec, BLK), BF16),
+            VM((count, n_vec, BLK), F32),
+            VM((3 * count, n_vec, BLK), BF16),
+            pltpu.SemaphoreType.DMA((3 * count,)),
+            pltpu.SemaphoreType.DMA((total_slots,)),
+        ],
         name="left",
     )(pos, *lists, pushed, y, e, couplings)
     both = exchange(both.reshape(n_dev, 2 * SLOTS * n_vec, BLK)).reshape(

time: 284 us -> 265 us (0.933)
  Pallas kernels: 71.1 us -> 55.4 us
  local copies, waits for them, and re-layouts: 13.3 us -> 9.93 us
    pallas_call x1, Pallas kernels: 16.9 us -> 8.63 us  [body(): call(with_factors(invert_kernel, factor_value), (blocks, shape((count, TR...]
    pallas_call x3, Pallas kernels: 30.9 us -> 25.4 us  [the longest x1 16.9 us: body(): call(with_factors(row_kernel, factor_value, coupling_factor), (shape((cou...]
    unnamed x42 -> x38, local copies, waits for them, and re-layouts: 13.3 us -> 9.93 us
  transfers between devices with their start and end apart: 3 -> 3, of which waited for: 2 -> 2; matrix products, arithmetic and copies ran while one was open for 0% -> 0% of each run, Pallas kernels for 9% -> 6%
where the time goes in v4:
time: 265 us; the launch traced here: 264 us
  blocking collectives  103 us (39%)
  waiting for transfers between devices  74 us (28%)
  Pallas kernels  55.4 us (21%)
  starting transfers between devices  22.3 us (8%)
  local copies, waits for them, and re-layouts  9.93 us (4%)
    all_to_all x2, blocking collectives, exchange(): return lax.all_to_all(x, 'rows', split_axis=0, concat_axis=0, tiled=True)  103 us
    all_to_all x3, waiting for transfers between devices, exchange(): return lax.all_to_all(x, 'rows', split_axis=0, concat_axis=0, tiled=True)  74 us
    all_to_all x3, starting transfers between devices, exchange(): return lax.all_to_all(x, 'rows', split_axis=0, concat_axis=0, tiled=True)  22.3 us
    pallas_call x1, Pallas kernels, body(): call(with_factors(row_kernel, factor_value, coupling_factor), (shape((cou...  16.9 us
    unnamed x38, local copies, waits for them, and re-layouts  9.93 us
    pallas_call x1, Pallas kernels, body(): call(with_factors(invert_kernel, factor_value), (blocks, shape((count, TR...  8.63 us
    pallas_call x1, Pallas kernels, body(): call(with_factors(left_kernel, coupling_factor), pltpu.HBM((n_dev, 2 * SL...  7.55 us
    pallas_call x1, Pallas kernels, body(): call(with_factors(middle_kernel, coupling_factor), (rows, shape((total_sl...  5.9 us
  transfers between devices with their start and end apart: 3, of which 2 were waited for; matrix products, arithmetic and copies ran while one was open for 0% of the time, Pallas kernels for 6%

profile of v4, /device:TPU:1, one launch (start us, length us, event | category | flops | bytes accessed | tf_op | source)
XLA Modules:
  0.0 264.5 jit_solution(10528695865216188084)
XLA Ops:
  0.0 0.0 copy-start.15
  0.0 0.7 copy-done.15
  0.7 0.0 copy-start.16
  0.7 0.7 copy-done.16
  1.4 2.7 %route.1 = (s32[128,1]{1,0:T(8,128)}, s32[42]{0:T(128)S(1)}) custom-call(s32[1]{0:T(128)} %bitcast.me_ref, s32[3,14]{1,0:T(4,128)S(1)} %bitcast.16, s32[3,14]{1,0:T(4,128)S(1)} %bitcast.17), custom_call_target="tpu_custom_call" | custom-call | tf_op jit(solution)/shard_map/route/pallas_call | solution.py:457
  4.1 11.5 %all-to-all-start = ((s32[128,1,1]{2,1,0:T(1,128)}), s32[128,1,1]{2,1,0:T(1,128)S(1)}, u32[]{:S(2)}, u32[]{:S(2)}) async-start(s32[128,1,1]{2,1,0:T(1,128)} %bitcast.3), calls=%async_computation | async-start | bytes 131072 | tf_op jit(solution)/shard_map/all_to_all | solution.py:433
  15.6 0.0 copy-start.6
  15.6 1.0 copy-done.6
  16.6 0.0 copy-start.13
  16.6 0.7 copy-done.13
  17.3 8.6 %invert.1 = (f32[14,128,128]{2,1,0:T(8,128)S(1)}, bf16[14,64,128]{2,1,0:T(8,128)(2,1)S(1)}, bf16[2,14,16,128]{3,2,1,0:T(8,128)(2,1)S(1)}) custom-call(bf16[14,128,128]{2,1,0:T(8,128)(2,1)S(1)} %copy-done.6, bf16[14,128]{1,0:T(8,128)(2,1)S(1)} %copy-done.13), custom_call_target="tpu_custom_call" | custom-call | flops 2000000000 | bytes 100000000 | tf_op jit(solution)/shard_map/invert/pallas_call | solution.py:466
  25.9 0.0 copy-start.17
  25.9 0.9 copy-done.17
  26.9 0.0 all-to-all-done
  26.9 2.9 %serve.1 = bf16[128,144,128]{2,1,0:T(8,128)(2,1)S(1)} custom-call(s32[128,1]{1,0:T(8,128)S(1)} %bitcast.14, bf16[14,64,128]{2,1,0:T(8,128)(2,1)S(1)} %get-tuple-element.23.tri, bf16[2,14,16,128]{3,2,1,0:T(8,128)(2,1)S(1)} %get-tuple-element.24.tail), custom_call_target="tpu_custom_call" | custom-call | tf_op jit(solution)/shard_map/serve/pallas_call | solution.py:480
  29.8 0.0 copy-start
  29.8 0.0 copy-start.7
  29.8 0.0 copy-start.9
  29.8 0.0 copy-start.14
  29.8 68.0 %all_to_all.31.refs_5_ = bf16[128,144,128]{2,1,0:T(8,128)(2,1)S(1)} all-to-all(bf16[128,144,128]{2,1,0:T(8,128)(2,1)S(1)} %serve.1), channel_id=1, replica_groups=mesh['rows'=128] {'rows'}, dimensions={0} | all-to-all | bytes 9437184 | tf_op jit(solution)/shard_map/all_to_all | solution.py:433
  97.8 0.0 copy-done
  97.8 0.0 copy-done.7
  97.8 0.0 copy-done.9
  97.8 0.0 copy-done.14
  97.8 16.9 %row.1 = (bf16[14,256,128]{2,1,0:T(8,128)(2,1)S(1)}, f32[14,32,128]{2,1,0:T(8,128)S(1)}, bf16[256,32,128]{2,1,0:T(8,128)(2,1)}) custom-call(s32[42]{0:T(128)S(1)} %get-tuple-element.18.refs_0_, bf16[14,128,128]{2,1,0:T(8,128)(2,1)S(1)} %copy-done.7, bf16[14,128]{1,0:T(8,128)(2,1)S(1)} %copy-done.14, bf16[14,3,128,128]{3,2,1,0:T(8,128)(2,1)S(1)} %copy-done, ...), custom_call_target="tpu_custom_call" | custom-call | tf_op jit(solution)/shard_map/row/pallas_call | solution.py:504
  114.7 0.0 copy-start.4
  114.7 1.0 copy-done.4
  115.7 0.0 copy-start.10
  115.7 0.7 copy-done.10
  116.4 5.1 %all-to-all-start.2 = ((bf16[128,64,128]{2,1,0:T(8,128)(2,1)}), bf16[128,64,128]{2,1,0:T(8,128)(2,1)S(1)}, u32[]{:S(2)}, u32[]{:S(2)}) async-start(bf16[128,64,128]{2,1,0:T(8,128)(2,1)} %bitcast.19), calls=%async_computation.2 | async-start | bytes 4194304 | tf_op jit(solution)/shard_map/all_to_all | solution.py:433
  121.5 0.0 copy-start.18
  121.5 1.2 copy-done.18
  122.7 1.0 gram.1.refs_6_
  123.7 0.0 copy-start.1
  123.7 0.9 copy-done.1
  124.6 3.7 %list.1 = (s32[258]{0:T(512)S(1)}, s32[258]{0:T(512)S(1)}, s32[1]{0:T(128)}) custom-call(s32[128,1]{1,0:T(8,128)S(1)} %bitcast.15), custom_call_target="tpu_custom_call" | custom-call | flops 1000000000 | bytes 10000000 | tf_op jit(solution)/shard_map/list/pallas_call | solution.py:488
  128.3 23.7 %all-to-all-done.2 = bf16[128,64,128]{2,1,0:T(8,128)(2,1)S(1)} async-done(((bf16[128,64,128]{2,1,0:T(8,128)(2,1)}), bf16[128,64,128]{2,1,0:T(8,128)(2,1)S(1)}, u32[]{:S(2)}, u32[]{:S(2)}) %all-to-all-start.2) | async-done | bytes 2097184 | tf_op jit(solution)/shard_map/all_to_all | solution.py:433
  152.0 0.0 copy-start.2
  152.0 1.2 copy-done.2
  153.2 0.0 copy-start.11
  153.2 0.9 copy-done.11
  154.1 7.5 %left.1 = bf16[128,4,32,128]{3,2,1,0:T(8,128)(2,1)} custom-call(s32[42]{0:T(128)S(1)} %get-tuple-element.18.refs_0_, s32[258]{0:T(512)S(1)} %get-tuple-element.20.refs_1_, s32[258]{0:T(512)S(1)} %get-tuple-element.21.refs_2_, s32[1]{0:T(128)} %get-tuple-element.22.refs_3_, bf16[256,32,128]{2,1,0:T(8,128)(2,1)S(1)} %bitcast.12, ...), custom_call_target="tpu_custom_call" | custom-call | tf_op jit(solution)/shard_map/left/pallas_call | solution.py:521
  161.7 0.0 copy-start.8
  161.7 0.0 copy-start.12
  161.7 5.8 %all-to-all-start.3 = ((bf16[128,128,128]{2,1,0:T(8,128)(2,1)}), bf16[128,128,128]{2,1,0:T(8,128)(2,1)}, u32[]{:S(2)}, u32[]{:S(2)}) async-start(bf16[128,128,128]{2,1,0:T(8,128)(2,1)} %bitcast.18), calls=%async_computation.3 | async-start | bytes 8388608 | tf_op jit(solution)/shard_map/all_to_all | solution.py:433
  167.5 0.0 copy-done.8
  167.5 0.0 copy-done.12
  167.5 0.0 copy-start.3
  167.5 2.6 own.1.refs_5_
  170.1 50.3 %all-to-all-done.3 = bf16[128,128,128]{2,1,0:T(8,128)(2,1)} async-done(((bf16[128,128,128]{2,1,0:T(8,128)(2,1)}), bf16[128,128,128]{2,1,0:T(8,128)(2,1)}, u32[]{:S(2)}, u32[]{:S(2)}) %all-to-all-start.3) | async-done | bytes 4194336 | tf_op jit(solution)/shard_map/all_to_all | solution.py:433
  220.4 0.0 copy-done.3
  220.4 5.9 %middle.1 = (f32[14,32,128]{2,1,0:T(8,128)S(1)}, bf16[256,32,128]{2,1,0:T(8,128)(2,1)S(1)}) custom-call(s32[42]{0:T(128)S(1)} %get-tuple-element.18.refs_0_, s32[258]{0:T(512)S(1)} %get-tuple-element.20.refs_1_, s32[258]{0:T(512)S(1)} %get-tuple-element.21.refs_2_, s32[1]{0:T(128)} %get-tuple-element.22.refs_3_, bf16[128,4,32,128]{3,2,1,0:T(8,128)(2,1)} %bitcast.8.refs_4_, ...), custom_call_target="tpu_custom_call" | custom-call | tf_op jit(solution)/shard_map/middle/pallas_call | solution.py:538
  226.4 0.0 copy-start.5
  226.4 34.6 %all_to_all.32 = bf16[128,64,128]{2,1,0:T(8,128)(2,1)S(1)} all-to-all(bf16[128,64,128]{2,1,0:T(8,128)(2,1)S(1)} %bitcast.13), channel_id=1, replica_groups=mesh['rows'=128] {'rows'}, dimensions={0} | all-to-all | bytes 4194304 | tf_op jit(solution)/shard_map/all_to_all | solution.py:433
  260.9 0.0 copy-done.5
  261.0 3.5 %result.1 = f32[32,1792]{1,0:T(8,128)} custom-call(s32[42]{0:T(128)S(1)} %get-tuple-element.18.refs_0_, bf16[256,32,128]{2,1,0:T(8,128)(2,1)S(1)} %bitcast.11, f32[14,32,128]{2,1,0:T(8,128)S(1)} %get-tuple-element.29.refs_2_, bf16[14,256,128]{2,1,0:T(8,128)(2,1)S(1)} %copy-done.5, bf16[14,3,128,128]{3,2,1,0:T(8,128)(2,1)S(1)} %copy-done), custom_call_target="tpu_custom_call" | custom-call | tf_op jit(solution)/shard_map/result/pallas_call | solution.py:547
Async XLA Ops:
  0.0 0.7 copy-start.15
  0.7 0.7 copy-start.16
  4.1 22.8 %all-to-all-start = ((s32[128,1,1]{2,1,0:T(1,128)}), s32[128,1,1]{2,1,0:T(1,128)S(1)}, u32[]{:S(2)}, u32[]{:S(2)}) async-start(s32[128,1,1]{2,1,0:T(1,128)} %bitcast.3), calls=%async_computation | async-start | bytes 131072 | tf_op jit(solution)/shard_map/all_to_all | solution.py:433
  15.6 1.0 copy-start.6
  16.6 0.7 copy-start.13
  25.9 0.9 copy-start.17
  29.8 68.1 %copy-start = (bf16[14,3,128,128]{3,2,1,0:T(8,128)(2,1)S(1)}, bf16[14,3,128,128]{3,2,1,0:T(8,128)(2,1)}, u32[]{:S(2)}) copy-start(bf16[14,3,128,128]{3,2,1,0:T(8,128)(2,1)} %refs_4_.3) | copy-start | bytes 4128772
  29.8 68.1 %copy-start.7 = (bf16[14,128,128]{2,1,0:T(8,128)(2,1)S(1)}, bf16[14,128,128]{2,1,0:T(8,128)(2,1)}, u32[]{:S(2)}) copy-start(bf16[14,128,128]{2,1,0:T(8,128)(2,1)} %refs_0_.3) | copy-start | bytes 1376260
  29.8 68.0 %copy-start.9 = (f32[32,1792]{1,0:T(8,128)S(1)}, f32[32,1792]{1,0:T(8,128)}, u32[]{:S(2)}) copy-start(f32[32,1792]{1,0:T(8,128)} %refs_4_.2) | copy-start | bytes 688132
  29.8 68.0 %copy-start.14 = (bf16[14,128]{1,0:T(8,128)(2,1)S(1)}, bf16[14,128]{1,0:T(8,128)(2,1)}, u32[]{:S(2)}) copy-start(bf16[14,128]{1,0:T(8,128)(2,1)} %refs_1_.5) | copy-start | bytes 10756
  114.7 1.0 copy-start.4
  115.7 0.7 copy-start.10
  116.4 35.6 %all-to-all-start.2 = ((bf16[128,64,128]{2,1,0:T(8,128)(2,1)}), bf16[128,64,128]{2,1,0:T(8,128)(2,1)S(1)}, u32[]{:S(2)}, u32[]{:S(2)}) async-start(bf16[128,64,128]{2,1,0:T(8,128)(2,1)} %bitcast.19), calls=%async_computation.2 | async-start | bytes 4194304 | tf_op jit(solution)/shard_map/all_to_all | solution.py:433
  121.5 1.2 copy-start.18
  123.7 0.9 copy-start.1
  152.0 1.2 copy-start.2
  153.2 0.9 copy-start.11
  161.7 5.8 %copy-start.8 = (bf16[14,128,128]{2,1,0:T(8,128)(2,1)S(1)}, bf16[14,128,128]{2,1,0:T(8,128)(2,1)}, u32[]{:S(2)}) copy-start(bf16[14,128,128]{2,1,0:T(8,128)(2,1)} %refs_0_.3) | copy-start | bytes 1376260
  161.7 5.8 %copy-start.12 = (f32[14,32,128]{2,1,0:T(8,128)S(1)}, f32[14,32,128]{2,1,0:T(8,128)}, u32[]{:S(2)}) copy-start(f32[14,32,128]{2,1,0:T(8,128)} %copy-done.10) | copy-start | bytes 688132
  161.7 58.7 %all-to-all-start.3 = ((bf16[128,128,128]{2,1,0:T(8,128)(2,1)}), bf16[128,128,128]{2,1,0:T(8,128)(2,1)}, u32[]{:S(2)}, u32[]{:S(2)}) async-start(bf16[128,128,128]{2,1,0:T(8,128)(2,1)} %bitcast.18), calls=%async_computation.3 | async-start | bytes 8388608 | tf_op jit(solution)/shard_map/all_to_all | solution.py:433
  167.5 52.9 %copy-start.3 = (bf16[14,128,256]{2,1,0:T(8,128)(2,1)S(1)}, bf16[14,128,256]{2,1,0:T(8,128)(2,1)}, u32[]{:S(2)}) copy-start(bf16[14,128,256]{2,1,0:T(8,128)(2,1)} %copy-done.1) | copy-start | bytes 2752516
  226.4 34.6 %copy-start.5 = (bf16[14,256,128]{2,1,0:T(8,128)(2,1)S(1)}, bf16[14,256,128]{2,1,0:T(8,128)(2,1)}, u32[]{:S(2)}) copy-start(bf16[14,256,128]{2,1,0:T(8,128)(2,1)} %copy-done.4) | copy-start | bytes 2752516

commit v5 on v4

--- a/solution.py
+++ b/solution.py
@@ -1,3 +1,4 @@
+import functools
 import math
 
 import jax
@@ -209,10 +210,11 @@
 
     def clear(t, carry):
         count_ref[t] = 0
-        ask_ref[t, 0] = 0
-        return carry
-
-    lax.fori_loop(0, n_dev, clear, 0, unroll=16)
+        return carry
+
+    lax.fori_loop(0, n_dev, clear, 0, unroll=32)
+    _, lane = iotas(8, n_dev)
+    codes = jnp.zeros((8, n_dev), jnp.int32)
     for i in range(dev_ref.shape[1]):
         for m in range(3):
             t = me - 1 - dev_ref[m, i]
@@ -220,21 +222,11 @@
             rank = count_ref[t]
             count_ref[t] = rank + 1
             code = slot_ref[m, i] + 1
-            ask_ref[t, 0] = ask_ref[t, 0] + jnp.where(rank == 0, code, code * CODE)
+            code = jnp.where(rank == 0, code, code * CODE)
+            codes = codes + jnp.where(lane == t, code, 0)
             pos_ref[i * 3 + m] = t * SLOTS + rank
-
-
-def list_kernel(incoming, list_pos, list_slot, list_count):
-    def one(t, n):
-        code = incoming[t, 0]
-        for r in range(SLOTS):
-            slot = (code % CODE if r == 0 else code // CODE) - 1
-            list_pos[n] = t * SLOTS + r
-            list_slot[n] = slot
-            n = n + (slot >= 0).astype(jnp.int32)
-        return n
-
-    list_count[0] = lax.fori_loop(0, incoming.shape[0], one, 0, unroll=8)
+    for t in range(n_dev // 8):
+        ask_ref[8 * t : 8 * t + 8, :] = codes
 
 
 def invert_kernel(factor_value, noise, shift, x_out, tri_out, tail_out, z):
@@ -263,9 +255,11 @@
             tail_out[r, b] = tail.astype(BF16)
 
 
-def serve_kernel(incoming, tri, tail, out):
+def serve_kernel(me_ref, incoming, tri, tail, out):
+    me = me_ref[0]
+
     def one(t, carry):
-        code = incoming[t, 0]
+        code = incoming[t, me]
         slots = [jnp.maximum(code % CODE - 1, 0), jnp.maximum(code // CODE - 1, 0)]
         for r in range(SLOTS):
             out[t, r * TRI : (r + 1) * TRI] = tri[slots[r]]
@@ -273,11 +267,6 @@
         return carry
 
     lax.fori_loop(0, out.shape[0], one, 0, unroll=8)
-
-
-def gram_kernel(x, e_out):
-    for b in range(x.shape[0]):
-        e_out[b] = pair(dot_exact(x[b], x[b], 0, 0), 1)
 
 
 def row_kernel(
@@ -337,18 +326,38 @@
         copy.wait()
 
 
-def own_kernel(factor_value, noise, shift, y, out):
+def between_kernel(
+    factor_value, me_ref, incoming, table, x, noise, shift, y,
+    e_out, own_out, list_pos, list_slot, list_count, clash,
+):
+    me = me_ref[0]
+
+    def one(t, n):
+        code = incoming[t, me]
+        for r in range(SLOTS):
+            slot = (code % CODE if r == 0 else code // CODE) - 1
+            list_pos[n] = t * SLOTS + r
+            list_slot[n] = slot
+            n = n + (slot >= 0).astype(jnp.int32)
+        return n
+
+    list_count[0] = lax.fori_loop(0, incoming.shape[0], one, 0, unroll=8)
+    double = (table[...] >= CODE).astype(F32)
+    clash[0] = (jnp.max(double * double.T) > 0.5).astype(jnp.int32)
     for b in range(noise.shape[0]):
+        e_out[b] = pair(dot_exact(x[b], x[b], 0, 0), 1)
         d = build_diag(noise, shift, b, factor_value)
-        out[b] = dot_pair(y[b], pair(d, 1))
+        own_out[b] = dot_pair(y[b], pair(d, 1))
+
+
+def push_slot(slots, rank):
+    return SLOTS + rank if slots == 2 * SLOTS else SLOTS - rank
 
 
 def left_kernel(
-    coupling_factor, pos, list_pos, list_slot, list_count, arrived, y, e, couplings, send,
-    left, total, stage, sems, give_sems,
+    coupling_factor, pos, list_pos, list_slot, list_count, arrived, y, e, couplings, send, left, total
 ):
     count = y.shape[0]
-    n_vec = y.shape[1]
     total[...] = jnp.zeros_like(total)
 
     def add(t, carry):
@@ -357,39 +366,20 @@
         return carry
 
     lax.fori_loop(0, list_count[0], add, 0)
-    copies = []
     for b in range(count):
         u = dot_pair(total[b], e[b])
         left[b] = (y[b] - u).astype(BF16)
         p = (rows_times_bf16(u, side_by_side(couplings, b)) * coupling_factor).astype(BF16)
         for m in range(3):
-            q = b * 3 + m
-            at = pos[q]
-            stage[q] = p[:, m * BLK : (m + 1) * BLK]
-            copy = pltpu.make_async_copy(
-                stage.at[q], send.at[at // SLOTS, SLOTS + at % SLOTS], sems.at[q]
-            )
-            copy.start()
-            copies.append(copy)
-
-    def gift(t):
+            at = pos[b * 3 + m]
+            send[at // SLOTS, push_slot(send.shape[1], at % SLOTS)] = p[:, m * BLK : (m + 1) * BLK]
+
+    def give(t, carry):
         at = list_pos[t]
-        return pltpu.make_async_copy(
-            left.at[list_slot[t]], send.at[at // SLOTS, at % SLOTS], give_sems.at[t]
-        )
-
-    def give(t, carry):
-        gift(t).start()
-        return carry
-
-    def finish(t, carry):
-        gift(t).wait()
+        send[at // SLOTS, at % SLOTS] = left[list_slot[t]]
         return carry
 
     lax.fori_loop(0, list_count[0], give, 0)
-    for copy in copies:
-        copy.wait()
-    lax.fori_loop(0, list_count[0], finish, 0)
 
 
 def middle_kernel(
@@ -402,7 +392,8 @@
     def add(t, carry):
         slot = list_slot[t]
         at = list_pos[t]
-        total[slot] += arrived[at // SLOTS, SLOTS + at % SLOTS].astype(F32)
+        place = push_slot(arrived.shape[1], at % SLOTS)
+        total[slot] += arrived[at // SLOTS, place].astype(F32)
         return carry
 
     lax.fori_loop(0, list_count[0], add, 0)
@@ -456,13 +447,13 @@
 
     ask, pos = call(
         route_kernel,
-        (shape((n_dev, 1), jnp.int32), shape((3 * count,), jnp.int32)),
+        (shape((n_dev, n_dev), jnp.int32), shape((3 * count,), jnp.int32)),
         [SM, SM, SM],
-        (SM, SM),
+        (VM, SM),
         [SM((n_dev,), jnp.int32)],
         name="route",
     )(me, near_devices.T, near_slots.T)
-    incoming = exchange(ask)
+    table = exchange(ask)
     x, tri, tail = call(
         with_factors(invert_kernel, factor_value),
         (
@@ -480,27 +471,11 @@
     answer = call(
         serve_kernel,
         shape((n_dev, CHUNK, BLK), BF16),
-        [SM, VM, VM],
+        [SM, SM, VM, VM],
         VM,
         name="serve",
-    )(incoming, tri, tail)
+    )(me, table, tri, tail)
     arrived = exchange(answer)
-    lists = call(
-        list_kernel,
-        (
-            shape((total_slots + SLOTS,), jnp.int32),
-            shape((total_slots + SLOTS,), jnp.int32),
-            shape((1,), jnp.int32),
-        ),
-        [SM],
-        (SM, SM, SM),
-        flops=10**9,
-        moved=10**7,
-        name="list",
-    )(incoming)
-    e = call(
-        gram_kernel, shape((count, BLK, 2 * BLK), BF16), [VM], VM, flops=10**9, moved=10**7, name="gram"
-    )(x)
     w, y, push = call(
         with_factors(row_kernel, factor_value, coupling_factor),
         (shape((count, 2 * BLK, BLK), BF16), rows, pltpu.HBM((total_slots, n_vec, BLK), BF16)),
@@ -514,35 +489,50 @@
         name="row",
     )(pos, diag_noise, shifts, couplings, vectors, arrived)
     pushed = exchange(push.reshape(n_dev, SLOTS * n_vec, BLK)).reshape(total_slots, n_vec, BLK)
-    own = call(
-        with_factors(own_kernel, factor_value),
-        rows, [VM, VM, VM], VM, flops=10**9, moved=10**7, name="own",
-    )(diag_noise, shifts, y)
-    both = call(
-        with_factors(left_kernel, coupling_factor),
-        pltpu.HBM((n_dev, 2 * SLOTS, n_vec, BLK), BF16),
-        [SM] * 4 + [VM] * 4,
-        pltpu.HBM,
-        [
-            VM((count, n_vec, BLK), BF16),
-            VM((count, n_vec, BLK), F32),
-            VM((3 * count, n_vec, BLK), BF16),
-            pltpu.SemaphoreType.DMA((3 * count,)),
-            pltpu.SemaphoreType.DMA((total_slots,)),
-        ],
-        name="left",
-    )(pos, *lists, pushed, y, e, couplings)
-    both = exchange(both.reshape(n_dev, 2 * SLOTS * n_vec, BLK)).reshape(
-        n_dev, 2 * SLOTS, n_vec, BLK
+    e, own, *lists, clash = call(
+        with_factors(between_kernel, factor_value),
+        (
+            shape((count, BLK, 2 * BLK), BF16),
+            rows,
+            shape((total_slots + SLOTS,), jnp.int32),
+            shape((total_slots + SLOTS,), jnp.int32),
+            shape((1,), jnp.int32),
+            shape((1,), jnp.int32),
+        ),
+        [SM, SM] + [VM] * 5,
+        (VM, VM, SM, SM, SM, SM),
+        flops=2 * 10**9,
+        moved=10**7,
+        name="between",
+    )(me, table, table, x, diag_noise, shifts, y)
+
+    def swap(slots, pos, lists, pushed, y, e, own, couplings):
+        both = call(
+            with_factors(left_kernel, coupling_factor),
+            shape((n_dev, slots, n_vec, BLK), BF16),
+            [SM] * 4 + [VM] * 4,
+            VM,
+            [VM((count, n_vec, BLK), BF16), VM((count, n_vec, BLK), F32)],
+            name="left",
+        )(pos, *lists, pushed, y, e, couplings)
+        both = exchange(both.reshape(n_dev, slots * n_vec, BLK)).reshape(
+            n_dev, slots, n_vec, BLK
+        )
+        return call(
+            with_factors(middle_kernel, coupling_factor),
+            (rows, shape((total_slots, n_vec, BLK), BF16)),
+            [SM] * 4 + [VM] * 4,
+            (VM, VM),
+            [VM((count, n_vec, BLK), F32), VM((count, n_vec, BLK), BF16)],
+            name="middle",
+        )(pos, *lists, both, own, e, couplings)
+
+    middle, back = lax.cond(
+        clash[0] > 0,
+        functools.partial(swap, 2 * SLOTS),
+        functools.partial(swap, 2 * SLOTS - 1),
+        pos, lists, pushed, y, e, own, couplings,
     )
-    middle, back = call(
-        with_factors(middle_kernel, coupling_factor),
-        (rows, shape((total_slots, n_vec, BLK), BF16)),
-        [SM] * 4 + [VM] * 4,
-        (VM, VM),
-        [VM((count, n_vec, BLK), F32), VM((count, n_vec, BLK), BF16)],
-        name="middle",
-    )(pos, *lists, both, own, e, couplings)
     back = exchange(back.reshape(n_dev, SLOTS * n_vec, BLK)).reshape(total_slots, n_vec, BLK)
     return call(
         with_factors(result_kernel, coupling_factor),

time: 265 us -> 246 us (0.928)
  waiting for transfers between devices: 74 us -> 23.7 us
  blocking collectives: 103 us -> 149 us
  local copies, waits for them, and re-layouts: 9.93 us -> 3.11 us
  starting transfers between devices: 22.3 us -> 17.1 us
  Pallas kernels: 55.4 us -> 51.9 us
    all_to_all x3 -> x2, waiting for transfers between devices: 74 us -> 23.7 us  [exchange(): return lax.all_to_all(x, 'rows', split_axis=0, concat_axis=0, tiled=True)]
    all_to_all x2 -> x3, blocking collectives: 103 us -> 149 us  [exchange(): return lax.all_to_all(x, 'rows', split_axis=0, concat_axis=0, tiled=True)]
    unnamed x38 -> x18, local copies, waits for them, and re-layouts: 9.93 us -> 3.09 us
    all_to_all x3 -> x2, starting transfers between devices: 22.3 us -> 17.1 us  [exchange(): return lax.all_to_all(x, 'rows', split_axis=0, concat_axis=0, tiled=True)]
    pallas_call x7 -> x5, Pallas kernels: 26.3 us -> 22.2 us  [the longest x1 5.96 us: swap(): call(with_factors(left_kernel, coupling_factor), shape((n_dev, slots, n_v...]
  transfers between devices with their start and end apart: 3 -> 2, of which waited for: 2 -> 1; matrix products, arithmetic and copies ran while one was open for 0% -> 0% of each run, Pallas kernels for 6% -> 6%
where the time goes in v5:
time: 246 us
  blocking collectives  149 us (61%)
  Pallas kernels  51.9 us (21%)
  waiting for transfers between devices  23.7 us (10%)
  starting transfers between devices  17.1 us (7%)
  local copies, waits for them, and re-layouts  3.11 us (1%)
    all_to_all x3, blocking collectives, exchange(): return lax.all_to_all(x, 'rows', split_axis=0, concat_axis=0, tiled=True)  149 us
    all_to_all x2, waiting for transfers between devices, exchange(): return lax.all_to_all(x, 'rows', split_axis=0, concat_axis=0, tiled=True)  23.7 us
    pallas_call x1, Pallas kernels, body(): call(with_factors(row_kernel, factor_value, coupling_factor), (shape((cou...  17.5 us
    all_to_all x2, starting transfers between devices, exchange(): return lax.all_to_all(x, 'rows', split_axis=0, concat_axis=0, tiled=True)  17.1 us
    pallas_call x1, Pallas kernels, body(): call(with_factors(invert_kernel, factor_value), (blocks, shape((count, TR...  8.62 us
    pallas_call x1, Pallas kernels, swap(): call(with_factors(left_kernel, coupling_factor), shape((n_dev, slots, n_v...  5.96 us
    pallas_call x1, Pallas kernels, body(): call(with_factors(between_kernel, factor_value), (shape((count, BLK, 2 *...  5.92 us
    pallas_call x1, Pallas kernels, swap(): call(with_factors(middle_kernel, coupling_factor), (rows, shape((total_sl...  5.76 us
  transfers between devices with their start and end apart: 2, of which 1 were waited for; matrix products, arithmetic and copies ran while one was open for 0% of the time, Pallas kernels for 6%

profile of v5, /device:TPU:1, one launch (start us, length us, event | category | flops | bytes accessed | tf_op | source)
XLA Modules:
  0.0 246.0 jit_solution(572449808678999398)
XLA Ops:
  0.0 0.0 copy-start.5
  0.0 0.7 copy-done.5
  0.7 0.0 copy-start.6
  0.7 0.7 copy-done.6
  1.4 1.5 route.1
  2.9 11.5 %all-to-all-start.2 = ((s32[128,1,128]{2,1,0:T(1,128)}), s32[128,1,128]{2,1,0:T(1,128)S(1)}, u32[]{:S(2)}, u32[]{:S(2)}) async-start(s32[128,1,128]{2,1,0:T(1,128)} %bitcast.8), calls=%async_computation.2 | async-start | bytes 131072 | tf_op jit(solution)/shard_map/all_to_all | solution.py:424
  14.4 0.0 copy-start
  14.4 1.0 copy-done
  15.4 0.0 copy-start.3
  15.4 0.7 copy-done.3
  16.1 8.6 %invert.1 = (f32[14,128,128]{2,1,0:T(8,128)S(1)}, bf16[14,64,128]{2,1,0:T(8,128)(2,1)S(1)}, bf16[2,14,16,128]{3,2,1,0:T(8,128)(2,1)S(1)}) custom-call(bf16[14,128,128]{2,1,0:T(8,128)(2,1)S(1)} %copy-done, bf16[14,128]{1,0:T(8,128)(2,1)S(1)} %copy-done.3), custom_call_target="tpu_custom_call" | custom-call | flops 2000000000 | bytes 100000000 | tf_op jit(solution)/shard_map/invert/pallas_call | solution.py:457
  24.7 0.0 all-to-all-done.2
  24.8 3.0 %serve.1 = bf16[128,144,128]{2,1,0:T(8,128)(2,1)S(1)} custom-call(s32[1]{0:T(128)} %bitcast.4.me_ref.refs_0_, s32[128,128]{1,0:T(8,128)S(1)} %bitcast.21, bf16[14,64,128]{2,1,0:T(8,128)(2,1)S(1)} %get-tuple-element.78.tri, bf16[2,14,16,128]{3,2,1,0:T(8,128)(2,1)S(1)} %get-tuple-element.79.tail), custom_call_target="tpu_custom_call" | custom-call | tf_op jit(solution)/shard_map/serve/pallas_call | solution.py:471
  27.8 0.0 copy-start.1
  27.8 0.0 copy-start.2
  27.8 0.0 copy-start.4
  27.8 0.0 copy-start.7
  27.8 68.0 %all_to_all.36.refs_5_ = bf16[128,144,128]{2,1,0:T(8,128)(2,1)S(1)} all-to-all(bf16[128,144,128]{2,1,0:T(8,128)(2,1)S(1)} %serve.1), channel_id=1, replica_groups=mesh['rows'=128] {'rows'}, dimensions={0} | all-to-all | bytes 9437184 | tf_op jit(solution)/shard_map/all_to_all | solution.py:424
  95.8 0.0 copy-done.1
  95.8 0.0 copy-done.2
  95.8 0.0 copy-done.4
  95.9 0.0 copy-done.7
  95.9 17.5 %row.1 = (bf16[14,256,128]{2,1,0:T(8,128)(2,1)S(1)}, f32[14,32,128]{2,1,0:T(8,128)}, bf16[256,32,128]{2,1,0:T(8,128)(2,1)}) custom-call(s32[42]{0:T(128)S(1)} %get-tuple-element.75.refs_0_, bf16[14,128,128]{2,1,0:T(8,128)(2,1)S(1)} %copy-done.1, bf16[14,128]{1,0:T(8,128)(2,1)S(1)} %copy-done.4, bf16[14,3,128,128]{3,2,1,0:T(8,128)(2,1)S(1)} %copy-done.7, ...), custom_call_target="tpu_custom_call" | custom-call | tf_op jit(solution)/shard_map/row/pallas_call | solution.py:479
  113.4 5.6 %all-to-all-start.4 = ((bf16[128,64,128]{2,1,0:T(8,128)(2,1)}), bf16[128,64,128]{2,1,0:T(8,128)(2,1)}, u32[]{:S(2)}, u32[]{:S(2)}) async-start(bf16[128,64,128]{2,1,0:T(8,128)(2,1)} %bitcast.26), calls=%async_computation.4 | async-start | bytes 4194304 | tf_op jit(solution)/shard_map/all_to_all | solution.py:424
  119.0 5.9 %between.1 = (bf16[14,128,256]{2,1,0:T(8,128)(2,1)S(1)}, f32[14,32,128]{2,1,0:T(8,128)S(1)}, s32[258]{0:T(512)S(1)}, s32[258]{0:T(512)S(1)}, s32[1]{0:T(128)}, /*index=5*/s32[1]{0:T(128)}) custom-call(s32[1]{0:T(128)} %bitcast.4.me_ref.refs_0_, s32[128,128]{1,0:T(8,128)S(1)} %bitcast.22, s32[128,128]{1,0:T(8,128)S(1)} %bitcast.23, ...), custom_call_target="tpu_custom_call" | custom-call | flops 2000000000 | bytes 10000000 | tf_op jit(solution)/shard_map/between/pallas_call | solution.py:492
  125.6 23.7 %all-to-all-done.4 = bf16[128,64,128]{2,1,0:T(8,128)(2,1)} async-done(((bf16[128,64,128]{2,1,0:T(8,128)(2,1)}), bf16[128,64,128]{2,1,0:T(8,128)(2,1)}, u32[]{:S(2)}, u32[]{:S(2)}) %all-to-all-start.4) | async-done | bytes 2097184 | tf_op jit(solution)/shard_map/all_to_all | solution.py:424
  149.3 57.8 %conditional.1 = ((f32[14,32,128]{2,1,0:T(8,128)S(1)}, bf16[256,32,128]{2,1,0:T(8,128)(2,1)})) conditional(s32[]{:T(128)} %bitcast.10, (s32[42]{0:T(128)S(1)}, s32[258]{0:T(512)S(1)}, s32[258]{0:T(512)S(1)}, s32[1]{0:T(128)}, bf16[256,32,128]{2,1,0:T(8,128)(2,1)}, /*index=5*/f32[14,32,128]{2,1,0:T(8,128)}, bf16[14,128,256]{2,1,0:T(8,128)(2,1)S(1)}, ...), branch_computations={%region_0.0_spmd, %region_1.0_spmd} | conditional | bytes 21233756 | solution.py:530
  149.3 0.0 copy-start.11
  149.3 6.0 %left.2 = bf16[128,3,32,128]{3,2,1,0:T(8,128)(2,1)S(1)} custom-call(s32[42]{0:T(128)S(1)} %get-tuple-element.41.refs_0_, s32[258]{0:T(512)S(1)} %get-tuple-element.42.refs_1_, s32[258]{0:T(512)S(1)} %get-tuple-element.43.refs_2_, s32[1]{0:T(128)} %get-tuple-element.44.refs_3_, bf16[256,32,128]{2,1,0:T(8,128)(2,1)} %get-tuple-element.45.refs_4_, ...), custom_call_target="tpu_custom_call" | custom-call | tf_op jit(solution)/shard_map/cond/branch_0_fun/left/pallas_call | solution.py:510
  155.3 0.0 copy-done.11
  155.3 0.0 copy-start.9
  155.3 0.0 copy-start.12
  155.3 46.0 %all_to_all.34 = bf16[128,96,128]{2,1,0:T(8,128)(2,1)S(1)} all-to-all(bf16[128,96,128]{2,1,0:T(8,128)(2,1)S(1)} %bitcast.19), channel_id=1, replica_groups=mesh['rows'=128] {'rows'}, dimensions={0} | all-to-all | bytes 6291456 | tf_op jit(solution)/shard_map/cond/branch_0_fun/all_to_all | solution.py:424
  201.3 0.0 copy-done.9
  201.3 0.0 copy-done.12
  201.3 5.8 %middle.2 = (f32[14,32,128]{2,1,0:T(8,128)S(1)}, bf16[256,32,128]{2,1,0:T(8,128)(2,1)}) custom-call(s32[42]{0:T(128)S(1)} %get-tuple-element.41.refs_0_, s32[258]{0:T(512)S(1)} %get-tuple-element.42.refs_1_, s32[258]{0:T(512)S(1)} %get-tuple-element.43.refs_2_, s32[1]{0:T(128)} %get-tuple-element.44.refs_3_, bf16[128,3,32,128]{3,2,1,0:T(8,128)(2,1)S(1)} %bitcast.18, ...), custom_call_target="tpu_custom_call" | custom-call | tf_op jit(solution)/shard_map/cond/branch_0_fun/middle/pallas_call | solution.py:521
  207.1 0.0 copy-start.8
  207.1 35.4 %all_to_all.37 = bf16[128,64,128]{2,1,0:T(8,128)(2,1)S(1)} all-to-all(bf16[128,64,128]{2,1,0:T(8,128)(2,1)} %bitcast.27), channel_id=1, replica_groups=mesh['rows'=128] {'rows'}, dimensions={0} | all-to-all | bytes 4194304 | tf_op jit(solution)/shard_map/all_to_all | solution.py:424
  242.5 0.0 copy-done.8
  242.5 3.5 %result.1 = f32[32,1792]{1,0:T(8,128)} custom-call(s32[42]{0:T(128)S(1)} %get-tuple-element.75.refs_0_, bf16[256,32,128]{2,1,0:T(8,128)(2,1)S(1)} %bitcast.20, f32[14,32,128]{2,1,0:T(8,128)S(1)} %get-tuple-element.89.refs_2_, bf16[14,256,128]{2,1,0:T(8,128)(2,1)S(1)} %get-tuple-element.90.refs_3_, bf16[14,3,128,128]{3,2,1,0:T(8,128)(2,1)S(1)} %copy-done.8), custom_call_target="tpu_custom_call" | custom-call | tf_op jit(solution)/shard_map/result/pallas_call | solution.py:537
Async XLA Ops:
  0.0 0.7 copy-start.5
  0.7 0.7 copy-start.6
  2.9 21.8 %all-to-all-start.2 = ((s32[128,1,128]{2,1,0:T(1,128)}), s32[128,1,128]{2,1,0:T(1,128)S(1)}, u32[]{:S(2)}, u32[]{:S(2)}) async-start(s32[128,1,128]{2,1,0:T(1,128)} %bitcast.8), calls=%async_computation.2 | async-start | bytes 131072 | tf_op jit(solution)/shard_map/all_to_all | solution.py:424
  14.4 1.0 copy-start
  15.4 0.7 copy-start.3
  27.8 68.1 %copy-start.1 = (bf16[14,128,128]{2,1,0:T(8,128)(2,1)S(1)}, bf16[14,128,128]{2,1,0:T(8,128)(2,1)}, u32[]{:S(2)}) copy-start(bf16[14,128,128]{2,1,0:T(8,128)(2,1)} %refs_4_.4) | copy-start | bytes 1376260
  27.8 68.1 %copy-start.2 = (f32[32,1792]{1,0:T(8,128)S(1)}, f32[32,1792]{1,0:T(8,128)}, u32[]{:S(2)}) copy-start(f32[32,1792]{1,0:T(8,128)} %refs_4_.3) | copy-start | bytes 688132
  27.8 68.1 %copy-start.4 = (bf16[14,128]{1,0:T(8,128)(2,1)S(1)}, bf16[14,128]{1,0:T(8,128)(2,1)}, u32[]{:S(2)}) copy-start(bf16[14,128]{1,0:T(8,128)(2,1)} %refs_5_.1) | copy-start | bytes 10756
  27.8 68.0 %copy-start.7 = (bf16[14,3,128,128]{3,2,1,0:T(8,128)(2,1)S(1)}, bf16[14,3,128,128]{3,2,1,0:T(8,128)(2,1)}, u32[]{:S(2)}) copy-start(bf16[14,3,128,128]{3,2,1,0:T(8,128)(2,1)} %refs_4_.5) | copy-start | bytes 4128772
  113.4 35.9 %all-to-all-start.4 = ((bf16[128,64,128]{2,1,0:T(8,128)(2,1)}), bf16[128,64,128]{2,1,0:T(8,128)(2,1)}, u32[]{:S(2)}, u32[]{:S(2)}) async-start(bf16[128,64,128]{2,1,0:T(8,128)(2,1)} %bitcast.26), calls=%async_computation.4 | async-start | bytes 4194304 | tf_op jit(solution)/shard_map/all_to_all | solution.py:424
  149.3 6.0 %copy-start.11 = (bf16[14,128,256]{2,1,0:T(8,128)(2,1)}, bf16[14,128,256]{2,1,0:T(8,128)(2,1)S(1)}, u32[]{:S(2)}) copy-start(bf16[14,128,256]{2,1,0:T(8,128)(2,1)S(1)} %get-tuple-element.47.refs_6_) | copy-start | bytes 2752516 | tf_op jit(solution)/shard_map/cond
  155.3 46.0 %copy-start.9 = (bf16[14,3,128,128]{3,2,1,0:T(8,128)(2,1)S(1)}, bf16[14,3,128,128]{3,2,1,0:T(8,128)(2,1)}, u32[]{:S(2)}) copy-start(bf16[14,3,128,128]{3,2,1,0:T(8,128)(2,1)} %get-tuple-element.48.refs_7_) | copy-start | bytes 4128772 | tf_op jit(solution)/shard_map/cond
  155.3 46.0 %copy-start.12 = (bf16[14,128,256]{2,1,0:T(8,128)(2,1)S(1)}, bf16[14,128,256]{2,1,0:T(8,128)(2,1)}, u32[]{:S(2)}) copy-start(bf16[14,128,256]{2,1,0:T(8,128)(2,1)} %copy-done.11) | copy-start | bytes 2752516 | tf_op jit(solution)/shard_map/cond
  207.1 35.4 %copy-start.8 = (bf16[14,3,128,128]{3,2,1,0:T(8,128)(2,1)S(1)}, bf16[14,3,128,128]{3,2,1,0:T(8,128)(2,1)}, u32[]{:S(2)}) copy-start(bf16[14,3,128,128]{3,2,1,0:T(8,128)(2,1)} %refs_4_.5) | copy-start | bytes 4128772

commit v6 on v5

--- a/solution.py
+++ b/solution.py
@@ -12,9 +12,11 @@
 BF16 = jnp.bfloat16
 BLK = 128
 SLOTS = 2
+CORES = 2
 TRI = 64
 TAIL = 16
-CHUNK = 2 * TRI + TAIL
+HALF = TRI // 2
+PAY = TRI + SLOTS * TAIL
 SEG = 16
 STEP = 8
 GROUP = BLK // SEG
@@ -204,7 +206,7 @@
     return sym + jnp.where(sub == lane, shift_row, 0.0)
 
 
-def route_kernel(me_ref, dev_ref, slot_ref, ask_ref, pos_ref, count_ref):
+def route_kernel(me_ref, dev_ref, slot_ref, ask_ref, pos_ref, chip_ref, count_ref):
     n_dev = count_ref.shape[0]
     me = me_ref[0]
 
@@ -225,11 +227,24 @@
             code = jnp.where(rank == 0, code, code * CODE)
             codes = codes + jnp.where(lane == t, code, 0)
             pos_ref[i * 3 + m] = t * SLOTS + rank
+    for q in range(3 * dev_ref.shape[1]):
+        at = pos_ref[q]
+        t = at // SLOTS
+        core = t % CORES
+        chip_ref[q] = at + core * (count_ref[t - core] - SLOTS)
     for t in range(n_dev // 8):
         ask_ref[8 * t : 8 * t + 8, :] = codes
 
 
-def invert_kernel(factor_value, noise, shift, x_out, tri_out, tail_out, z):
+def crowd_kernel(table, crowd):
+    n_dev = table.shape[1]
+    asked = (table[...] > 0).astype(F32) + (table[...] >= CODE).astype(F32)
+    _, device = iotas(n_dev, n_dev)
+    shared = jnp.where(device % CORES == 0, asked + pltpu.roll(asked, n_dev - 1, 1), 0.0)
+    crowd[0] = (jnp.max(shared) > SLOTS + 1.5).astype(jnp.int32)
+
+
+def invert_kernel(factor_value, noise, shift, x_out, pay_out, z):
     count = noise.shape[0]
     for b in range(count):
         z[b] = build_diag(noise, shift, b, factor_value)
@@ -244,7 +259,7 @@
         bottom = jnp.concatenate([x[TRI:].astype(BF16), jnp.zeros((TRI, BLK), BF16)], axis=0)
         turned = dot(low_eye, bottom, 1, 1)
         tri = jnp.where(top_lane > top_sub, x[:TRI], jnp.where(top_lane < top_sub, turned, 0.0))
-        tri_out[b] = tri.astype(BF16)
+        pay_out[b, :TRI] = tri.astype(BF16)
         diag = jnp.sum(jnp.where(sub == lane, x, 0.0), axis=0, keepdims=True)
         hi, lo = split(diag)
         hi, lo = hi.astype(F32), lo.astype(F32)
@@ -252,25 +267,54 @@
             tail = jnp.where(
                 tail_sub == 2 * r, hi, jnp.where(tail_sub == 2 * r + 1, lo, 0.0)
             )
-            tail_out[r, b] = tail.astype(BF16)
-
-
-def serve_kernel(me_ref, incoming, tri, tail, out):
+            pay_out[b, TRI + r * TAIL : TRI + (r + 1) * TAIL] = tail.astype(BF16)
+
+
+def serve_kernel(me_ref, incoming, pay, out):
     me = me_ref[0]
 
     def one(t, carry):
         code = incoming[t, me]
         slots = [jnp.maximum(code % CODE - 1, 0), jnp.maximum(code // CODE - 1, 0)]
         for r in range(SLOTS):
-            out[t, r * TRI : (r + 1) * TRI] = tri[slots[r]]
-        out[t, SLOTS * TRI :] = tail[0, slots[0]] + tail[1, slots[1]]
+            out[t, r * TRI : (r + 1) * TRI] = pay[slots[r], :TRI]
+        out[t, SLOTS * TRI :] = pay[slots[0], TRI : TRI + TAIL] + pay[slots[1], TRI + TAIL :]
         return carry
 
     lax.fori_loop(0, out.shape[0], one, 0, unroll=8)
 
 
+def serve_chip_kernel(me_ref, incoming, own, sibling, out, pay):
+    me = me_ref[0]
+    core = me % CORES
+    pay[core] = own[...]
+    pay[1 - core] = sibling[...]
+    half = pl.multiple_of(core * HALF, HALF)
+
+    def one(t, carry):
+        low = incoming[t, me - core]
+        high = incoming[t, me - core + 1]
+        first, second = low % CODE, low // CODE
+        third, fourth = high % CODE, high // CODE
+        none, one_low = first == 0, second == 0
+        mine_core = jnp.where(core == 0, none, one_low).astype(jnp.int32)
+        mine = jnp.where(
+            core == 0,
+            jnp.where(none, third, first),
+            jnp.where(none, fourth, jnp.where(one_low, third, second)),
+        )
+        mine = jnp.maximum(mine - 1, 0)
+        last = jnp.maximum(jnp.where(one_low, fourth, third) - 1, 0)
+        out[t, :TRI] = pay[mine_core, mine, :TRI]
+        out[t, TRI : TRI + HALF] = pay[1, last, pl.ds(half, HALF)]
+        out[t, TRI + HALF :] = pay[mine_core, mine, TRI : TRI + TAIL] + pay[1, last, TRI + TAIL :]
+        return carry
+
+    lax.fori_loop(0, out.shape[0], one, 0, unroll=8)
+
+
 def row_kernel(
-    factor_value, coupling_factor, pos, noise, shift, couplings, vectors, arrived,
+    factor_value, coupling_factor, by_chip, pos, chip_pos, noise, shift, couplings, vectors, arrived,
     w_out, y_out, send, z, stage, sems,
 ):
     count = noise.shape[0]
@@ -286,14 +330,31 @@
         wide = []
         for m in range(3):
             q = b * 3 + m
-            at = pos[q]
-            dev, rank = at // SLOTS, at % SLOTS
-            first = pl.multiple_of(rank * TRI, TRI)
-            tri = arrived[dev, pl.ds(first, TRI), :].astype(F32)
+            if by_chip:
+                at = chip_pos[q]
+                chip, k = at // (CORES * SLOTS), at % (CORES * SLOTS)
+                rank = k // SLOTS
+                dev = chip * CORES + k % SLOTS
+                dev_two = dev + rank
+                row = rank * TRI
+                row_two = jnp.where(rank == 0, HALF, TRI)
+            else:
+                at = pos[q]
+                dev, rank = at // SLOTS, at % SLOTS
+                dev_two = dev
+                row = rank * TRI
+                row_two = row + HALF
+            tri = jnp.concatenate(
+                [
+                    arrived[dev, pl.ds(pl.multiple_of(row, HALF), HALF), :],
+                    arrived[dev_two, pl.ds(pl.multiple_of(row_two, HALF), HALF), :],
+                ],
+                axis=0,
+            ).astype(F32)
             upper = jnp.where(top_lane > top_sub, tri, 0.0).astype(BF16)
             lower = pltpu.roll(jnp.where(top_lane < top_sub, tri, 0.0), TRI, 1).astype(BF16)
             diag = jnp.sum(
-                jnp.where(tail_sub // 2 == rank, arrived[dev, SLOTS * TRI :, :].astype(F32), 0.0),
+                jnp.where(tail_sub // 2 == rank, arrived[dev, arrived.shape[1] - TAIL :, :].astype(F32), 0.0),
                 axis=0,
                 keepdims=True,
             )
@@ -305,7 +366,7 @@
         z[b] = z[b] - dot(wide, wide, 1, 1) * (coupling_factor * coupling_factor)
         return carry
 
-    lax.fori_loop(0, count, schur, 0, unroll=2)
+    lax.fori_loop(0, count, schur, 0, unroll=7)
     factor(z, count)
     sub, lane = iotas(BLK)
     copies = []
@@ -445,49 +506,82 @@
 
         return wrapped
 
-    ask, pos = call(
+    ask, pos, chip_pos = call(
         route_kernel,
-        (shape((n_dev, n_dev), jnp.int32), shape((3 * count,), jnp.int32)),
+        (
+            shape((n_dev, n_dev), jnp.int32),
+            shape((3 * count,), jnp.int32),
+            shape((3 * count,), jnp.int32),
+        ),
         [SM, SM, SM],
-        (VM, SM),
+        (VM, SM, SM),
         [SM((n_dev,), jnp.int32)],
         name="route",
     )(me, near_devices.T, near_slots.T)
     table = exchange(ask)
-    x, tri, tail = call(
+    x, pay = call(
         with_factors(invert_kernel, factor_value),
-        (
-            blocks,
-            shape((count, TRI, BLK), BF16),
-            shape((SLOTS, count, TAIL, BLK), BF16),
-        ),
+        (blocks, shape((count, PAY, BLK), BF16)),
         [VM, VM],
-        (VM, VM, VM),
+        (VM, VM),
         [VM((count, BLK, BLK), F32)],
         flops=2 * 10**9,
         moved=10**8,
         name="invert",
     )(diag_noise, shifts)
-    answer = call(
-        serve_kernel,
-        shape((n_dev, CHUNK, BLK), BF16),
-        [SM, SM, VM, VM],
-        VM,
-        name="serve",
-    )(me, table, tri, tail)
-    arrived = exchange(answer)
-    w, y, push = call(
-        with_factors(row_kernel, factor_value, coupling_factor),
-        (shape((count, 2 * BLK, BLK), BF16), rows, pltpu.HBM((total_slots, n_vec, BLK), BF16)),
-        [SM, VM, VM, VM, VM, VM],
-        (VM, VM, pltpu.HBM),
-        [
-            VM((count, BLK, BLK), F32),
-            VM((3 * count, n_vec, BLK), BF16),
-            pltpu.SemaphoreType.DMA((3 * count,)),
-        ],
-        name="row",
-    )(pos, diag_noise, shifts, couplings, vectors, arrived)
+    pay, table = lax.optimization_barrier((pay, table))
+    sibling = lax.ppermute(pay, "rows", [(i, i + 1 - 2 * (i % CORES)) for i in range(n_dev)])
+    crowd = call(
+        crowd_kernel,
+        shape((1,), jnp.int32),
+        [VM],
+        SM,
+        flops=10**8,
+        moved=10**6,
+        name="crowd",
+    )(table)
+
+    def setup(by_chip, me, table, pay, sibling, pos, chip_pos, diag_noise, shifts, couplings, vectors):
+        if by_chip:
+            answer = call(
+                serve_chip_kernel,
+                shape((n_dev, TRI + HALF + TAIL, BLK), BF16),
+                [SM, SM, VM, VM],
+                VM,
+                [VM((CORES, count, PAY, BLK), BF16)],
+                name="serve",
+            )(me, table, pay, sibling)
+        else:
+            answer = call(
+                serve_kernel,
+                shape((n_dev, SLOTS * TRI + TAIL, BLK), BF16),
+                [SM, SM, VM],
+                VM,
+                name="serve",
+            )(me, table, pay)
+        return call(
+            with_factors(row_kernel, factor_value, coupling_factor, by_chip),
+            (
+                shape((count, 2 * BLK, BLK), BF16),
+                rows,
+                pltpu.HBM((total_slots, n_vec, BLK), BF16),
+            ),
+            [SM, SM, VM, VM, VM, VM, VM],
+            (VM, VM, pltpu.HBM),
+            [
+                VM((count, BLK, BLK), F32),
+                VM((3 * count, n_vec, BLK), BF16),
+                pltpu.SemaphoreType.DMA((3 * count,)),
+            ],
+            name="row",
+        )(pos, chip_pos, diag_noise, shifts, couplings, vectors, exchange(answer))
+
+    w, y, push = lax.cond(
+        crowd[0] > 0,
+        functools.partial(setup, False),
+        functools.partial(setup, True),
+        me, table, pay, sibling, pos, chip_pos, diag_noise, shifts, couplings, vectors,
+    )
     pushed = exchange(push.reshape(n_dev, SLOTS * n_vec, BLK)).reshape(total_slots, n_vec, BLK)
     e, own, *lists, clash = call(
         with_factors(between_kernel, factor_value),

time: 246 us -> 237 us (0.963)
  blocking collectives: 149 us -> 137 us
  Pallas kernels: 51.9 us -> 54.6 us
    all_to_all x3, blocking collectives: 149 us -> 137 us  [exchange(): return lax.all_to_all(x, 'rows', split_axis=0, concat_axis=0, tiled=True)]
    pallas_call x3 -> x4, Pallas kernels: 29.2 us -> 31.9 us  [the longest x1 16.8 us: setup(): call(with_factors(row_kernel, factor_value, coupling_factor, by_chip), (s...]
  transfers between devices with their start and end apart: 2 -> 3, of which waited for: 1 -> 1; matrix products, arithmetic and copies ran while one was open for 0% -> 0% of each run, Pallas kernels for 6% -> 7%
where the time goes in v6:
time: 237 us; the launch traced here: 236 us
  blocking collectives  137 us (58%)
  Pallas kernels  54.6 us (23%)
  waiting for transfers between devices  23.7 us (10%)
  starting transfers between devices  18 us (8%)
    all_to_all x3, blocking collectives, exchange(): return lax.all_to_all(x, 'rows', split_axis=0, concat_axis=0, tiled=True)  137 us
    all_to_all x2, waiting for transfers between devices, exchange(): return lax.all_to_all(x, 'rows', split_axis=0, concat_axis=0, tiled=True)  23.7 us
    all_to_all x2, starting transfers between devices, exchange(): return lax.all_to_all(x, 'rows', split_axis=0, concat_axis=0, tiled=True)  16.8 us
    pallas_call x1, Pallas kernels, setup(): call(with_factors(row_kernel, factor_value, coupling_factor, by_chip), (s...  16.8 us
    pallas_call x1, Pallas kernels, body(): call(with_factors(invert_kernel, factor_value), (blocks, shape((count, PA...  9.78 us
    pallas_call x1, Pallas kernels, body(): call(with_factors(between_kernel, factor_value), (shape((count, BLK, 2 *...  5.93 us
    pallas_call x1, Pallas kernels, swap(): call(with_factors(middle_kernel, coupling_factor), (rows, shape((total_sl...  5.7 us
    pallas_call x1, Pallas kernels, swap(): call(with_factors(left_kernel, coupling_factor), shape((n_dev, slots, n_v...  5.65 us
  transfers between devices with their start and end apart: 3, of which 1 were waited for; matrix products, arithmetic and copies ran while one was open for 0% of the time, Pallas kernels for 7%

profile of v6, /device:TPU:1, one launch (start us, length us, event | category | flops | bytes accessed | tf_op | source)
XLA Modules:
  0.0 236.4 jit_solution(10356422035470904379)
XLA Ops:
  0.0 0.0 copy-start
  0.0 0.7 copy-done
  0.7 0.0 copy-start.1
  0.7 0.7 copy-done.1
  1.4 1.9 route.1
  3.2 11.5 %all-to-all-start.4 = ((s32[128,1,128]{2,1,0:T(1,128)}), s32[128,1,128]{2,1,0:T(1,128)S(1)}, u32[]{:S(2)}, u32[]{:S(2)}) async-start(s32[128,1,128]{2,1,0:T(1,128)} %bitcast.8), calls=%async_computation.4 | async-start | bytes 131072 | tf_op jit(solution)/shard_map/all_to_all | solution.py:485
  14.8 0.0 copy-start.2
  14.8 0.0 copy-start.3
  14.8 0.0 copy-start.5
  14.8 0.0 copy-start.6
  14.8 9.8 %invert.1 = (f32[14,128,128]{2,1,0:T(8,128)S(1)}, bf16[14,96,128]{2,1,0:T(8,128)(2,1)S(1)}) custom-call(bf16[14,128,128]{2,1,0:T(8,128)(2,1)} %refs_4_.2, bf16[14,128]{1,0:T(8,128)(2,1)} %refs_5_.1), custom_call_target="tpu_custom_call" | custom-call | flops 2000000000 | bytes 100000000 | tf_op jit(solution)/shard_map/invert/pallas_call | solution.py:522
  24.6 0.0 all-to-all-done.4
  24.6 1.1 collective-permute-start
  25.7 0.7 crowd.1
  27.1 0.0 collective-permute-done
  27.1 0.0 copy-done.2
  27.1 0.0 copy-done.3
  27.2 0.0 copy-done.5
  27.2 0.0 copy-done.6
  27.2 77.9 %conditional.2 = ((bf16[14,256,128]{2,1,0:T(8,128)(2,1)}, f32[14,32,128]{2,1,0:T(8,128)}, bf16[256,32,128]{2,1,0:T(8,128)(2,1)})) conditional(s32[]{:T(128)} %bitcast.10, (s32[1]{0:T(128)}, s32[128,128]{1,0:T(8,128)S(1)}, bf16[14,96,128]{2,1,0:T(8,128)(2,1)S(1)}, bf16[14,96,128]{2,1,0:T(8,128)(2,1)S(1)}, s32[42]{0:T(128)S(1)}, ...), branch_computations={%region_0.0_spmd, %region_1.0_spmd} | conditional | bytes 9437192 | solution.py:579
  27.2 4.6 %serve.2 = bf16[128,112,128]{2,1,0:T(8,128)(2,1)S(1)} custom-call(s32[1]{0:T(128)} %get-tuple-element.85.me_ref, s32[128,128]{1,0:T(8,128)S(1)} %get-tuple-element.86.incoming, bf16[14,96,128]{2,1,0:T(8,128)(2,1)S(1)} %get-tuple-element.87.own, bf16[14,96,128]{2,1,0:T(8,128)(2,1)S(1)} %get-tuple-element.88.sibling), custom_call_target="tpu_custom_call" | custom-call | tf_op jit(solution)/shard_map/cond/branch_0_fun/serve/pallas_call | solution.py:546
  31.8 56.3 %all_to_all.38.refs_6_ = bf16[128,112,128]{2,1,0:T(8,128)(2,1)S(1)} all-to-all(bf16[128,112,128]{2,1,0:T(8,128)(2,1)S(1)} %serve.2), channel_id=1, replica_groups=mesh['rows'=128] {'rows'}, dimensions={0} | all-to-all | bytes 7340032 | tf_op jit(solution)/shard_map/cond/branch_0_fun/all_to_all | solution.py:485
  88.1 16.8 %row.2 = (bf16[14,256,128]{2,1,0:T(8,128)(2,1)}, f32[14,32,128]{2,1,0:T(8,128)}, bf16[256,32,128]{2,1,0:T(8,128)(2,1)}) custom-call(s32[42]{0:T(128)S(1)} %get-tuple-element.79.refs_0_, s32[42]{0:T(128)S(1)} %get-tuple-element.80.refs_1_, bf16[14,128,128]{2,1,0:T(8,128)(2,1)S(1)} %get-tuple-element.81.refs_2_, ...), custom_call_target="tpu_custom_call" | custom-call | tf_op jit(solution)/shard_map/cond/branch_0_fun/row/pallas_call | solution.py:562
  105.1 5.3 %all-to-all-start.5 = ((bf16[128,64,128]{2,1,0:T(8,128)(2,1)}), bf16[128,64,128]{2,1,0:T(8,128)(2,1)}, u32[]{:S(2)}, u32[]{:S(2)}) async-start(bf16[128,64,128]{2,1,0:T(8,128)(2,1)} %bitcast.24), calls=%async_computation.5 | async-start | bytes 4194304 | tf_op jit(solution)/shard_map/all_to_all | solution.py:485
  110.5 5.9 %between.1 = (bf16[14,128,256]{2,1,0:T(8,128)(2,1)S(1)}, f32[14,32,128]{2,1,0:T(8,128)S(1)}, s32[258]{0:T(512)S(1)}, s32[258]{0:T(512)S(1)}, s32[1]{0:T(128)}, /*index=5*/s32[1]{0:T(128)}) custom-call(s32[1]{0:T(128)} %bitcast.4.me_ref.refs_0_, s32[128,128]{1,0:T(8,128)S(1)} %bitcast.29, s32[128,128]{1,0:T(8,128)S(1)} %bitcast.30, ...), custom_call_target="tpu_custom_call" | custom-call | flops 2000000000 | bytes 10000000 | tf_op jit(solution)/shard_map/between/pallas_call | solution.py:586
  117.1 23.7 %all-to-all-done.5 = bf16[128,64,128]{2,1,0:T(8,128)(2,1)} async-done(((bf16[128,64,128]{2,1,0:T(8,128)(2,1)}), bf16[128,64,128]{2,1,0:T(8,128)(2,1)}, u32[]{:S(2)}, u32[]{:S(2)}) %all-to-all-start.5) | async-done | bytes 2097184 | tf_op jit(solution)/shard_map/all_to_all | solution.py:485
  140.8 57.0 %conditional.3 = ((f32[14,32,128]{2,1,0:T(8,128)S(1)}, bf16[256,32,128]{2,1,0:T(8,128)(2,1)})) conditional(s32[]{:T(128)} %bitcast.11, (s32[42]{0:T(128)S(1)}, s32[258]{0:T(512)S(1)}, s32[258]{0:T(512)S(1)}, s32[1]{0:T(128)}, bf16[256,32,128]{2,1,0:T(8,128)(2,1)}, /*index=5*/f32[14,32,128]{2,1,0:T(8,128)}, bf16[14,128,256]{2,1,0:T(8,128)(2,1)S(1)}, ...), branch_computations={%region_2.0_spmd, %region_3.0_spmd} | conditional | bytes 8388616 | solution.py:624
  140.8 5.7 %left.2 = bf16[128,3,32,128]{3,2,1,0:T(8,128)(2,1)S(1)} custom-call(s32[42]{0:T(128)S(1)} %get-tuple-element.98.refs_0_, s32[258]{0:T(512)S(1)} %get-tuple-element.99.refs_1_, s32[258]{0:T(512)S(1)} %get-tuple-element.100.refs_2_, s32[1]{0:T(128)} %get-tuple-element.101.refs_3_, bf16[256,32,128]{2,1,0:T(8,128)(2,1)} %get-tuple-element.102.refs_4_, ...), custom_call_target="tpu_custom_call" | custom-call | tf_op jit(solution)/shard_map/cond/branch_0_fun/left/pallas_call | solution.py:604
  146.4 45.6 %all_to_all.40 = bf16[128,96,128]{2,1,0:T(8,128)(2,1)S(1)} all-to-all(bf16[128,96,128]{2,1,0:T(8,128)(2,1)S(1)} %bitcast.20), channel_id=1, replica_groups=mesh['rows'=128] {'rows'}, dimensions={0} | all-to-all | bytes 6291456 | tf_op jit(solution)/shard_map/cond/branch_0_fun/all_to_all | solution.py:485
  192.1 5.7 %middle.2 = (f32[14,32,128]{2,1,0:T(8,128)S(1)}, bf16[256,32,128]{2,1,0:T(8,128)(2,1)}) custom-call(s32[42]{0:T(128)S(1)} %get-tuple-element.98.refs_0_, s32[258]{0:T(512)S(1)} %get-tuple-element.99.refs_1_, s32[258]{0:T(512)S(1)} %get-tuple-element.100.refs_2_, s32[1]{0:T(128)} %get-tuple-element.101.refs_3_, bf16[128,3,32,128]{3,2,1,0:T(8,128)(2,1)S(1)} %bitcast.19, ...), custom_call_target="tpu_custom_call" | custom-call | tf_op jit(solution)/shard_map/cond/branch_0_fun/middle/pallas_call | solution.py:615
  197.8 0.0 copy-start.4
  197.8 35.2 %all_to_all.42 = bf16[128,64,128]{2,1,0:T(8,128)(2,1)S(1)} all-to-all(bf16[128,64,128]{2,1,0:T(8,128)(2,1)} %bitcast.25), channel_id=1, replica_groups=mesh['rows'=128] {'rows'}, dimensions={0} | all-to-all | bytes 4194304 | tf_op jit(solution)/shard_map/all_to_all | solution.py:485
  232.9 0.0 copy-done.4
  232.9 3.5 %result.1 = f32[32,1792]{1,0:T(8,128)} custom-call(s32[42]{0:T(128)S(1)} %get-tuple-element.134.refs_0_, bf16[256,32,128]{2,1,0:T(8,128)(2,1)S(1)} %bitcast.21, f32[14,32,128]{2,1,0:T(8,128)S(1)} %get-tuple-element.150.refs_2_, bf16[14,256,128]{2,1,0:T(8,128)(2,1)S(1)} %copy-done.4, bf16[14,3,128,128]{3,2,1,0:T(8,128)(2,1)S(1)} %copy-done.2), custom_call_target="tpu_custom_call" | custom-call | tf_op jit(solution)/shard_map/result/pallas_call | solution.py:631
Async XLA Ops:
  0.0 0.7 copy-start
  0.7 0.7 copy-start.1
  3.2 21.3 %all-to-all-start.4 = ((s32[128,1,128]{2,1,0:T(1,128)}), s32[128,1,128]{2,1,0:T(1,128)S(1)}, u32[]{:S(2)}, u32[]{:S(2)}) async-start(s32[128,1,128]{2,1,0:T(1,128)} %bitcast.8), calls=%async_computation.4 | async-start | bytes 131072 | tf_op jit(solution)/shard_map/all_to_all | solution.py:485
  14.8 12.4 %copy-start.2 = (bf16[14,3,128,128]{3,2,1,0:T(8,128)(2,1)S(1)}, bf16[14,3,128,128]{3,2,1,0:T(8,128)(2,1)}, u32[]{:S(2)}) copy-start(bf16[14,3,128,128]{3,2,1,0:T(8,128)(2,1)} %refs_4_.3) | copy-start | bytes 4128772
  14.8 12.4 %copy-start.3 = (bf16[14,128,128]{2,1,0:T(8,128)(2,1)S(1)}, bf16[14,128,128]{2,1,0:T(8,128)(2,1)}, u32[]{:S(2)}) copy-start(bf16[14,128,128]{2,1,0:T(8,128)(2,1)} %refs_4_.2) | copy-start | bytes 1376260
  14.8 12.4 %copy-start.5 = (f32[32,1792]{1,0:T(8,128)S(1)}, f32[32,1792]{1,0:T(8,128)}, u32[]{:S(2)}) copy-start(f32[32,1792]{1,0:T(8,128)} %param.15) | copy-start | bytes 688132
  14.8 12.4 %copy-start.6 = (bf16[14,128]{1,0:T(8,128)(2,1)S(1)}, bf16[14,128]{1,0:T(8,128)(2,1)}, u32[]{:S(2)}) copy-start(bf16[14,128]{1,0:T(8,128)(2,1)} %refs_5_.1) | copy-start | bytes 10756
  24.6 2.5 %collective-permute-start = (bf16[14,96,128]{2,1,0:T(8,128)(2,1)S(1)}, bf16[14,96,128]{2,1,0:T(8,128)(2,1)S(1)}, u32[]{:S(2)}, u32[]{:S(2)}) collective-permute-start(bf16[14,96,128]{2,1,0:T(8,128)(2,1)S(1)} %get-tuple-element.139), channel_id=1, source_target_pairs={{0,1},{1,0},{2,3},{3,2},{4,5},{5,4},{6,7},{7,6},{8,9},{9,8},{10,11... | collective-permute-start | bytes 1032200 | tf_op jit(solution)/shard_map/ppermute | solution.py:533
  105.1 35.7 %all-to-all-start.5 = ((bf16[128,64,128]{2,1,0:T(8,128)(2,1)}), bf16[128,64,128]{2,1,0:T(8,128)(2,1)}, u32[]{:S(2)}, u32[]{:S(2)}) async-start(bf16[128,64,128]{2,1,0:T(8,128)(2,1)} %bitcast.24), calls=%async_computation.5 | async-start | bytes 4194304 | tf_op jit(solution)/shard_map/all_to_all | solution.py:485
  197.8 35.2 %copy-start.4 = (bf16[14,256,128]{2,1,0:T(8,128)(2,1)S(1)}, bf16[14,256,128]{2,1,0:T(8,128)(2,1)}, u32[]{:S(2)}) copy-start(bf16[14,256,128]{2,1,0:T(8,128)(2,1)} %get-tuple-element.151.refs_3_) | copy-start | bytes 2752516

commit v7 on v6

--- a/solution.py
+++ b/solution.py
@@ -44,6 +44,14 @@
     )
 
 
+def whole(x, n):
+    return lax.shift_right_logical(x, jnp.int32(n.bit_length() - 1))
+
+
+def rest(x, n):
+    return x & (n - 1)
+
+
 def iotas(rows, lanes=BLK):
     return (
         lax.broadcasted_iota(jnp.int32, (rows, lanes), 0),
@@ -107,7 +115,7 @@
 
 def eliminate(packs):
     sub, lane = iotas(8)
-    start = lane - lane % SEG
+    start = lane - rest(lane, SEG)
     parts = [[p[8 * t : 8 * t + 8] for t in range(SEG // 8)] for p in packs]
     for k in range(SEG - 1, -1, -STEP):
         i = k // 8
@@ -153,7 +161,7 @@
 
 def factor(z, count):
     sub, lane = iotas(SEG)
-    seg = lane // SEG
+    seg = whole(lane, SEG)
     groups = -(-count // GROUP)
     for kb in range(GROUP - 1, -1, -1):
         r0 = kb * SEG
@@ -173,7 +181,7 @@
         packs = eliminate(packs)
         eye = (lane - r0 == sub).astype(F32)
         for q in range(groups):
-            w = jnp.where(lane % SEG >= sub, packs[q], 0.0)
+            w = jnp.where(rest(lane, SEG) >= sub, packs[q], 0.0)
             wide = jnp.concatenate([jnp.where(seg == g, w, 0.0) for g in range(GROUP)], axis=0)
             tall = jnp.concatenate(
                 [jnp.where(seg == kb, eye, panels[q][g]) for g in range(GROUP)], axis=0
@@ -193,7 +201,7 @@
                     top = z[b, 0:r0, :]
                     update = dot_wide(top, jnp.concatenate(pads, axis=0))
                     _, top_lane = iotas(r0)
-                    z[b, 0:r0, :] = jnp.where(top_lane // SEG == kb, 0.0, top) - update
+                    z[b, 0:r0, :] = jnp.where((top_lane >= r0) & (top_lane < r0 + SEG), 0.0, top) - update
 
 
 def build_diag(noise, shift, b, factor_value):
@@ -229,8 +237,8 @@
             pos_ref[i * 3 + m] = t * SLOTS + rank
     for q in range(3 * dev_ref.shape[1]):
         at = pos_ref[q]
-        t = at // SLOTS
-        core = t % CORES
+        t = whole(at, SLOTS)
+        core = rest(t, CORES)
         chip_ref[q] = at + core * (count_ref[t - core] - SLOTS)
     for t in range(n_dev // 8):
         ask_ref[8 * t : 8 * t + 8, :] = codes
@@ -240,7 +248,7 @@
     n_dev = table.shape[1]
     asked = (table[...] > 0).astype(F32) + (table[...] >= CODE).astype(F32)
     _, device = iotas(n_dev, n_dev)
-    shared = jnp.where(device % CORES == 0, asked + pltpu.roll(asked, n_dev - 1, 1), 0.0)
+    shared = jnp.where(rest(device, CORES) == 0, asked + pltpu.roll(asked, n_dev - 1, 1), 0.0)
     crowd[0] = (jnp.max(shared) > SLOTS + 1.5).astype(jnp.int32)
 
 
@@ -275,7 +283,7 @@
 
     def one(t, carry):
         code = incoming[t, me]
-        slots = [jnp.maximum(code % CODE - 1, 0), jnp.maximum(code // CODE - 1, 0)]
+        slots = [jnp.maximum(rest(code, CODE) - 1, 0), jnp.maximum(whole(code, CODE) - 1, 0)]
         for r in range(SLOTS):
             out[t, r * TRI : (r + 1) * TRI] = pay[slots[r], :TRI]
         out[t, SLOTS * TRI :] = pay[slots[0], TRI : TRI + TAIL] + pay[slots[1], TRI + TAIL :]
@@ -286,7 +294,7 @@
 
 def serve_chip_kernel(me_ref, incoming, own, sibling, out, pay):
     me = me_ref[0]
-    core = me % CORES
+    core = rest(me, CORES)
     pay[core] = own[...]
     pay[1 - core] = sibling[...]
     half = pl.multiple_of(core * HALF, HALF)
@@ -294,8 +302,8 @@
     def one(t, carry):
         low = incoming[t, me - core]
         high = incoming[t, me - core + 1]
-        first, second = low % CODE, low // CODE
-        third, fourth = high % CODE, high // CODE
+        first, second = rest(low, CODE), whole(low, CODE)
+        third, fourth = rest(high, CODE), whole(high, CODE)
         none, one_low = first == 0, second == 0
         mine_core = jnp.where(core == 0, none, one_low).astype(jnp.int32)
         mine = jnp.where(
@@ -332,15 +340,15 @@
             q = b * 3 + m
             if by_chip:
                 at = chip_pos[q]
-                chip, k = at // (CORES * SLOTS), at % (CORES * SLOTS)
-                rank = k // SLOTS
-                dev = chip * CORES + k % SLOTS
+                chip, k = whole(at, CORES * SLOTS), rest(at, CORES * SLOTS)
+                rank = whole(k, SLOTS)
+                dev = chip * CORES + rest(k, SLOTS)
                 dev_two = dev + rank
                 row = rank * TRI
                 row_two = jnp.where(rank == 0, HALF, TRI)
             else:
                 at = pos[q]
-                dev, rank = at // SLOTS, at % SLOTS
+                dev, rank = whole(at, SLOTS), rest(at, SLOTS)
                 dev_two = dev
                 row = rank * TRI
                 row_two = row + HALF
@@ -354,7 +362,7 @@
             upper = jnp.where(top_lane > top_sub, tri, 0.0).astype(BF16)
             lower = pltpu.roll(jnp.where(top_lane < top_sub, tri, 0.0), TRI, 1).astype(BF16)
             diag = jnp.sum(
-                jnp.where(tail_sub // 2 == rank, arrived[dev, arrived.shape[1] - TAIL :, :].astype(F32), 0.0),
+                jnp.where(whole(tail_sub, SLOTS) == rank, arrived[dev, arrived.shape[1] - TAIL :, :].astype(F32), 0.0),
                 axis=0,
                 keepdims=True,
             )
@@ -396,7 +404,7 @@
     def one(t, n):
         code = incoming[t, me]
         for r in range(SLOTS):
-            slot = (code % CODE if r == 0 else code // CODE) - 1
+            slot = (rest(code, CODE) if r == 0 else whole(code, CODE)) - 1
             list_pos[n] = t * SLOTS + r
             list_slot[n] = slot
             n = n + (slot >= 0).astype(jnp.int32)
@@ -433,11 +441,11 @@
         p = (rows_times_bf16(u, side_by_side(couplings, b)) * coupling_factor).astype(BF16)
         for m in range(3):
             at = pos[b * 3 + m]
-            send[at // SLOTS, push_slot(send.shape[1], at % SLOTS)] = p[:, m * BLK : (m + 1) * BLK]
+            send[whole(at, SLOTS), push_slot(send.shape[1], rest(at, SLOTS))] = p[:, m * BLK : (m + 1) * BLK]
 
     def give(t, carry):
         at = list_pos[t]
-        send[at // SLOTS, at % SLOTS] = left[list_slot[t]]
+        send[whole(at, SLOTS), rest(at, SLOTS)] = left[list_slot[t]]
         return carry
 
     lax.fori_loop(0, list_count[0], give, 0)
@@ -453,14 +461,14 @@
     def add(t, carry):
         slot = list_slot[t]
         at = list_pos[t]
-        place = push_slot(arrived.shape[1], at % SLOTS)
-        total[slot] += arrived[at // SLOTS, place].astype(F32)
+        place = push_slot(arrived.shape[1], rest(at, SLOTS))
+        total[slot] += arrived[whole(at, SLOTS), place].astype(F32)
         return carry
 
     lax.fori_loop(0, list_count[0], add, 0)
     for b in range(count):
         places = [pos[b * 3 + m] for m in range(3)]
-        near = jnp.concatenate([arrived[at // SLOTS, at % SLOTS] for at in places], axis=1)
+        near = jnp.concatenate([arrived[whole(at, SLOTS), rest(at, SLOTS)] for at in places], axis=1)
         near = dot(near, side_by_side(couplings, b), 1, 1)
         mid = own[b] - total[b] + near * coupling_factor
         middle[b] = mid
@@ -517,7 +525,11 @@
         (VM, SM, SM),
         [SM((n_dev,), jnp.int32)],
         name="route",
-    )(me, near_devices.T, near_slots.T)
+    )(
+        me,
+        pltpu.with_memory_space_constraint(near_devices.T, pltpu.HBM),
+        pltpu.with_memory_space_constraint(near_slots.T, pltpu.HBM),
+    )
     table = exchange(ask)
     x, pay = call(
         with_factors(invert_kernel, factor_value),

time: 237 us -> 234 us (0.987)
  Pallas kernels: 54.6 us -> 52.1 us
where the time goes in v7:
time: 234 us; the launch traced here: 233 us
  blocking collectives  137 us (59%)
  Pallas kernels  52.1 us (22%)
  waiting for transfers between devices  24.3 us (10%)
  starting transfers between devices  18 us (8%)
    all_to_all x3, blocking collectives, exchange(): return lax.all_to_all(x, 'rows', split_axis=0, concat_axis=0, tiled=True)  137 us
    all_to_all x2, waiting for transfers between devices, exchange(): return lax.all_to_all(x, 'rows', split_axis=0, concat_axis=0, tiled=True)  24.3 us
    all_to_all x2, starting transfers between devices, exchange(): return lax.all_to_all(x, 'rows', split_axis=0, concat_axis=0, tiled=True)  16.9 us
    pallas_call x1, Pallas kernels, setup(): call(with_factors(row_kernel, factor_value, coupling_factor, by_chip), (s...  16.7 us
    pallas_call x1, Pallas kernels, body(): call(with_factors(invert_kernel, factor_value), (blocks, shape((count, PA...  9.78 us
    pallas_call x1, Pallas kernels, swap(): call(with_factors(middle_kernel, coupling_factor), (rows, shape((total_sl...  5.57 us
    pallas_call x1, Pallas kernels, body(): call(with_factors(between_kernel, factor_value), (shape((count, BLK, 2 *...  5.33 us
    pallas_call x1, Pallas kernels, swap(): call(with_factors(left_kernel, coupling_factor), shape((n_dev, slots, n_v...  5.31 us
  transfers between devices with their start and end apart: 3, of which 1 were waited for; matrix products, arithmetic and copies ran while one was open for 0% of the time, Pallas kernels for 7%

profile of v7, /device:TPU:1, one launch (start us, length us, event | category | flops | bytes accessed | tf_op | source)
XLA Modules:
  0.0 233.4 jit_solution(116411133377567976)
XLA Ops:
  0.0 1.8 route.1
  1.8 11.5 %all-to-all-start.4 = ((s32[128,1,128]{2,1,0:T(1,128)}), s32[128,1,128]{2,1,0:T(1,128)S(1)}, u32[]{:S(2)}, u32[]{:S(2)}) async-start(s32[128,1,128]{2,1,0:T(1,128)} %bitcast.8), calls=%async_computation.4 | async-start | bytes 131072 | tf_op jit(solution)/shard_map/all_to_all | solution.py:493
  13.3 0.0 copy-start
  13.3 0.0 copy-start.1
  13.3 0.0 copy-start.3
  13.3 0.0 copy-start.4
  13.3 9.8 %invert.1 = (f32[14,128,128]{2,1,0:T(8,128)S(1)}, bf16[14,96,128]{2,1,0:T(8,128)(2,1)S(1)}) custom-call(bf16[14,128,128]{2,1,0:T(8,128)(2,1)} %refs_4_.2, bf16[14,128]{1,0:T(8,128)(2,1)} %refs_5_.1), custom_call_target="tpu_custom_call" | custom-call | flops 2000000000 | bytes 100000000 | tf_op jit(solution)/shard_map/invert/pallas_call | solution.py:534
  23.1 0.0 all-to-all-done.4
  23.1 1.1 collective-permute-start
  24.3 0.7 crowd.1
  25.6 0.0 collective-permute-done
  25.7 0.0 copy-done
  25.7 0.0 copy-done.1
  25.7 0.0 copy-done.3
  25.7 0.0 copy-done.4
  25.7 76.7 %conditional.2 = ((bf16[14,256,128]{2,1,0:T(8,128)(2,1)}, f32[14,32,128]{2,1,0:T(8,128)}, bf16[256,32,128]{2,1,0:T(8,128)(2,1)})) conditional(s32[]{:T(128)} %bitcast.10, (s32[1]{0:T(128)}, s32[128,128]{1,0:T(8,128)S(1)}, bf16[14,96,128]{2,1,0:T(8,128)(2,1)S(1)}, bf16[14,96,128]{2,1,0:T(8,128)(2,1)S(1)}, s32[42]{0:T(128)S(1)}, ...), branch_computations={%region_0.0_spmd, %region_1.0_spmd} | conditional | bytes 9437192 | solution.py:591
  25.7 3.4 %serve.2 = bf16[128,112,128]{2,1,0:T(8,128)(2,1)S(1)} custom-call(s32[1]{0:T(128)} %get-tuple-element.85.me_ref, s32[128,128]{1,0:T(8,128)S(1)} %get-tuple-element.86.incoming, bf16[14,96,128]{2,1,0:T(8,128)(2,1)S(1)} %get-tuple-element.87.own, bf16[14,96,128]{2,1,0:T(8,128)(2,1)S(1)} %get-tuple-element.88.sibling), custom_call_target="tpu_custom_call" | custom-call | tf_op jit(solution)/shard_map/cond/branch_0_fun/serve/pallas_call | solution.py:558
  29.1 56.3 %all_to_all.38.refs_6_ = bf16[128,112,128]{2,1,0:T(8,128)(2,1)S(1)} all-to-all(bf16[128,112,128]{2,1,0:T(8,128)(2,1)S(1)} %serve.2), channel_id=1, replica_groups=mesh['rows'=128] {'rows'}, dimensions={0} | all-to-all | bytes 7340032 | tf_op jit(solution)/shard_map/cond/branch_0_fun/all_to_all | solution.py:493
  85.4 16.7 %row.2 = (bf16[14,256,128]{2,1,0:T(8,128)(2,1)}, f32[14,32,128]{2,1,0:T(8,128)}, bf16[256,32,128]{2,1,0:T(8,128)(2,1)}) custom-call(s32[42]{0:T(128)S(1)} %get-tuple-element.79.refs_0_, s32[42]{0:T(128)S(1)} %get-tuple-element.80.refs_1_, bf16[14,128,128]{2,1,0:T(8,128)(2,1)S(1)} %get-tuple-element.81.refs_2_, ...), custom_call_target="tpu_custom_call" | custom-call | tf_op jit(solution)/shard_map/cond/branch_0_fun/row/pallas_call | solution.py:574
  102.4 5.3 %all-to-all-start.5 = ((bf16[128,64,128]{2,1,0:T(8,128)(2,1)}), bf16[128,64,128]{2,1,0:T(8,128)(2,1)}, u32[]{:S(2)}, u32[]{:S(2)}) async-start(bf16[128,64,128]{2,1,0:T(8,128)(2,1)} %bitcast.22), calls=%async_computation.5 | async-start | bytes 4194304 | tf_op jit(solution)/shard_map/all_to_all | solution.py:493
  107.7 5.3 %between.1 = (bf16[14,128,256]{2,1,0:T(8,128)(2,1)S(1)}, f32[14,32,128]{2,1,0:T(8,128)S(1)}, s32[258]{0:T(512)S(1)}, s32[258]{0:T(512)S(1)}, s32[1]{0:T(128)}, /*index=5*/s32[1]{0:T(128)}) custom-call(s32[1]{0:T(128)} %bitcast.4.me_ref.refs_0_, s32[128,128]{1,0:T(8,128)S(1)} %bitcast.27, s32[128,128]{1,0:T(8,128)S(1)} %bitcast.28, ...), custom_call_target="tpu_custom_call" | custom-call | flops 2000000000 | bytes 10000000 | tf_op jit(solution)/shard_map/between/pallas_call | solution.py:598
  113.7 24.3 %all-to-all-done.5 = bf16[128,64,128]{2,1,0:T(8,128)(2,1)} async-done(((bf16[128,64,128]{2,1,0:T(8,128)(2,1)}), bf16[128,64,128]{2,1,0:T(8,128)(2,1)}, u32[]{:S(2)}, u32[]{:S(2)}) %all-to-all-start.5) | async-done | bytes 2097184 | tf_op jit(solution)/shard_map/all_to_all | solution.py:493
  138.0 56.6 %conditional.3 = ((f32[14,32,128]{2,1,0:T(8,128)S(1)}, bf16[256,32,128]{2,1,0:T(8,128)(2,1)})) conditional(s32[]{:T(128)} %bitcast.11, (s32[42]{0:T(128)S(1)}, s32[258]{0:T(512)S(1)}, s32[258]{0:T(512)S(1)}, s32[1]{0:T(128)}, bf16[256,32,128]{2,1,0:T(8,128)(2,1)}, /*index=5*/f32[14,32,128]{2,1,0:T(8,128)}, bf16[14,128,256]{2,1,0:T(8,128)(2,1)S(1)}, ...), branch_computations={%region_2.0_spmd, %region_3.0_spmd} | conditional | bytes 8388616 | solution.py:636
  138.0 5.3 %left.2 = bf16[128,3,32,128]{3,2,1,0:T(8,128)(2,1)S(1)} custom-call(s32[42]{0:T(128)S(1)} %get-tuple-element.98.refs_0_, s32[258]{0:T(512)S(1)} %get-tuple-element.99.refs_1_, s32[258]{0:T(512)S(1)} %get-tuple-element.100.refs_2_, s32[1]{0:T(128)} %get-tuple-element.101.refs_3_, bf16[256,32,128]{2,1,0:T(8,128)(2,1)} %get-tuple-element.102.refs_4_, ...), custom_call_target="tpu_custom_call" | custom-call | tf_op jit(solution)/shard_map/cond/branch_0_fun/left/pallas_call | solution.py:616
  143.4 45.7 %all_to_all.40 = bf16[128,96,128]{2,1,0:T(8,128)(2,1)S(1)} all-to-all(bf16[128,96,128]{2,1,0:T(8,128)(2,1)S(1)} %bitcast.20), channel_id=1, replica_groups=mesh['rows'=128] {'rows'}, dimensions={0} | all-to-all | bytes 6291456 | tf_op jit(solution)/shard_map/cond/branch_0_fun/all_to_all | solution.py:493
  189.1 5.6 %middle.2 = (f32[14,32,128]{2,1,0:T(8,128)S(1)}, bf16[256,32,128]{2,1,0:T(8,128)(2,1)}) custom-call(s32[42]{0:T(128)S(1)} %get-tuple-element.98.refs_0_, s32[258]{0:T(512)S(1)} %get-tuple-element.99.refs_1_, s32[258]{0:T(512)S(1)} %get-tuple-element.100.refs_2_, s32[1]{0:T(128)} %get-tuple-element.101.refs_3_, bf16[128,3,32,128]{3,2,1,0:T(8,128)(2,1)S(1)} %bitcast.19, ...), custom_call_target="tpu_custom_call" | custom-call | tf_op jit(solution)/shard_map/cond/branch_0_fun/middle/pallas_call | solution.py:627
  194.6 0.0 copy-start.2
  194.6 35.2 %all_to_all.42 = bf16[128,64,128]{2,1,0:T(8,128)(2,1)S(1)} all-to-all(bf16[128,64,128]{2,1,0:T(8,128)(2,1)} %bitcast.23), channel_id=1, replica_groups=mesh['rows'=128] {'rows'}, dimensions={0} | all-to-all | bytes 4194304 | tf_op jit(solution)/shard_map/all_to_all | solution.py:493
  229.9 0.0 copy-done.2
  229.9 3.5 %result.1 = f32[32,1792]{1,0:T(8,128)} custom-call(s32[42]{0:T(128)S(1)} %get-tuple-element.134.refs_0_, bf16[256,32,128]{2,1,0:T(8,128)(2,1)S(1)} %bitcast.21, f32[14,32,128]{2,1,0:T(8,128)S(1)} %get-tuple-element.150.refs_2_, bf16[14,256,128]{2,1,0:T(8,128)(2,1)S(1)} %copy-done.2, bf16[14,3,128,128]{3,2,1,0:T(8,128)(2,1)S(1)} %copy-done), custom_call_target="tpu_custom_call" | custom-call | tf_op jit(solution)/shard_map/result/pallas_call | solution.py:643
Async XLA Ops:
  1.8 21.3 %all-to-all-start.4 = ((s32[128,1,128]{2,1,0:T(1,128)}), s32[128,1,128]{2,1,0:T(1,128)S(1)}, u32[]{:S(2)}, u32[]{:S(2)}) async-start(s32[128,1,128]{2,1,0:T(1,128)} %bitcast.8), calls=%async_computation.4 | async-start | bytes 131072 | tf_op jit(solution)/shard_map/all_to_all | solution.py:493
  13.3 12.4 %copy-start = (bf16[14,3,128,128]{3,2,1,0:T(8,128)(2,1)S(1)}, bf16[14,3,128,128]{3,2,1,0:T(8,128)(2,1)}, u32[]{:S(2)}) copy-start(bf16[14,3,128,128]{3,2,1,0:T(8,128)(2,1)} %refs_4_.3) | copy-start | bytes 4128772
  13.3 12.4 %copy-start.1 = (bf16[14,128,128]{2,1,0:T(8,128)(2,1)S(1)}, bf16[14,128,128]{2,1,0:T(8,128)(2,1)}, u32[]{:S(2)}) copy-start(bf16[14,128,128]{2,1,0:T(8,128)(2,1)} %refs_4_.2) | copy-start | bytes 1376260
  13.3 12.4 %copy-start.3 = (f32[32,1792]{1,0:T(8,128)S(1)}, f32[32,1792]{1,0:T(8,128)}, u32[]{:S(2)}) copy-start(f32[32,1792]{1,0:T(8,128)} %param.15) | copy-start | bytes 688132
  13.3 12.4 %copy-start.4 = (bf16[14,128]{1,0:T(8,128)(2,1)S(1)}, bf16[14,128]{1,0:T(8,128)(2,1)}, u32[]{:S(2)}) copy-start(bf16[14,128]{1,0:T(8,128)(2,1)} %refs_5_.1) | copy-start | bytes 10756
  23.1 2.5 %collective-permute-start = (bf16[14,96,128]{2,1,0:T(8,128)(2,1)S(1)}, bf16[14,96,128]{2,1,0:T(8,128)(2,1)S(1)}, u32[]{:S(2)}, u32[]{:S(2)}) collective-permute-start(bf16[14,96,128]{2,1,0:T(8,128)(2,1)S(1)} %get-tuple-element.139), channel_id=1, source_target_pairs={{0,1},{1,0},{2,3},{3,2},{4,5},{5,4},{6,7},{7,6},{8,9},{9,8},{10,11... | collective-permute-start | bytes 1032200 | tf_op jit(solution)/shard_map/ppermute | solution.py:545
  102.4 35.7 %all-to-all-start.5 = ((bf16[128,64,128]{2,1,0:T(8,128)(2,1)}), bf16[128,64,128]{2,1,0:T(8,128)(2,1)}, u32[]{:S(2)}, u32[]{:S(2)}) async-start(bf16[128,64,128]{2,1,0:T(8,128)(2,1)} %bitcast.22), calls=%async_computation.5 | async-start | bytes 4194304 | tf_op jit(solution)/shard_map/all_to_all | solution.py:493
  194.6 35.2 %copy-start.2 = (bf16[14,256,128]{2,1,0:T(8,128)(2,1)S(1)}, bf16[14,256,128]{2,1,0:T(8,128)(2,1)}, u32[]{:S(2)}) copy-start(bf16[14,256,128]{2,1,0:T(8,128)(2,1)} %get-tuple-element.151.refs_3_) | copy-start | bytes 2752516
